TPU v7x, 512 devices: a whole 4x4x16 slice. The times are simulated.
512 devices in a mesh: section: 16 (over z), frame: 32 (over x, y, core).
Axes of the slice: x: 4, y: 4, z: 16, core: 2. Of those that a mesh axis runs over, the one named last changes fastest.
Arguments:
- inflow: bfloat16 [128, 4096], P(None, 'frame'), may hold values from -6 to 6
- gains: bfloat16 [16, 4096], P('section'), may hold values from 0.25 to 1.75
- w_query: bfloat16 [16, 4096, 4096], P('section', None, 'frame'), may hold values from -1 to 1
- w_key: bfloat16 [16, 4096, 4096], P('section', None, 'frame'), may hold values from -0.046875 to 0.046875
- w_value: bfloat16 [16, 4096, 4096], P('section', None, 'frame'), may hold values from -0.046875 to 0.046875
- cache_keys: bfloat16 [16, 256, 4096], P('section', None, 'frame'), may hold values from -6 to 6
- cache_values: bfloat16 [16, 256, 4096], P('section', None, 'frame'), may hold values from -6 to 6
- w_depth_in: bfloat16 [4096, 1024], P(None, 'section'), may hold values from -0.046875 to 0.046875
- code_table: bfloat16 [2048, 1024], P(None, 'section'), may hold values from -6 to 6
- w_dquery: bfloat16 [1024, 1024], P(None, 'section'), may hold values from -1 to 1
- w_dkey: bfloat16 [1024, 1024], P(None, 'section'), may hold values from -1 to 1
- w_dvalue: bfloat16 [1024, 1024], P(None, 'section'), may hold values from -0.1875 to 0.1875
- w_dout: bfloat16 [1024, 1024], P('section'), may hold values from -0.1875 to 0.1875
- codes: int32 [128, 7], P('frame'), may hold values from 0 to 2047
- speaker_mask: int32 [128], P('frame'), may hold values 0 or 1
- cotangent: bfloat16 [128, 8, 1024], P('frame', None, 'section'), may hold values from -6 to 6
Outputs:
- new_keys: bfloat16 [16, 128, 4096], P('section', None, 'frame')
- new_values: bfloat16 [16, 128, 4096], P('section', None, 'frame')
- depth_out: bfloat16 [128, 8, 1024], P('frame', None, 'section')
- temporal_grad: bfloat16 [128, 4096], P('frame', 'section')
All inputs are finite; a program needn't handle non-finite values. No bound on the sum of `speaker_mask` on one device may be relied on, other than what follows from the above.
Results may differ from a plain program's by a relative error of at most 0.038.
Values may be sent and summed in bfloat16 or wider, within the bound.
No kernel may reach another device: no remote copies, remote signals or barrier semaphores. Data moves between devices by JAX's collectives and lax.ppermute only.
A program may use at most 64 MiB of HBM per device.

v0:
```python
import jax
import jax.numpy as jnp
from jax import lax
from jax.experimental import pallas as pl
from jax.experimental.pallas import tpu as pltpu
from jax.sharding import PartitionSpec as P

HEAD = 128
CH = 64
CACHE = 256
DHEAD = 64
SECTIONS = 16
CHIPS = 16
PIECES = 8

EPSILON = 1e-05
MASKED = -1e30
BOTH = ("section", "frame")


def device_id(section, chip, core):
    return section * 2 * CHIPS + chip * 2 + core


def plane_pairs(first):
    lows = range(first, SECTIONS - 1, 2)
    groups = [
        [device_id(low + up, chip, core) for up in range(2) for chip in range(CHIPS)]
        for low in lows
        for core in range(2)
    ]
    for alone in sorted(set(range(SECTIONS)) - {low + up for low in lows for up in range(2)}):
        groups.append([device_id(alone, chip, core) for core in range(2) for chip in range(CHIPS)])
    return groups


def core_pairs():
    return [
        [device_id(section, chip, core) for core in range(2)]
        for section in range(SECTIONS)
        for chip in range(CHIPS)
    ]


def layer_kernel(
    where_ref,
    rows_ref,
    weight_ref,
    stash_k_ref,
    stash_v_ref,
    held_ref,
    next_ref,
    found_ref,
    send_ref,
):
    tick = where_ref[0]
    section = where_ref[1]
    chip = where_ref[2]
    core = where_ref[3]
    next_ref[0] = tick + 1
    next_ref[1] = section
    next_ref[2] = chip
    next_ref[3] = core
    block = tick - section
    total = jnp.zeros((CH, 3 * HEAD), jnp.float32)
    squares = jnp.zeros((CH, 2 * HEAD), jnp.float32)
    per_piece = CHIPS // PIECES
    depth = 2 * HEAD * per_piece
    for piece in range(PIECES):
        parts = []
        for at in range(piece * per_piece, (piece + 1) * per_piece):
            part = jnp.concatenate([rows_ref[0, at], rows_ref[1, at]], axis=1)
            wide = part.astype(jnp.float32)
            squares = squares + wide * wide
            parts.append(part)
        total = total + jnp.dot(
            jnp.concatenate(parts, axis=1),
            weight_ref[pl.ds(piece * depth, depth), :],
            preferred_element_type=jnp.float32,
        )
    scale_rows = lax.rsqrt(
        jnp.sum(squares, axis=1, keepdims=True) * (1.0 / (2 * CHIPS * HEAD)) + EPSILON
    )
    projected = (total * scale_rows).astype(jnp.bfloat16)
    query = projected[:, :HEAD]
    key_new = projected[:, HEAD : 2 * HEAD]
    value_new = projected[:, 2 * HEAD :]
    keys = jnp.concatenate([stash_k_ref[...], held_ref[0, :CH], key_new], axis=0)
    values = jnp.concatenate([stash_v_ref[...], held_ref[1, :CH], value_new], axis=0)
    scores = lax.dot_general(
        query, keys, (((1,), (1,)), ((), ())), preferred_element_type=jnp.float32
    ) * HEAD ** (-0.5)
    at_key = lax.broadcasted_iota(jnp.int32, scores.shape, 1)
    at_row = lax.broadcasted_iota(jnp.int32, scores.shape, 0)
    old = jnp.where(block > 0, CACHE + CH, CACHE)
    allowed = (at_key < old) | ((at_key >= CACHE + CH) & (at_key - (CACHE + CH) <= at_row))
    scores = jnp.where(allowed, scores, MASKED)
    peak = jnp.max(scores, axis=-1, keepdims=True)
    raised = jnp.exp(scores - peak)
    probs = (raised / jnp.sum(raised, axis=-1, keepdims=True)).astype(jnp.bfloat16)
    attended = jnp.dot(probs, values, preferred_element_type=jnp.float32)
    own = rows_ref[core, chip].astype(jnp.float32)
    x_out = (own + attended).astype(jnp.bfloat16)

    def keep(rows):
        found_ref[0, rows] = key_new
        found_ref[1, rows] = value_new
        found_ref[2, rows] = x_out

    early, late = pl.ds(0, CH), pl.ds(CH, CH)
    found_ref[...] = held_ref[...]
    pl.when(block == 0)(lambda: keep(early))
    pl.when(block == 2)(lambda: keep(late))
    for at in range(send_ref.shape[0]):
        send_ref[at] = x_out


def layer_step(where, rows, weight, stash_k, stash_v, held):
    vmem = pl.BlockSpec(memory_space=pltpu.VMEM)
    smem = pl.BlockSpec(memory_space=pltpu.SMEM)
    return pl.pallas_call(
        layer_kernel,
        out_shape=(
            jax.ShapeDtypeStruct(where.shape, where.dtype),
            jax.ShapeDtypeStruct(held.shape, held.dtype),
            jax.ShapeDtypeStruct((2 * CHIPS, CH, HEAD), jnp.bfloat16),
        ),
        in_specs=[smem, vmem, vmem, vmem, vmem, vmem],
        out_specs=(smem, vmem, vmem),
        input_output_aliases={5: 1},
        compiler_params=pltpu.CompilerParams(vmem_limit_bytes=16 * 1024 * 1024),
        cost_estimate=pl.CostEstimate(
            flops=2 * CH * weight.size, bytes_accessed=2 * weight.size, transcendentals=0
        ),
    )(where, rows, weight, stash_k, stash_v, held)


def contract_last(a, b):
    return lax.dot_general(a, b, (((1,), (1,)), ((), ())), preferred_element_type=jnp.float32)


def depth_forward(z, whole, in_head, frames, levels):
    width = z.shape[1]
    high = lax.Precision.HIGHEST
    heads = in_head.shape[1]
    query, key, value = (
        contract_last(z, whole[at]).reshape(frames, levels, width) for at in range(3)
    )
    pairs = (query[:, :, None, :] * key[:, None, :, :]).reshape(-1, width)
    scores = jnp.dot(pairs, in_head, precision=high).reshape(frames, levels, levels, heads)
    scores = scores * DHEAD ** (-0.5)
    causal = jnp.arange(levels)[:, None] >= jnp.arange(levels)[None, :]
    scores = jnp.where(causal[None, :, :, None], scores, MASKED)
    peak = jnp.max(scores, axis=2, keepdims=True)
    raised = jnp.exp(scores - peak)
    probs = raised / jnp.sum(raised, axis=2, keepdims=True)
    spread = jnp.dot(probs.reshape(-1, heads), in_head.T, precision=high).reshape(
        frames, levels, levels, width
    )
    mixed = jnp.sum(spread * value[:, None, :, :], axis=2)
    return query, key, value, probs, spread, mixed


def depth_backward(grad_mixed, query, key, value, probs, spread, in_head):
    frames, levels, width = query.shape
    heads = in_head.shape[1]
    high = lax.Precision.HIGHEST
    grad_value = jnp.sum(spread * grad_mixed[:, :, None, :], axis=1)
    pairs = (grad_mixed[:, :, None, :] * value[:, None, :, :]).reshape(-1, width)
    grad_probs = jnp.dot(pairs, in_head, precision=high).reshape(probs.shape)
    inner = jnp.sum(grad_probs * probs, axis=2, keepdims=True)
    grad_scores = probs * (grad_probs - inner) * DHEAD ** (-0.5)
    wide = jnp.dot(grad_scores.reshape(-1, heads), in_head.T, precision=high).reshape(
        frames, levels, levels, width
    )
    grad_query = jnp.sum(wide * key[:, None, :, :], axis=2)
    grad_key = jnp.sum(wide * query[:, :, None, :], axis=1)
    return grad_query, grad_key, grad_value


def body(
    inflow,
    gains,
    w_query,
    w_key,
    w_value,
    cache_keys,
    cache_values,
    w_depth_in,
    code_table,
    w_dquery,
    w_dkey,
    w_dvalue,
    w_dout,
    codes,
    speaker_mask,
    cotangent,
):
    section_id = lax.axis_index("section")
    frame_id = lax.axis_index("frame")
    frames, levels, part = cotangent.shape
    width = part * SECTIONS
    features = w_depth_in.shape[0]

    core = frame_id % 2
    half = part // 2
    looked = jnp.take(code_table, codes, axis=0).reshape(-1, part)
    masked = cotangent.astype(jnp.float32) * speaker_mask.astype(jnp.float32)[:, None, None]
    masked = masked.astype(jnp.bfloat16).reshape(-1, part)
    extra = jnp.concatenate([looked, masked], axis=0)
    extra = jnp.pad(extra, ((0, HEAD - extra.shape[0]), (0, 0))).T
    extra = lax.all_gather(extra, BOTH, axis=1, tiled=True, axis_index_groups=core_pairs())
    shares = jnp.concatenate(
        [
            lax.dynamic_slice_in_dim(share, core * half, half, 0)
            for share in (w_depth_in.T, w_dquery.T, w_dkey.T, w_dvalue.T, w_dout, extra)
        ],
        axis=1,
    )
    along = [
        [device_id(section, chip, at) for section in range(SECTIONS) for at in range(2)]
        for chip in range(CHIPS)
    ]
    shares = lax.all_gather(shares, BOTH, axis=0, tiled=True, axis_index_groups=along)

    gain = gains[0].astype(jnp.float32)[:, None]
    weight = jnp.concatenate([w_query[0], w_key[0], w_value[0]], axis=1)
    weight = (weight.astype(jnp.float32) * gain).astype(jnp.bfloat16)
    stash_k, stash_v = cache_keys[0], cache_values[0]

    def spread_out(block):
        return jnp.broadcast_to(block[None], (2 * CHIPS,) + block.shape)

    def pass_on(first, send):
        return lax.all_to_all(
            send, BOTH, split_axis=0, concat_axis=0, tiled=True, axis_index_groups=plane_pairs(first)
        )

    def layer(where, got, held):
        rows = lax.all_gather(got, BOTH, axis=0, axis_index_groups=core_pairs())
        return layer_step(where, rows, weight, stash_k, stash_v, held)

    where = jnp.stack([jnp.int32(0), section_id, frame_id // 2, core]).astype(jnp.int32)
    held = jnp.zeros((3, 2 * CH, HEAD), jnp.bfloat16)
    entry = pass_on(0, spread_out(jnp.where(section_id % 2 == 0, inflow[:CH], inflow[CH:])))
    second = entry[CHIPS:]
    where, held, send = layer(where, entry[:CHIPS], held)
    for tick in range(1, SECTIONS + 2):
        got = pass_on((tick - 1) % 2, send)[:CHIPS]
        if tick == 2:
            got = jnp.where(section_id == 0, second, got)
        where, held, send = layer(where, got, held)
    new_keys, new_values, finished = held[0], held[1], held[2]

    finished = finished.reshape(2 * CHIPS, frames, HEAD)
    temporal = lax.all_to_all(finished, "frame", split_axis=0, concat_axis=0, tiled=True)
    temporal = temporal.transpose(1, 0, 2).reshape(frames, features)
    w_in = shares[:, :features]
    whole = [
        shares[:, features + at * width : features + (at + 1) * width] for at in range(4)
    ]
    extra = shares[:, features + 4 * width :].reshape(width, 2, HEAD)
    extra = lax.dynamic_index_in_dim(extra, core, 1, keepdims=False).T
    looked = extra[: frames * (levels - 1)].reshape(frames, levels - 1, width)
    masked = extra[frames * (levels - 1) : frames * (2 * levels - 1)]
    in_head = (jnp.arange(width)[:, None] // DHEAD == jnp.arange(width // DHEAD)[None, :]).astype(
        jnp.float32
    )
    grad_mixed = contract_last(masked, whole[3]).reshape(frames, levels, width)

    base = contract_last(temporal, w_in)[:, None, :]
    z = jnp.concatenate([base, base + looked.astype(jnp.float32)], axis=1).astype(jnp.bfloat16)
    z = z.reshape(frames * levels, width)
    query, key, value, probs, spread, mixed = depth_forward(z, whole, in_head, frames, levels)
    mixed = mixed.astype(jnp.bfloat16).reshape(frames * levels, width)
    depth_out = (
        z.astype(jnp.float32) + jnp.dot(mixed, whole[3], preferred_element_type=jnp.float32)
    ).astype(jnp.bfloat16)
    grads = depth_backward(grad_mixed, query, key, value, probs, spread, in_head)
    grad_base = jnp.sum(masked.astype(jnp.float32).reshape(frames, levels, width), axis=1)
    for grad, weights in zip(grads, whole[:3]):
        summed = jnp.sum(grad, axis=1).astype(jnp.bfloat16)
        grad_base = grad_base + jnp.dot(summed, weights, preferred_element_type=jnp.float32)
    temporal_grad = jnp.dot(
        grad_base.astype(jnp.bfloat16), w_in, preferred_element_type=jnp.float32
    ).astype(jnp.bfloat16)

    depth_out = depth_out.reshape(frames * levels, SECTIONS, part).transpose(1, 0, 2)
    temporal_grad = temporal_grad.reshape(frames, SECTIONS, -1).transpose(1, 0, 2)
    results = jnp.concatenate(
        [depth_out.reshape(SECTIONS, -1, HEAD), temporal_grad.reshape(SECTIONS, -1, HEAD)], axis=1
    )
    results = lax.all_to_all(results, "section", split_axis=0, concat_axis=0, tiled=True)
    mine = results[SECTIONS - 1]
    cut = frames * levels * part // HEAD
    depth_out = mine[:cut].reshape(frames, levels, part)
    temporal_grad = mine[cut:].reshape(frames, -1)
    return (new_keys[None], new_values[None], depth_out, temporal_grad)


def solution(mesh):
    return jax.shard_map(
        body,
        mesh=mesh,
        in_specs=(
            P(None, "frame"),
            P("section", None),
            P("section", None, "frame"),
            P("section", None, "frame"),
            P("section", None, "frame"),
            P("section", None, "frame"),
            P("section", None, "frame"),
            P(None, "section"),
            P(None, "section"),
            P(None, "section"),
            P(None, "section"),
            P(None, "section"),
            P("section", None),
            P("frame", None),
            P("frame"),
            P("frame", None, "section"),
        ),
        out_specs=(
            P("section", None, "frame"),
            P("section", None, "frame"),
            P("frame", None, "section"),
            P("frame", "section"),
        ),
        check_vma=False,
    )
```

profile of v0, /device:TPU:6, one launch (start us, length us, event | category | flops | bytes accessed | tf_op | source)
XLA Modules:
  0.0 494.8 jit_solution(1645345252459990901)
XLA Ops:
  8.9 10.1 %all-to-all-start = ((bf16[32,64,128]{2,1,0:T(8,128)(2,1)}), bf16[32,64,128]{2,1,0:T(8,128)(2,1)}, u32[]{:S(2)}, u32[]{:S(2)}) async-start(bf16[32,64,128]{2,1,0:T(8,128)(2,1)} %broadcast_in_dim.48), calls=%async_computation | async-start | bytes 1048576 | tf_op jit(solution)/shard_map/all_to_all | solution.py:235
  19.9 2.2 multiply_convert_fusion.weight_ref
  22.1 6.0 %all-to-all-done = bf16[32,64,128]{2,1,0:T(8,128)(2,1)} async-done(((bf16[32,64,128]{2,1,0:T(8,128)(2,1)}), bf16[32,64,128]{2,1,0:T(8,128)(2,1)}, u32[]{:S(2)}, u32[]{:S(2)}) %all-to-all-start) | async-done | bytes 524320 | tf_op jit(solution)/shard_map/all_to_all | solution.py:235
  29.1 2.2 all-gather
  31.3 2.2 shard_map.183
  34.3 5.8 %all-to-all-start.1 = ((bf16[32,64,128]{2,1,0:T(8,128)(2,1)}), bf16[32,64,128]{2,1,0:T(8,128)(2,1)}, u32[]{:S(2)}, u32[]{:S(2)}) async-start(bf16[32,64,128]{2,1,0:T(8,128)(2,1)} %copy-done.2), calls=%async_computation.1 | async-start | bytes 1048576 | tf_op jit(solution)/shard_map/all_to_all | solution.py:235
  46.9 4.1 all-to-all-done.1
  52.0 2.2 all-gather.1
  54.2 2.2 shard_map.184
  57.2 5.8 %all-to-all-start.2 = ((bf16[32,64,128]{2,1,0:T(8,128)(2,1)}), bf16[32,64,128]{2,1,0:T(8,128)(2,1)}, u32[]{:S(2)}, u32[]{:S(2)}) async-start(bf16[32,64,128]{2,1,0:T(8,128)(2,1)} %copy-done.3), calls=%async_computation.2 | async-start | bytes 1048576 | tf_op jit(solution)/shard_map/all_to_all | solution.py:235
  70.5 2.6 all-to-all-done.2
  74.1 2.2 all-gather.2
  76.3 2.3 shard_map.185
  78.6 18.5 %all_to_all.100 = bf16[32,64,128]{2,1,0:T(8,128)(2,1)S(1)} all-to-all(bf16[32,64,128]{2,1,0:T(8,128)(2,1)S(1)} %get-tuple-element.63), channel_id=1, replica_groups={{0,2,4,6,8,10,12,14,16,18,20,22,24,26,28,30,32,34,36,38,40,42,44,46,48,..., dimensions={0} | all-to-all | bytes 1048576 | tf_op jit(solution)/shard_map/all_to_all | solution.py:235
  97.1 2.3 all-gather.3
  99.4 2.3 shard_map.186
  101.6 15.1 %all_to_all.101 = bf16[32,64,128]{2,1,0:T(8,128)(2,1)S(1)} all-to-all(bf16[32,64,128]{2,1,0:T(8,128)(2,1)S(1)} %get-tuple-element.66), channel_id=1, replica_groups={{32,34,36,38,40,42,44,46,48,50,52,54,56,58,60,62,64,66,68,70,72,74,76,7..., dimensions={0} | all-to-all | bytes 1048576 | tf_op jit(solution)/shard_map/all_to_all | solution.py:235
  116.7 2.2 all-gather.4
  118.9 2.2 shard_map.187
  121.1 36.4 %all_to_all.102 = bf16[32,64,128]{2,1,0:T(8,128)(2,1)S(1)} all-to-all(bf16[32,64,128]{2,1,0:T(8,128)(2,1)S(1)} %get-tuple-element.69), channel_id=1, replica_groups={{0,2,4,6,8,10,12,14,16,18,20,22,24,26,28,30,32,34,36,38,40,42,44,46,48,..., dimensions={0} | all-to-all | bytes 1048576 | tf_op jit(solution)/shard_map/all_to_all | solution.py:235
  157.6 2.2 all-gather.5
  159.8 2.2 shard_map.188
  162.0 14.9 %all_to_all.103 = bf16[32,64,128]{2,1,0:T(8,128)(2,1)S(1)} all-to-all(bf16[32,64,128]{2,1,0:T(8,128)(2,1)S(1)} %get-tuple-element.72), channel_id=1, replica_groups={{32,34,36,38,40,42,44,46,48,50,52,54,56,58,60,62,64,66,68,70,72,74,76,7..., dimensions={0} | all-to-all | bytes 1048576 | tf_op jit(solution)/shard_map/all_to_all | solution.py:235
  177.0 2.3 all-gather.6
  179.2 2.3 shard_map.189
  181.5 22.6 %all_to_all.104 = bf16[32,64,128]{2,1,0:T(8,128)(2,1)S(1)} all-to-all(bf16[32,64,128]{2,1,0:T(8,128)(2,1)S(1)} %get-tuple-element.75), channel_id=1, replica_groups={{0,2,4,6,8,10,12,14,16,18,20,22,24,26,28,30,32,34,36,38,40,42,44,46,48,..., dimensions={0} | all-to-all | bytes 1048576 | tf_op jit(solution)/shard_map/all_to_all | solution.py:235
  206.3 2.2 shard_map.190
  208.6 15.2 %all_to_all.105 = bf16[32,64,128]{2,1,0:T(8,128)(2,1)S(1)} all-to-all(bf16[32,64,128]{2,1,0:T(8,128)(2,1)S(1)} %get-tuple-element.78), channel_id=1, replica_groups={{32,34,36,38,40,42,44,46,48,50,52,54,56,58,60,62,64,66,68,70,72,74,76,7..., dimensions={0} | all-to-all | bytes 1048576 | tf_op jit(solution)/shard_map/all_to_all | solution.py:235
  223.8 2.4 all-gather.8
  226.1 2.3 shard_map.191
  228.4 22.2 %all_to_all.106 = bf16[32,64,128]{2,1,0:T(8,128)(2,1)S(1)} all-to-all(bf16[32,64,128]{2,1,0:T(8,128)(2,1)S(1)} %get-tuple-element.81), channel_id=1, replica_groups={{0,2,4,6,8,10,12,14,16,18,20,22,24,26,28,30,32,34,36,38,40,42,44,46,48,..., dimensions={0} | all-to-all | bytes 1048576 | tf_op jit(solution)/shard_map/all_to_all | solution.py:235
  250.6 2.2 all-gather.9
  252.8 2.2 shard_map.192
  255.1 15.2 %all_to_all.107 = bf16[32,64,128]{2,1,0:T(8,128)(2,1)S(1)} all-to-all(bf16[32,64,128]{2,1,0:T(8,128)(2,1)S(1)} %get-tuple-element.84), channel_id=1, replica_groups={{32,34,36,38,40,42,44,46,48,50,52,54,56,58,60,62,64,66,68,70,72,74,76,7..., dimensions={0} | all-to-all | bytes 1048576 | tf_op jit(solution)/shard_map/all_to_all | solution.py:235
  270.3 2.2 all-gather.10
  272.4 2.2 shard_map.193
  274.7 17.5 %all_to_all.108 = bf16[32,64,128]{2,1,0:T(8,128)(2,1)S(1)} all-to-all(bf16[32,64,128]{2,1,0:T(8,128)(2,1)S(1)} %get-tuple-element.87), channel_id=1, replica_groups={{0,2,4,6,8,10,12,14,16,18,20,22,24,26,28,30,32,34,36,38,40,42,44,46,48,..., dimensions={0} | all-to-all | bytes 1048576 | tf_op jit(solution)/shard_map/all_to_all | solution.py:235
  292.2 2.2 all-gather.11
  294.4 2.3 shard_map.194
  296.7 15.2 %all_to_all.109 = bf16[32,64,128]{2,1,0:T(8,128)(2,1)S(1)} all-to-all(bf16[32,64,128]{2,1,0:T(8,128)(2,1)S(1)} %get-tuple-element.90), channel_id=1, replica_groups={{32,34,36,38,40,42,44,46,48,50,52,54,56,58,60,62,64,66,68,70,72,74,76,7..., dimensions={0} | all-to-all | bytes 1048576 | tf_op jit(solution)/shard_map/all_to_all | solution.py:235
  311.9 2.2 all-gather.12
  314.0 2.2 shard_map.195
  316.3 18.2 %all_to_all.110 = bf16[32,64,128]{2,1,0:T(8,128)(2,1)S(1)} all-to-all(bf16[32,64,128]{2,1,0:T(8,128)(2,1)S(1)} %get-tuple-element.93), channel_id=1, replica_groups={{0,2,4,6,8,10,12,14,16,18,20,22,24,26,28,30,32,34,36,38,40,42,44,46,48,..., dimensions={0} | all-to-all | bytes 1048576 | tf_op jit(solution)/shard_map/all_to_all | solution.py:235
  334.5 2.2 all-gather.13
  336.7 2.2 shard_map.196
  339.0 15.2 %all_to_all.111 = bf16[32,64,128]{2,1,0:T(8,128)(2,1)S(1)} all-to-all(bf16[32,64,128]{2,1,0:T(8,128)(2,1)S(1)} %get-tuple-element.96), channel_id=1, replica_groups={{32,34,36,38,40,42,44,46,48,50,52,54,56,58,60,62,64,66,68,70,72,74,76,7..., dimensions={0} | all-to-all | bytes 1048576 | tf_op jit(solution)/shard_map/all_to_all | solution.py:235
  354.2 2.2 all-gather.14
  356.3 2.2 shard_map.197
  358.6 17.5 %all_to_all.112 = bf16[32,64,128]{2,1,0:T(8,128)(2,1)S(1)} all-to-all(bf16[32,64,128]{2,1,0:T(8,128)(2,1)S(1)} %get-tuple-element.99), channel_id=1, replica_groups={{0,2,4,6,8,10,12,14,16,18,20,22,24,26,28,30,32,34,36,38,40,42,44,46,48,..., dimensions={0} | all-to-all | bytes 1048576 | tf_op jit(solution)/shard_map/all_to_all | solution.py:235
  378.3 2.2 shard_map.198
  380.6 15.2 %all_to_all.113 = bf16[32,64,128]{2,1,0:T(8,128)(2,1)S(1)} all-to-all(bf16[32,64,128]{2,1,0:T(8,128)(2,1)S(1)} %get-tuple-element.102), channel_id=1, replica_groups={{32,34,36,38,40,42,44,46,48,50,52,54,56,58,60,62,64,66,68,70,72,74,76,7..., dimensions={0} | all-to-all | bytes 1048576 | tf_op jit(solution)/shard_map/all_to_all | solution.py:235
  397.9 2.2 shard_map.199
  401.0 7.3 %all-to-all-start.17 = ((bf16[32,64,128]{2,1,0:T(8,128)(2,1)}), bf16[32,64,128]{2,1,0:T(8,128)(2,1)}, u32[]{:S(2)}, u32[]{:S(2)}) async-start(bf16[32,64,128]{2,1,0:T(8,128)(2,1)} %copy-done.4), calls=%async_computation.17 | async-start | bytes 1048576 | tf_op jit(solution)/shard_map/all_to_all | solution.py:235
  412.2 2.4 constant_dynamic-slice_fusion
  416.4 3.0 fusion.26
  423.5 2.5 shard_map.200
  426.6 7.4 %all-to-all-start.18 = ((bf16[32,4,128]{2,1,0:T(4,128)(2,1)}), bf16[32,4,128]{2,1,0:T(4,128)(2,1)S(1)}, u32[]{:S(2)}, u32[]{:S(2)}) async-start(bf16[32,4,128]{2,1,0:T(4,128)(2,1)} %bitcast.27), calls=%async_computation.18 | async-start | bytes 65536 | tf_op jit(solution)/shard_map/all_to_all | solution.py:256
  435.0 4.6 all-to-all-done.18
  439.6 5.6 %fusion.2 = f32[4,1024]{1,0:T(4,128)S(1)} fusion(bf16[1024,8448]{1,0:T(8,128)(2,1)} %all-gather.20.cloned.1.call-done, bf16[32,4,128]{2,1,0:T(4,128)(2,1)S(1)} %all-to-all-done.18), kind=kOutput, calls=%fused_computation.3 | convolution fusion | flops 33554432 | bytes 8437760 | tf_op jit(solution)/shard_map/dot_general | solution.py:139
  445.3 2.3 fusion.11
  447.6 2.3 fusion.9
  450.6 2.3 fusion.7
  461.5 5.5 %fusion.4 = bf16[4,4096]{1,0:T(4,128)(2,1)S(1)} fusion(bf16[1024,8448]{1,0:T(8,128)(2,1)} %all-gather.20.cloned.1.call-done, f32[4,1024]{1,0:T(4,128)S(1)} %fusion.17, f32[4,1024]{1,0:T(4,128)S(1)} %fusion.20, f32[4,1024]{1,0:T(4,128)S(1)} %convert_reduce_fusion, bf16[4,1024]{1,0:T(4,128)(2,1)S(1)} %get-tuple-element.110), kind=kOutput, calls=%fused_computation.6 | convolution fusion | flops 41975808 | bytes 10575872 | tf_op jit(solution)/shard_map/dot_general | solution.py:284
  467.1 19.6 %all_to_all.114 = bf16[16,24,128]{2,1,0:T(8,128)(2,1)S(1)} all-to-all(bf16[16,24,128]{2,1,0:T(8,128)(2,1)S(1)} %pad_maximum_fusion), channel_id=1, replica_groups=mesh['section'=16,'frame'=32] {'section'}, dimensions={0} | all-to-all | bytes 196608 | tf_op jit(solution)/shard_map/all_to_all | solution.py:293
  (97 shorter events, 50.8 us)
Async XLA Ops:
  7.2 24.1 %copy-start = (bf16[1,256,128]{2,1,0:T(8,128)(2,1)S(1)}, bf16[1,256,128]{2,1,0:T(8,128)(2,1)}, u32[]{:S(2)}) copy-start(bf16[1,256,128]{2,1,0:T(8,128)(2,1)} %param.21) | copy-start | bytes 196612
  7.2 24.1 %copy-start.1 = (bf16[1,256,128]{2,1,0:T(8,128)(2,1)S(1)}, bf16[1,256,128]{2,1,0:T(8,128)(2,1)}, u32[]{:S(2)}) copy-start(bf16[1,256,128]{2,1,0:T(8,128)(2,1)} %param.22) | copy-start | bytes 196612
  8.9 19.2 %all-to-all-start = ((bf16[32,64,128]{2,1,0:T(8,128)(2,1)}), bf16[32,64,128]{2,1,0:T(8,128)(2,1)}, u32[]{:S(2)}, u32[]{:S(2)}) async-start(bf16[32,64,128]{2,1,0:T(8,128)(2,1)} %broadcast_in_dim.48), calls=%async_computation | async-start | bytes 1048576 | tf_op jit(solution)/shard_map/all_to_all | solution.py:235
  19.9 22.3 %copy-start.6 = (s32[4,7]{1,0:T(4,128)S(1)}, s32[4,7]{1,0:T(4,128)}, u32[]{:S(2)}) copy-start(s32[4,7]{1,0:T(4,128)} %param.29) | copy-start | bytes 340
  19.9 24.3 %copy-start.7 = (s32[4]{0:T(128)S(1)}, s32[4]{0:T(128)}, u32[]{:S(2)}) copy-start(s32[4]{0:T(128)} %param.30) | copy-start | bytes 52
  31.3 33.5 %copy-start.5 = (bf16[1024,64]{0,1:T(8,128)(2,1)S(1)}, bf16[1024,64]{0,1:T(8,128)(2,1)}, u32[]{:S(2)}) copy-start(bf16[1024,64]{0,1:T(8,128)(2,1)} %param.25) | copy-start | bytes 393220
  33.5 0.8 copy-start.2
  34.3 16.7 %all-to-all-start.1 = ((bf16[32,64,128]{2,1,0:T(8,128)(2,1)}), bf16[32,64,128]{2,1,0:T(8,128)(2,1)}, u32[]{:S(2)}, u32[]{:S(2)}) async-start(bf16[32,64,128]{2,1,0:T(8,128)(2,1)} %copy-done.2), calls=%async_computation.1 | async-start | bytes 1048576 | tf_op jit(solution)/shard_map/all_to_all | solution.py:235
  56.4 0.8 copy-start.3
  57.2 15.9 %all-to-all-start.2 = ((bf16[32,64,128]{2,1,0:T(8,128)(2,1)}), bf16[32,64,128]{2,1,0:T(8,128)(2,1)}, u32[]{:S(2)}, u32[]{:S(2)}) async-start(bf16[32,64,128]{2,1,0:T(8,128)(2,1)} %copy-done.3), calls=%async_computation.2 | async-start | bytes 1048576 | tf_op jit(solution)/shard_map/all_to_all | solution.py:235
  63.1 345.3 %all-gather.20.cloned.1.call-start = ((), (), s32[]{:S(2)}) async-start(), calls=%async_computation.20 | async-start | bytes 17842176 | tf_op jit(solution)/shard_map/all_gather | solution.py:224
  400.2 0.8 copy-start.4
  401.0 19.3 %all-to-all-start.17 = ((bf16[32,64,128]{2,1,0:T(8,128)(2,1)}), bf16[32,64,128]{2,1,0:T(8,128)(2,1)}, u32[]{:S(2)}, u32[]{:S(2)}) async-start(bf16[32,64,128]{2,1,0:T(8,128)(2,1)} %copy-done.4), calls=%async_computation.17 | async-start | bytes 1048576 | tf_op jit(solution)/shard_map/all_to_all | solution.py:235
  426.6 12.9 %all-to-all-start.18 = ((bf16[32,4,128]{2,1,0:T(4,128)(2,1)}), bf16[32,4,128]{2,1,0:T(4,128)(2,1)S(1)}, u32[]{:S(2)}, u32[]{:S(2)}) async-start(bf16[32,4,128]{2,1,0:T(4,128)(2,1)} %bitcast.27), calls=%async_computation.18 | async-start | bytes 65536 | tf_op jit(solution)/shard_map/all_to_all | solution.py:256
  435.0 17.9 %copy-start.8 = (f32[4,8,1024]{2,1,0:T(8,128)S(1)}, f32[4,8,1024]{2,1,0:T(8,128)}, u32[]{:S(2)}) copy-start(f32[4,8,1024]{2,1,0:T(8,128)} %fusion.26) | copy-start | bytes 393220
Sparse Core Ops, SparseCore 0:
  70.6 128.2 all-gather.19
where the time goes:
time: 498 us; the launch traced here: 495 us
  blocking collectives  320 us (64%)
  Pallas kernels  40.7 us (8%)
  starting transfers between devices  36.6 us (7%)
  matrix products  30 us (6%)
  local copies, waits for them, and re-layouts  28.2 us (6%)
  waiting for transfers between devices  17.2 us (3%)
  between operations  14.6 us (3%)
  other arithmetic  7.65 us (2%)
    all_to_all x14, blocking collectives, pass_on(): lax.all_to_all(send, BOTH, split_axis=0, concat_axis=0, tiled=True, axis_...  259 us
    pallas_call x18, Pallas kernels, layer_step(): pl.pallas_call(layer_kernel, out_shape=(jax.ShapeDtypeStruct(where.shape,...  40.7 us
    all_gather x18, blocking collectives, layer(): rows = lax.all_gather(got, BOTH, axis=0, axis_index_groups=core_pairs())  39.7 us
    all_to_all x4, starting transfers between devices, pass_on(): lax.all_to_all(send, BOTH, split_axis=0, concat_axis=0, tiled=True, axis_...  29.1 us
    all_to_all x1, blocking collectives, body(): lax.all_to_all(results, 'section', split_axis=0, concat_axis=0, tiled=True)  19.6 us
    dot_general x5, matrix products, contract_last(): lax.dot_general(a, b, (((1,), (1,)), ((), ())), preferred_element_type=jn...  15.6 us
    all_to_all x4, waiting for transfers between devices, pass_on(): lax.all_to_all(send, BOTH, split_axis=0, concat_axis=0, tiled=True, axis_...  12.6 us
    unnamed x24, local copies, waits for them, and re-layouts  11.1 us
  transfers between devices with their start and end apart: 6, of which 4 were waited for; matrix products, arithmetic and copies ran while one was open for 6% of the time, Pallas kernels for 7%

commit v1 on v0

--- a/solution.py
+++ b/solution.py
@@ -24,14 +24,23 @@
 
 def plane_pairs(first):
     lows = range(first, SECTIONS - 1, 2)
-    groups = [
-        [device_id(low + up, chip, core) for up in range(2) for chip in range(CHIPS)]
+    pairs = [
+        [device_id(low + up, chip, core) for up in range(2)]
         for low in lows
+        for chip in range(CHIPS)
         for core in range(2)
     ]
     for alone in sorted(set(range(SECTIONS)) - {low + up for low in lows for up in range(2)}):
-        groups.append([device_id(alone, chip, core) for core in range(2) for chip in range(CHIPS)])
-    return groups
+        pairs += [[device_id(alone, chip, core) for core in range(2)] for chip in range(CHIPS)]
+    return pairs
+
+
+def plane_groups():
+    return [
+        [device_id(section, chip, core) for chip in range(CHIPS)]
+        for section in range(SECTIONS)
+        for core in range(2)
+    ]
 
 
 def core_pairs():
@@ -111,8 +120,7 @@
     found_ref[...] = held_ref[...]
     pl.when(block == 0)(lambda: keep(early))
     pl.when(block == 2)(lambda: keep(late))
-    for at in range(send_ref.shape[0]):
-        send_ref[at] = x_out
+    send_ref[...] = x_out
 
 
 def layer_step(where, rows, weight, stash_k, stash_v, held):
@@ -123,7 +131,7 @@
         out_shape=(
             jax.ShapeDtypeStruct(where.shape, where.dtype),
             jax.ShapeDtypeStruct(held.shape, held.dtype),
-            jax.ShapeDtypeStruct((2 * CHIPS, CH, HEAD), jnp.bfloat16),
+            jax.ShapeDtypeStruct((CH, HEAD), jnp.bfloat16),
         ),
         in_specs=[smem, vmem, vmem, vmem, vmem, vmem],
         out_specs=(smem, vmem, vmem),
@@ -228,28 +236,27 @@
     weight = (weight.astype(jnp.float32) * gain).astype(jnp.bfloat16)
     stash_k, stash_v = cache_keys[0], cache_values[0]
 
-    def spread_out(block):
-        return jnp.broadcast_to(block[None], (2 * CHIPS,) + block.shape)
-
-    def pass_on(first, send):
-        return lax.all_to_all(
-            send, BOTH, split_axis=0, concat_axis=0, tiled=True, axis_index_groups=plane_pairs(first)
+    def layer(where, block, held):
+        got = lax.all_to_all(
+            jnp.broadcast_to(block[None], (CHIPS,) + block.shape),
+            BOTH,
+            split_axis=0,
+            concat_axis=0,
+            tiled=True,
+            axis_index_groups=plane_groups(),
         )
-
-    def layer(where, got, held):
         rows = lax.all_gather(got, BOTH, axis=0, axis_index_groups=core_pairs())
         return layer_step(where, rows, weight, stash_k, stash_v, held)
 
     where = jnp.stack([jnp.int32(0), section_id, frame_id // 2, core]).astype(jnp.int32)
     held = jnp.zeros((3, 2 * CH, HEAD), jnp.bfloat16)
-    entry = pass_on(0, spread_out(jnp.where(section_id % 2 == 0, inflow[:CH], inflow[CH:])))
-    second = entry[CHIPS:]
-    where, held, send = layer(where, entry[:CHIPS], held)
+    where, held, block = layer(where, inflow[:CH], held)
     for tick in range(1, SECTIONS + 2):
-        got = pass_on((tick - 1) % 2, send)[:CHIPS]
+        pairs = plane_pairs((tick - 1) % 2)
+        block = lax.all_gather(block, BOTH, axis=0, axis_index_groups=pairs)[0]
         if tick == 2:
-            got = jnp.where(section_id == 0, second, got)
-        where, held, send = layer(where, got, held)
+            block = jnp.where(section_id == 0, inflow[CH:], block)
+        where, held, block = layer(where, block, held)
     new_keys, new_values, finished = held[0], held[1], held[2]
 
     finished = finished.reshape(2 * CHIPS, frames, HEAD)

time: 498 us -> 491 us (0.986)
  blocking collectives: 320 us -> 333 us
  local copies, waits for them, and re-layouts: 28.2 us -> 15.5 us
  starting transfers between devices: 36.6 us -> 28.3 us
    all_gather x0 -> x17, blocking collectives: none -> 79.6 us  [body(): block = lax.all_gather(block, BOTH, axis=0, axis_index_groups=pairs)[0]]
    all_to_all x14 -> x15, blocking collectives: 259 us -> 182 us  [layer(): lax.all_to_all(jnp.broadcast_to(block[None], (CHIPS,) + block.shape), BOT...]
    all_to_all x1, blocking collectives: 19.6 us -> 30.3 us  [body(): lax.all_to_all(results, 'section', split_axis=0, concat_axis=0, tiled=True)]
    all_to_all x4 -> x3, starting transfers between devices: 29.1 us -> 22.2 us  [layer(): lax.all_to_all(jnp.broadcast_to(block[None], (CHIPS,) + block.shape), BOT...]
    unnamed x24 -> x14, local copies, waits for them, and re-layouts: 11.1 us -> 6.39 us
    all_to_all x4 -> x3, waiting for transfers between devices: 12.6 us -> 17 us  [layer(): lax.all_to_all(jnp.broadcast_to(block[None], (CHIPS,) + block.shape), BOT...]
  transfers between devices with their start and end apart: 6 -> 5, of which waited for: 4 -> 4; matrix products, arithmetic and copies ran while one was open for 6% -> 2% of each run, Pallas kernels for 7% -> 8%
where the time goes in v1:
time: 491 us; the launch traced here: 488 us
  blocking collectives  333 us (68%)
  Pallas kernels  40.5 us (8%)
  matrix products  29.3 us (6%)
  starting transfers between devices  28.3 us (6%)
  waiting for transfers between devices  20.4 us (4%)
  local copies, waits for them, and re-layouts  15.5 us (3%)
  between operations  14.6 us (3%)
  other arithmetic  6.1 us (1%)
    all_to_all x15, blocking collectives, layer(): lax.all_to_all(jnp.broadcast_to(block[None], (CHIPS,) + block.shape), BOT...  182 us
    all_gather x17, blocking collectives, body(): block = lax.all_gather(block, BOTH, axis=0, axis_index_groups=pairs)[0]  79.6 us
    pallas_call x18, Pallas kernels, layer_step(): pl.pallas_call(layer_kernel, out_shape=(jax.ShapeDtypeStruct(where.shape,...  40.5 us
    all_gather x18, blocking collectives, layer(): rows = lax.all_gather(got, BOTH, axis=0, axis_index_groups=core_pairs())  39.7 us
    all_to_all x1, blocking collectives, body(): lax.all_to_all(results, 'section', split_axis=0, concat_axis=0, tiled=True)  30.3 us
    all_to_all x3, starting transfers between devices, layer(): lax.all_to_all(jnp.broadcast_to(block[None], (CHIPS,) + block.shape), BOT...  22.2 us
    all_to_all x3, waiting for transfers between devices, layer(): lax.all_to_all(jnp.broadcast_to(block[None], (CHIPS,) + block.shape), BOT...  17 us
    dot_general x5, matrix products, contract_last(): lax.dot_general(a, b, (((1,), (1,)), ((), ())), preferred_element_type=jn...  14.8 us
  transfers between devices with their start and end apart: 5, of which 4 were waited for; matrix products, arithmetic and copies ran while one was open for 2% of the time, Pallas kernels for 8%

profile of v1, /device:TPU:6, one launch (start us, length us, event | category | flops | bytes accessed | tf_op | source)
XLA Modules:
  0.0 487.9 jit_solution(32282871298582001)
XLA Ops:
  20.8 9.8 %all-to-all-start = ((bf16[16,64,128]{2,1,0:T(8,128)(2,1)}), bf16[16,64,128]{2,1,0:T(8,128)(2,1)}, u32[]{:S(2)}, u32[]{:S(2)}) async-start(bf16[16,64,128]{2,1,0:T(8,128)(2,1)} %broadcast_in_dim.166), calls=%async_computation | async-start | bytes 524288 | tf_op jit(solution)/shard_map/all_to_all | solution.py:240
  31.4 2.2 multiply_convert_fusion.weight_ref
  33.8 4.0 all-to-all-done
  37.8 2.4 all-gather
  40.2 2.2 shard_map.183
  42.4 4.7 all-gather.1
  48.0 6.2 %all-to-all-start.1 = ((bf16[16,64,128]{2,1,0:T(8,128)(2,1)}), bf16[16,64,128]{2,1,0:T(8,128)(2,1)}, u32[]{:S(2)}, u32[]{:S(2)}) async-start(bf16[16,64,128]{2,1,0:T(8,128)(2,1)} %broadcast_in_dim.169), calls=%async_computation.1 | async-start | bytes 524288 | tf_op jit(solution)/shard_map/all_to_all | solution.py:240
  54.2 6.5 %all-to-all-done.1 = bf16[16,64,128]{2,1,0:T(8,128)(2,1)} async-done(((bf16[16,64,128]{2,1,0:T(8,128)(2,1)}), bf16[16,64,128]{2,1,0:T(8,128)(2,1)}, u32[]{:S(2)}, u32[]{:S(2)}) %all-to-all-start.1) | async-done | bytes 262176 | tf_op jit(solution)/shard_map/all_to_all | solution.py:240
  60.7 2.4 all-gather.2
  63.0 2.3 shard_map.184
  67.2 12.3 %all_to_all.100 = bf16[16,64,128]{2,1,0:T(8,128)(2,1)S(1)} all-to-all(bf16[16,64,128]{2,1,0:T(8,128)(2,1)S(1)} %broadcast_in_dim.170), channel_id=1, replica_groups={{0,2,4,6,8,10,12,14,16,18,20,22,24,26,28,30},{1,3,5,7,9,11,13,15,17,19,..., dimensions={0} | all-to-all | bytes 524288 | tf_op jit(solution)/shard_map/all_to_all | solution.py:240
  81.7 2.3 shard_map.185
  83.9 5.2 %all-gather.5 = bf16[128,128]{1,0:T(8,128)(2,1)S(1)} all-gather(bf16[64,128]{1,0:T(8,128)(2,1)S(1)} %get-tuple-element.63), channel_id=7, replica_groups={{0,32},{1,33},{2,34},{3,35},{4,36},{5,37},{6,38},{7,39},{8,40},{9,41},{..., dimensions={0}, use_global_device_ids=true | all-gather | bytes 49152 | tf_op jit(solution)/shard_map/all_gather | solution.py:256
  89.2 11.9 %all_to_all.101 = bf16[16,64,128]{2,1,0:T(8,128)(2,1)S(1)} all-to-all(bf16[16,64,128]{2,1,0:T(8,128)(2,1)S(1)} %broadcast_in_dim.172), channel_id=1, replica_groups={{0,2,4,6,8,10,12,14,16,18,20,22,24,26,28,30},{1,3,5,7,9,11,13,15,17,19,..., dimensions={0} | all-to-all | bytes 524288 | tf_op jit(solution)/shard_map/all_to_all | solution.py:240
  103.3 2.2 shard_map.186
  107.4 12.3 %all_to_all.102 = bf16[16,64,128]{2,1,0:T(8,128)(2,1)S(1)} all-to-all(bf16[16,64,128]{2,1,0:T(8,128)(2,1)S(1)} %broadcast_in_dim.174), channel_id=1, replica_groups={{0,2,4,6,8,10,12,14,16,18,20,22,24,26,28,30},{1,3,5,7,9,11,13,15,17,19,..., dimensions={0} | all-to-all | bytes 524288 | tf_op jit(solution)/shard_map/all_to_all | solution.py:240
  121.9 2.2 shard_map.187
  124.2 7.4 %all-gather.9 = bf16[128,128]{1,0:T(8,128)(2,1)S(1)} all-gather(bf16[64,128]{1,0:T(8,128)(2,1)S(1)} %get-tuple-element.69), channel_id=11, replica_groups={{0,32},{1,33},{2,34},{3,35},{4,36},{5,37},{6,38},{7,39},{8,40},{9,41},{..., dimensions={0}, use_global_device_ids=true | all-gather | bytes 49152 | tf_op jit(solution)/shard_map/all_gather | solution.py:256
  131.7 12.0 %all_to_all.103 = bf16[16,64,128]{2,1,0:T(8,128)(2,1)S(1)} all-to-all(bf16[16,64,128]{2,1,0:T(8,128)(2,1)S(1)} %broadcast_in_dim.176), channel_id=1, replica_groups={{0,2,4,6,8,10,12,14,16,18,20,22,24,26,28,30},{1,3,5,7,9,11,13,15,17,19,..., dimensions={0} | all-to-all | bytes 524288 | tf_op jit(solution)/shard_map/all_to_all | solution.py:240
  143.7 2.2 all-gather.10
  145.9 2.3 shard_map.188
  150.0 12.3 %all_to_all.104 = bf16[16,64,128]{2,1,0:T(8,128)(2,1)S(1)} all-to-all(bf16[16,64,128]{2,1,0:T(8,128)(2,1)S(1)} %broadcast_in_dim.178), channel_id=1, replica_groups={{0,2,4,6,8,10,12,14,16,18,20,22,24,26,28,30},{1,3,5,7,9,11,13,15,17,19,..., dimensions={0} | all-to-all | bytes 524288 | tf_op jit(solution)/shard_map/all_to_all | solution.py:240
  164.4 2.3 shard_map.189
  166.7 8.0 %all-gather.13 = bf16[128,128]{1,0:T(8,128)(2,1)S(1)} all-gather(bf16[64,128]{1,0:T(8,128)(2,1)S(1)} %get-tuple-element.75), channel_id=15, replica_groups={{0,32},{1,33},{2,34},{3,35},{4,36},{5,37},{6,38},{7,39},{8,40},{9,41},{..., dimensions={0}, use_global_device_ids=true | all-gather | bytes 49152 | tf_op jit(solution)/shard_map/all_gather | solution.py:256
  174.8 11.9 %all_to_all.105 = bf16[16,64,128]{2,1,0:T(8,128)(2,1)S(1)} all-to-all(bf16[16,64,128]{2,1,0:T(8,128)(2,1)S(1)} %broadcast_in_dim.180), channel_id=1, replica_groups={{0,2,4,6,8,10,12,14,16,18,20,22,24,26,28,30},{1,3,5,7,9,11,13,15,17,19,..., dimensions={0} | all-to-all | bytes 524288 | tf_op jit(solution)/shard_map/all_to_all | solution.py:240
  188.9 2.2 shard_map.190
  193.0 12.3 %all_to_all.106 = bf16[16,64,128]{2,1,0:T(8,128)(2,1)S(1)} all-to-all(bf16[16,64,128]{2,1,0:T(8,128)(2,1)S(1)} %broadcast_in_dim.182), channel_id=1, replica_groups={{0,2,4,6,8,10,12,14,16,18,20,22,24,26,28,30},{1,3,5,7,9,11,13,15,17,19,..., dimensions={0} | all-to-all | bytes 524288 | tf_op jit(solution)/shard_map/all_to_all | solution.py:240
  205.3 2.2 all-gather.16
  207.5 2.3 shard_map.191
  209.7 7.9 %all-gather.17 = bf16[128,128]{1,0:T(8,128)(2,1)S(1)} all-gather(bf16[64,128]{1,0:T(8,128)(2,1)S(1)} %get-tuple-element.81), channel_id=19, replica_groups={{0,32},{1,33},{2,34},{3,35},{4,36},{5,37},{6,38},{7,39},{8,40},{9,41},{..., dimensions={0}, use_global_device_ids=true | all-gather | bytes 49152 | tf_op jit(solution)/shard_map/all_gather | solution.py:256
  217.7 11.9 %all_to_all.107 = bf16[16,64,128]{2,1,0:T(8,128)(2,1)S(1)} all-to-all(bf16[16,64,128]{2,1,0:T(8,128)(2,1)S(1)} %broadcast_in_dim.184), channel_id=1, replica_groups={{0,2,4,6,8,10,12,14,16,18,20,22,24,26,28,30},{1,3,5,7,9,11,13,15,17,19,..., dimensions={0} | all-to-all | bytes 524288 | tf_op jit(solution)/shard_map/all_to_all | solution.py:240
  229.6 2.2 all-gather.18
  231.8 2.3 shard_map.192
  236.1 12.3 %all_to_all.108 = bf16[16,64,128]{2,1,0:T(8,128)(2,1)S(1)} all-to-all(bf16[16,64,128]{2,1,0:T(8,128)(2,1)S(1)} %broadcast_in_dim.186), channel_id=1, replica_groups={{0,2,4,6,8,10,12,14,16,18,20,22,24,26,28,30},{1,3,5,7,9,11,13,15,17,19,..., dimensions={0} | all-to-all | bytes 524288 | tf_op jit(solution)/shard_map/all_to_all | solution.py:240
  250.5 2.3 shard_map.193
  252.8 7.9 %all-gather.21 = bf16[128,128]{1,0:T(8,128)(2,1)S(1)} all-gather(bf16[64,128]{1,0:T(8,128)(2,1)S(1)} %get-tuple-element.87), channel_id=23, replica_groups={{0,32},{1,33},{2,34},{3,35},{4,36},{5,37},{6,38},{7,39},{8,40},{9,41},{..., dimensions={0}, use_global_device_ids=true | all-gather | bytes 49152 | tf_op jit(solution)/shard_map/all_gather | solution.py:256
  260.8 11.9 %all_to_all.109 = bf16[16,64,128]{2,1,0:T(8,128)(2,1)S(1)} all-to-all(bf16[16,64,128]{2,1,0:T(8,128)(2,1)S(1)} %broadcast_in_dim.188), channel_id=1, replica_groups={{0,2,4,6,8,10,12,14,16,18,20,22,24,26,28,30},{1,3,5,7,9,11,13,15,17,19,..., dimensions={0} | all-to-all | bytes 524288 | tf_op jit(solution)/shard_map/all_to_all | solution.py:240
  274.9 2.2 shard_map.194
  279.0 12.3 %all_to_all.110 = bf16[16,64,128]{2,1,0:T(8,128)(2,1)S(1)} all-to-all(bf16[16,64,128]{2,1,0:T(8,128)(2,1)S(1)} %broadcast_in_dim.190), channel_id=1, replica_groups={{0,2,4,6,8,10,12,14,16,18,20,22,24,26,28,30},{1,3,5,7,9,11,13,15,17,19,..., dimensions={0} | all-to-all | bytes 524288 | tf_op jit(solution)/shard_map/all_to_all | solution.py:240
  293.4 2.3 shard_map.195
  295.7 7.9 %all-gather.25 = bf16[128,128]{1,0:T(8,128)(2,1)S(1)} all-gather(bf16[64,128]{1,0:T(8,128)(2,1)S(1)} %get-tuple-element.93), channel_id=27, replica_groups={{0,32},{1,33},{2,34},{3,35},{4,36},{5,37},{6,38},{7,39},{8,40},{9,41},{..., dimensions={0}, use_global_device_ids=true | all-gather | bytes 49152 | tf_op jit(solution)/shard_map/all_gather | solution.py:256
  303.6 11.9 %all_to_all.111 = bf16[16,64,128]{2,1,0:T(8,128)(2,1)S(1)} all-to-all(bf16[16,64,128]{2,1,0:T(8,128)(2,1)S(1)} %broadcast_in_dim.192), channel_id=1, replica_groups={{0,2,4,6,8,10,12,14,16,18,20,22,24,26,28,30},{1,3,5,7,9,11,13,15,17,19,..., dimensions={0} | all-to-all | bytes 524288 | tf_op jit(solution)/shard_map/all_to_all | solution.py:240
  317.8 2.3 shard_map.196
  321.9 12.3 %all_to_all.112 = bf16[16,64,128]{2,1,0:T(8,128)(2,1)S(1)} all-to-all(bf16[16,64,128]{2,1,0:T(8,128)(2,1)S(1)} %broadcast_in_dim.194), channel_id=1, replica_groups={{0,2,4,6,8,10,12,14,16,18,20,22,24,26,28,30},{1,3,5,7,9,11,13,15,17,19,..., dimensions={0} | all-to-all | bytes 524288 | tf_op jit(solution)/shard_map/all_to_all | solution.py:240
  336.3 2.2 shard_map.197
  338.6 7.9 %all-gather.29 = bf16[128,128]{1,0:T(8,128)(2,1)S(1)} all-gather(bf16[64,128]{1,0:T(8,128)(2,1)S(1)} %get-tuple-element.99), channel_id=31, replica_groups={{0,32},{1,33},{2,34},{3,35},{4,36},{5,37},{6,38},{7,39},{8,40},{9,41},{..., dimensions={0}, use_global_device_ids=true | all-gather | bytes 49152 | tf_op jit(solution)/shard_map/all_gather | solution.py:256
  346.5 11.9 %all_to_all.113 = bf16[16,64,128]{2,1,0:T(8,128)(2,1)S(1)} all-to-all(bf16[16,64,128]{2,1,0:T(8,128)(2,1)S(1)} %broadcast_in_dim.196), channel_id=1, replica_groups={{0,2,4,6,8,10,12,14,16,18,20,22,24,26,28,30},{1,3,5,7,9,11,13,15,17,19,..., dimensions={0} | all-to-all | bytes 524288 | tf_op jit(solution)/shard_map/all_to_all | solution.py:240
  360.7 2.2 shard_map.198
  364.8 12.3 %all_to_all.114 = bf16[16,64,128]{2,1,0:T(8,128)(2,1)S(1)} all-to-all(bf16[16,64,128]{2,1,0:T(8,128)(2,1)S(1)} %broadcast_in_dim.198), channel_id=1, replica_groups={{0,2,4,6,8,10,12,14,16,18,20,22,24,26,28,30},{1,3,5,7,9,11,13,15,17,19,..., dimensions={0} | all-to-all | bytes 524288 | tf_op jit(solution)/shard_map/all_to_all | solution.py:240
  379.2 2.3 shard_map.199
  381.5 7.9 %all-gather.33 = bf16[128,128]{1,0:T(8,128)(2,1)S(1)} all-gather(bf16[64,128]{1,0:T(8,128)(2,1)S(1)} %get-tuple-element.105), channel_id=35, replica_groups={{0,32},{1,33},{2,34},{3,35},{4,36},{5,37},{6,38},{7,39},{8,40},{9,41},{..., dimensions={0}, use_global_device_ids=true | all-gather | bytes 49152 | tf_op jit(solution)/shard_map/all_gather | solution.py:256
  390.2 6.2 %all-to-all-start.17 = ((bf16[16,64,128]{2,1,0:T(8,128)(2,1)}), bf16[16,64,128]{2,1,0:T(8,128)(2,1)}, u32[]{:S(2)}, u32[]{:S(2)}) async-start(bf16[16,64,128]{2,1,0:T(8,128)(2,1)} %broadcast_in_dim.200), calls=%async_computation.17 | async-start | bytes 524288 | tf_op jit(solution)/shard_map/all_to_all | solution.py:240
  396.4 6.5 %all-to-all-done.17 = bf16[16,64,128]{2,1,0:T(8,128)(2,1)} async-done(((bf16[16,64,128]{2,1,0:T(8,128)(2,1)}), bf16[16,64,128]{2,1,0:T(8,128)(2,1)}, u32[]{:S(2)}, u32[]{:S(2)}) %all-to-all-start.17) | async-done | bytes 262176 | tf_op jit(solution)/shard_map/all_to_all | solution.py:240
  402.9 2.4 all-gather.34
  405.2 2.3 shard_map.200
  408.1 6.0 %all-to-all-start.18 = ((bf16[32,4,128]{2,1,0:T(4,128)(2,1)}), bf16[32,4,128]{2,1,0:T(4,128)(2,1)S(1)}, u32[]{:S(2)}, u32[]{:S(2)}) async-start(bf16[32,4,128]{2,1,0:T(4,128)(2,1)} %bitcast.27), calls=%async_computation.18 | async-start | bytes 65536 | tf_op jit(solution)/shard_map/all_to_all | solution.py:263
  416.3 3.3 all-to-all-done.18
  419.6 5.6 %fusion.2 = f32[4,1024]{1,0:T(4,128)S(1)} fusion(bf16[1024,8448]{1,0:T(8,128)(2,1)} %all-gather.37.cloned.1.call-done, bf16[32,4,128]{2,1,0:T(4,128)(2,1)S(1)} %all-to-all-done.18), kind=kOutput, calls=%fused_computation.3 | convolution fusion | flops 33554432 | bytes 8437760 | tf_op jit(solution)/shard_map/dot_general | solution.py:147
  425.3 2.3 fusion.11
  427.6 2.3 fusion.9
  430.7 2.3 fusion.7
  433.0 2.3 fusion.26
  443.9 5.5 %fusion.4 = bf16[4,4096]{1,0:T(4,128)(2,1)S(1)} fusion(bf16[1024,8448]{1,0:T(8,128)(2,1)} %all-gather.37.cloned.1.call-done, f32[4,1024]{1,0:T(4,128)S(1)} %fusion.17, f32[4,1024]{1,0:T(4,128)S(1)} %fusion.20, f32[4,1024]{1,0:T(4,128)S(1)} %convert_reduce_fusion, bf16[4,1024]{1,0:T(4,128)(2,1)S(1)} %get-tuple-element.110), kind=kOutput, calls=%fused_computation.6 | convolution fusion | flops 41975808 | bytes 10575872 | tf_op jit(solution)/shard_map/dot_general | solution.py:291
  449.5 30.3 %all_to_all.115 = bf16[16,24,128]{2,1,0:T(8,128)(2,1)S(1)} all-to-all(bf16[16,24,128]{2,1,0:T(8,128)(2,1)S(1)} %pad_maximum_fusion), channel_id=1, replica_groups=mesh['section'=16,'frame'=32] {'section'}, dimensions={0} | all-to-all | bytes 196608 | tf_op jit(solution)/shard_map/all_to_all | solution.py:300
  (119 shorter events, 71.1 us)
Async XLA Ops:
  7.2 33.0 %copy-start = (bf16[1,256,128]{2,1,0:T(8,128)(2,1)S(1)}, bf16[1,256,128]{2,1,0:T(8,128)(2,1)}, u32[]{:S(2)}) copy-start(bf16[1,256,128]{2,1,0:T(8,128)(2,1)} %param.21) | copy-start | bytes 196612
  7.2 33.0 %copy-start.1 = (bf16[1,256,128]{2,1,0:T(8,128)(2,1)S(1)}, bf16[1,256,128]{2,1,0:T(8,128)(2,1)}, u32[]{:S(2)}) copy-start(bf16[1,256,128]{2,1,0:T(8,128)(2,1)} %param.22) | copy-start | bytes 196612
  7.2 406.9 %all-gather.37.cloned.1.call-start = ((), (), s32[]{:S(2)}) async-start(), calls=%async_computation.20 | async-start | bytes 17842176 | tf_op jit(solution)/shard_map/all_gather | solution.py:232
  18.5 0.8 copy-start.2
  20.8 16.9 %all-to-all-start = ((bf16[16,64,128]{2,1,0:T(8,128)(2,1)}), bf16[16,64,128]{2,1,0:T(8,128)(2,1)}, u32[]{:S(2)}, u32[]{:S(2)}) async-start(bf16[16,64,128]{2,1,0:T(8,128)(2,1)} %broadcast_in_dim.166), calls=%async_computation | async-start | bytes 524288 | tf_op jit(solution)/shard_map/all_to_all | solution.py:240
  33.6 33.5 %copy-start.3 = (bf16[128,128]{1,0:T(8,128)(2,1)S(1)}, bf16[128,128]{1,0:T(8,128)(2,1)}, u32[]{:S(2)}) copy-start(bf16[128,128]{1,0:T(8,128)(2,1)} %param.16) | copy-start | bytes 98308
  48.0 12.7 %all-to-all-start.1 = ((bf16[16,64,128]{2,1,0:T(8,128)(2,1)}), bf16[16,64,128]{2,1,0:T(8,128)(2,1)}, u32[]{:S(2)}, u32[]{:S(2)}) async-start(bf16[16,64,128]{2,1,0:T(8,128)(2,1)} %broadcast_in_dim.169), calls=%async_computation.1 | async-start | bytes 524288 | tf_op jit(solution)/shard_map/all_to_all | solution.py:240
  390.2 12.7 %all-to-all-start.17 = ((bf16[16,64,128]{2,1,0:T(8,128)(2,1)}), bf16[16,64,128]{2,1,0:T(8,128)(2,1)}, u32[]{:S(2)}, u32[]{:S(2)}) async-start(bf16[16,64,128]{2,1,0:T(8,128)(2,1)} %broadcast_in_dim.200), calls=%async_computation.17 | async-start | bytes 524288 | tf_op jit(solution)/shard_map/all_to_all | solution.py:240
  408.1 11.5 %all-to-all-start.18 = ((bf16[32,4,128]{2,1,0:T(4,128)(2,1)}), bf16[32,4,128]{2,1,0:T(4,128)(2,1)S(1)}, u32[]{:S(2)}, u32[]{:S(2)}) async-start(bf16[32,4,128]{2,1,0:T(4,128)(2,1)} %bitcast.27), calls=%async_computation.18 | async-start | bytes 65536 | tf_op jit(solution)/shard_map/all_to_all | solution.py:263
Sparse Core Ops, SparseCore 0:
  19.5 113.8 all-gather.36

commit v2 on v1

--- a/solution.py
+++ b/solution.py
@@ -9,6 +9,7 @@
 CH = 64
 CACHE = 256
 DHEAD = 64
+LEVELS = 8
 SECTIONS = 16
 CHIPS = 16
 PIECES = 8
@@ -143,47 +144,197 @@
     )(where, rows, weight, stash_k, stash_v, held)
 
 
-def contract_last(a, b):
-    return lax.dot_general(a, b, (((1,), (1,)), ((), ())), preferred_element_type=jnp.float32)
-
-
-def depth_forward(z, whole, in_head, frames, levels):
-    width = z.shape[1]
-    high = lax.Precision.HIGHEST
-    heads = in_head.shape[1]
-    query, key, value = (
-        contract_last(z, whole[at]).reshape(frames, levels, width) for at in range(3)
+def depth_kernel(
+    core_ref,
+    temporal_ref,
+    shares_ref,
+    result_ref,
+    w_in,
+    w_rest,
+    extra,
+    in_sem,
+    rest_sem,
+    extra_sem,
+):
+    width, features = w_in.shape
+    frames = temporal_ref.shape[1]
+    columns = 2 * HEAD
+    rows = columns // LEVELS
+    heads = width // DHEAD
+    shift = columns // 2
+    fetch_extra = pltpu.make_async_copy(
+        shares_ref.at[:, pl.ds(pl.multiple_of(features + 4 * width + core_ref[0] * HEAD, HEAD), HEAD)],
+        extra,
+        extra_sem,
     )
-    pairs = (query[:, :, None, :] * key[:, None, :, :]).reshape(-1, width)
-    scores = jnp.dot(pairs, in_head, precision=high).reshape(frames, levels, levels, heads)
-    scores = scores * DHEAD ** (-0.5)
-    causal = jnp.arange(levels)[:, None] >= jnp.arange(levels)[None, :]
-    scores = jnp.where(causal[None, :, :, None], scores, MASKED)
-    peak = jnp.max(scores, axis=2, keepdims=True)
-    raised = jnp.exp(scores - peak)
-    probs = raised / jnp.sum(raised, axis=2, keepdims=True)
-    spread = jnp.dot(probs.reshape(-1, heads), in_head.T, precision=high).reshape(
-        frames, levels, levels, width
+    fetch_extra.start()
+    fetch_rest = []
+    for at in range(4):
+        span = pl.ds(features + at * width, width)
+        fetch_rest.append(
+            pltpu.make_async_copy(shares_ref.at[:, span], w_rest.at[at], rest_sem.at[at])
+        )
+    fetch_in = []
+    step = width // PIECES
+    for piece in range(PIECES):
+        span = pl.ds(piece * step, step)
+        fetch_in.append(
+            pltpu.make_async_copy(
+                shares_ref.at[span, pl.ds(0, features)], w_in.at[span], in_sem.at[piece]
+            )
+        )
+    fetch_rest[3].start()
+    for copy in fetch_in:
+        copy.start()
+    for copy in fetch_rest[:3]:
+        copy.start()
+
+    def iota(shape, axis):
+        return lax.broadcasted_iota(jnp.int32, shape, axis)
+
+    def product(left, right):
+        return jnp.dot(left, right, preferred_element_type=jnp.float32)
+
+    source, target = iota((HEAD, columns), 0), iota((HEAD, columns), 1)
+    distance, level = target // rows, target % LEVELS
+    same = (source == target % rows).astype(jnp.bfloat16)
+    behind = ((source == target % rows - distance) & (level >= distance)).astype(jnp.bfloat16)
+
+    fetch_extra.wait()
+    known = extra[...]
+    own = (iota((HEAD, HEAD), 0) == iota((HEAD, HEAD), 1) + rows).astype(jnp.bfloat16)
+    own = jnp.where(iota((HEAD, HEAD), 1) < rows, own, jnp.zeros_like(own))
+    masked = product(known, own).astype(jnp.bfloat16)
+    masked_all = product(masked, same).astype(jnp.bfloat16)
+    fetch_rest[3].wait()
+    w_out = w_rest[3]
+    grad_mixed = product(w_out, masked_all)
+
+    parts = []
+    for at in range(2 * CHIPS):
+        part = temporal_ref[at].astype(jnp.float32)
+        part = jnp.broadcast_to(part[:, None, :], (frames, LEVELS, HEAD))
+        parts.append(part.reshape(rows, HEAD).astype(jnp.bfloat16))
+    x_rows = jnp.concatenate(parts, axis=1)
+    bases = []
+    for piece in range(PIECES):
+        fetch_in[piece].wait()
+        bases.append(
+            lax.dot_general(
+                w_in[pl.ds(piece * step, step), :],
+                x_rows,
+                (((1,), (1,)), ((), ())),
+                preferred_element_type=jnp.float32,
+            )
+        )
+    base = jnp.concatenate(bases, axis=0)
+    z_narrow = (base + known[:, :rows].astype(jnp.float32)).astype(jnp.bfloat16)
+    z = jnp.concatenate(
+        [z_narrow.astype(jnp.float32), jnp.zeros((width, HEAD - rows), jnp.float32)], axis=1
     )
-    mixed = jnp.sum(spread * value[:, None, :, :], axis=2)
-    return query, key, value, probs, spread, mixed
-
-
-def depth_backward(grad_mixed, query, key, value, probs, spread, in_head):
-    frames, levels, width = query.shape
-    heads = in_head.shape[1]
-    high = lax.Precision.HIGHEST
-    grad_value = jnp.sum(spread * grad_mixed[:, :, None, :], axis=1)
-    pairs = (grad_mixed[:, :, None, :] * value[:, None, :, :]).reshape(-1, width)
-    grad_probs = jnp.dot(pairs, in_head, precision=high).reshape(probs.shape)
-    inner = jnp.sum(grad_probs * probs, axis=2, keepdims=True)
+    z_low = z.astype(jnp.bfloat16)
+    z_same = product(z_low, same).astype(jnp.bfloat16)
+    z_behind = product(z_low, behind).astype(jnp.bfloat16)
+    for copy in fetch_rest[:3]:
+        copy.wait()
+    query = product(w_rest[0], z_same)
+    key = product(w_rest[1], z_behind)
+    value = product(w_rest[2], z_behind)
+
+    def per_head(terms):
+        return jnp.sum(terms.reshape(heads, DHEAD, columns), axis=1)
+
+    def over_heads(terms):
+        return jnp.broadcast_to(terms[:, None, :], (heads, DHEAD, columns)).reshape(width, columns)
+
+    def over_distances(terms, combine):
+        terms = combine(terms, pltpu.roll(terms, shift, 1))
+        terms = combine(terms, pltpu.roll(terms, shift // 2, 1))
+        return combine(terms, pltpu.roll(terms, shift // 4, 1))
+
+    at_column = iota((heads, columns), 1)
+    seen = at_column % LEVELS >= at_column // rows
+    scores = jnp.where(seen, per_head(query * key) * DHEAD ** (-0.5), MASKED)
+    raised = jnp.exp(scores - over_distances(scores, jnp.maximum))
+    probs = raised / over_distances(raised, jnp.add)
+    wide_probs = over_heads(probs)
+    mixed = wide_probs * value
+    mixed = mixed[:, :HEAD] + mixed[:, HEAD:]
+    mixed = mixed + pltpu.roll(mixed, HEAD // 2, 1)
+    mixed = mixed + pltpu.roll(mixed, HEAD // 4, 1)
+    both = jnp.where(iota((width, HEAD), 1) < rows, mixed, pltpu.roll(z, rows, 1)).T
+    depth_out = both[rows : 2 * rows] + product(both[:rows].astype(jnp.bfloat16), w_out)
+    depth_out = depth_out.astype(jnp.bfloat16).astype(jnp.float32)
+
+    grad_probs = per_head(grad_mixed * value)
+    inner = over_distances(grad_probs * probs, jnp.add)
     grad_scores = probs * (grad_probs - inner) * DHEAD ** (-0.5)
-    wide = jnp.dot(grad_scores.reshape(-1, heads), in_head.T, precision=high).reshape(
-        frames, levels, levels, width
-    )
-    grad_query = jnp.sum(wide * key[:, None, :, :], axis=2)
-    grad_key = jnp.sum(wide * query[:, :, None, :], axis=1)
-    return grad_query, grad_key, grad_value
+    wide_scores = over_heads(grad_scores)
+
+    def to_frames(slot, limit):
+        at, to = iota((limit, HEAD), 0), iota((limit, HEAD), 1)
+        return (at % rows // LEVELS + 8 * slot == to).astype(jnp.bfloat16)
+
+    summed = product(masked, jnp.where(iota((HEAD, HEAD), 0) < rows, to_frames(3, HEAD), 0))
+    for slot, terms in enumerate((wide_scores * key, wide_scores * query, wide_probs * grad_mixed)):
+        high = terms.astype(jnp.bfloat16)
+        low = (terms - high.astype(jnp.float32)).astype(jnp.bfloat16)
+        pick = to_frames(slot, columns)
+        summed = summed + product(high, pick) + product(low, pick)
+    summed = summed.T
+    grad_base = summed[24:32]
+    for slot in range(3):
+        grad_base = grad_base + product(
+            summed[8 * slot : 8 * slot + 8].astype(jnp.bfloat16), w_rest[slot]
+        )
+    grad = product(grad_base.astype(jnp.bfloat16), w_in[...])
+
+    left = iota((rows // 2, HEAD), 1) < DHEAD
+    share = features // SECTIONS
+    for pair in range(SECTIONS // 2):
+        block = depth_out[:, pair * HEAD : (pair + 1) * HEAD]
+        top, bottom = block[: rows // 2], block[rows // 2 :]
+        outs = (
+            jnp.where(left, top, pltpu.roll(bottom, DHEAD, 1)),
+            jnp.where(left, pltpu.roll(top, DHEAD, 1), bottom),
+        )
+        for up in range(2):
+            section = 2 * pair + up
+            result_ref[section, : rows // 2] = outs[up].astype(jnp.bfloat16)
+            for half in range(2):
+                first = section * share + half * HEAD
+                result_ref[section, rows // 2 + 8 * half : rows // 2 + 8 * half + 8] = grad[
+                    :, first : first + HEAD
+                ].astype(jnp.bfloat16)
+
+
+def depth_part(core, temporal, shares):
+    width = shares.shape[0]
+    features = 2 * CHIPS * HEAD
+    rows = temporal.shape[1] * LEVELS
+    vmem = pl.BlockSpec(memory_space=pltpu.VMEM)
+    return pl.pallas_call(
+        depth_kernel,
+        out_shape=jax.ShapeDtypeStruct((SECTIONS, rows // 2 + 16, HEAD), jnp.bfloat16),
+        in_specs=[
+            pl.BlockSpec(memory_space=pltpu.SMEM),
+            vmem,
+            pl.BlockSpec(memory_space=pl.ANY),
+        ],
+        out_specs=vmem,
+        scratch_shapes=[
+            pltpu.VMEM((width, features), jnp.bfloat16),
+            pltpu.VMEM((4, width, width), jnp.bfloat16),
+            pltpu.VMEM((width, HEAD), jnp.bfloat16),
+            pltpu.SemaphoreType.DMA((PIECES,)),
+            pltpu.SemaphoreType.DMA((4,)),
+            pltpu.SemaphoreType.DMA,
+        ],
+        compiler_params=pltpu.CompilerParams(vmem_limit_bytes=50 * 1024 * 1024),
+        cost_estimate=pl.CostEstimate(
+            flops=64 * shares.size, bytes_accessed=2 * shares.size, transcendentals=0
+        ),
+    )(core, temporal, shares)
 
 
 def body(
@@ -207,12 +358,32 @@
     section_id = lax.axis_index("section")
     frame_id = lax.axis_index("frame")
     frames, levels, part = cotangent.shape
-    width = part * SECTIONS
-    features = w_depth_in.shape[0]
 
     core = frame_id % 2
+    gain = gains[0].astype(jnp.float32)[:, None]
+    weight = jnp.concatenate([w_query[0], w_key[0], w_value[0]], axis=1)
+    weight = (weight.astype(jnp.float32) * gain).astype(jnp.bfloat16)
+    stash_k, stash_v = cache_keys[0], cache_values[0]
+
+    def layer(where, block, held):
+        got = lax.all_to_all(
+            jnp.broadcast_to(block[None], (CHIPS,) + block.shape),
+            BOTH,
+            split_axis=0,
+            concat_axis=0,
+            tiled=True,
+            axis_index_groups=plane_groups(),
+        )
+        rows = lax.all_gather(got, BOTH, axis=0, axis_index_groups=core_pairs())
+        return layer_step(where, rows, weight, stash_k, stash_v, held)
+
+    where = jnp.stack([jnp.int32(0), section_id, frame_id // 2, core]).astype(jnp.int32)
+    held = jnp.zeros((3, 2 * CH, HEAD), jnp.bfloat16)
+    where, held, block = layer(where, inflow[:CH], held)
     half = part // 2
-    looked = jnp.take(code_table, codes, axis=0).reshape(-1, part)
+    late_core = where[3]
+    looked = jnp.take(code_table, codes + (late_core - core), axis=0)
+    looked = jnp.pad(looked, ((0, 0), (1, 0), (0, 0))).reshape(-1, part)
     masked = cotangent.astype(jnp.float32) * speaker_mask.astype(jnp.float32)[:, None, None]
     masked = masked.astype(jnp.bfloat16).reshape(-1, part)
     extra = jnp.concatenate([looked, masked], axis=0)
@@ -220,7 +391,7 @@
     extra = lax.all_gather(extra, BOTH, axis=1, tiled=True, axis_index_groups=core_pairs())
     shares = jnp.concatenate(
         [
-            lax.dynamic_slice_in_dim(share, core * half, half, 0)
+            lax.dynamic_slice_in_dim(share, late_core * half, half, 0)
             for share in (w_depth_in.T, w_dquery.T, w_dkey.T, w_dvalue.T, w_dout, extra)
         ],
         axis=1,
@@ -231,26 +402,6 @@
     ]
     shares = lax.all_gather(shares, BOTH, axis=0, tiled=True, axis_index_groups=along)
 
-    gain = gains[0].astype(jnp.float32)[:, None]
-    weight = jnp.concatenate([w_query[0], w_key[0], w_value[0]], axis=1)
-    weight = (weight.astype(jnp.float32) * gain).astype(jnp.bfloat16)
-    stash_k, stash_v = cache_keys[0], cache_values[0]
-
-    def layer(where, block, held):
-        got = lax.all_to_all(
-            jnp.broadcast_to(block[None], (CHIPS,) + block.shape),
-            BOTH,
-            split_axis=0,
-            concat_axis=0,
-            tiled=True,
-            axis_index_groups=plane_groups(),
-        )
-        rows = lax.all_gather(got, BOTH, axis=0, axis_index_groups=core_pairs())
-        return layer_step(where, rows, weight, stash_k, stash_v, held)
-
-    where = jnp.stack([jnp.int32(0), section_id, frame_id // 2, core]).astype(jnp.int32)
-    held = jnp.zeros((3, 2 * CH, HEAD), jnp.bfloat16)
-    where, held, block = layer(where, inflow[:CH], held)
     for tick in range(1, SECTIONS + 2):
         pairs = plane_pairs((tick - 1) % 2)
         block = lax.all_gather(block, BOTH, axis=0, axis_index_groups=pairs)[0]
@@ -261,47 +412,13 @@
 
     finished = finished.reshape(2 * CHIPS, frames, HEAD)
     temporal = lax.all_to_all(finished, "frame", split_axis=0, concat_axis=0, tiled=True)
-    temporal = temporal.transpose(1, 0, 2).reshape(frames, features)
-    w_in = shares[:, :features]
-    whole = [
-        shares[:, features + at * width : features + (at + 1) * width] for at in range(4)
-    ]
-    extra = shares[:, features + 4 * width :].reshape(width, 2, HEAD)
-    extra = lax.dynamic_index_in_dim(extra, core, 1, keepdims=False).T
-    looked = extra[: frames * (levels - 1)].reshape(frames, levels - 1, width)
-    masked = extra[frames * (levels - 1) : frames * (2 * levels - 1)]
-    in_head = (jnp.arange(width)[:, None] // DHEAD == jnp.arange(width // DHEAD)[None, :]).astype(
-        jnp.float32
-    )
-    grad_mixed = contract_last(masked, whole[3]).reshape(frames, levels, width)
-
-    base = contract_last(temporal, w_in)[:, None, :]
-    z = jnp.concatenate([base, base + looked.astype(jnp.float32)], axis=1).astype(jnp.bfloat16)
-    z = z.reshape(frames * levels, width)
-    query, key, value, probs, spread, mixed = depth_forward(z, whole, in_head, frames, levels)
-    mixed = mixed.astype(jnp.bfloat16).reshape(frames * levels, width)
-    depth_out = (
-        z.astype(jnp.float32) + jnp.dot(mixed, whole[3], preferred_element_type=jnp.float32)
-    ).astype(jnp.bfloat16)
-    grads = depth_backward(grad_mixed, query, key, value, probs, spread, in_head)
-    grad_base = jnp.sum(masked.astype(jnp.float32).reshape(frames, levels, width), axis=1)
-    for grad, weights in zip(grads, whole[:3]):
-        summed = jnp.sum(grad, axis=1).astype(jnp.bfloat16)
-        grad_base = grad_base + jnp.dot(summed, weights, preferred_element_type=jnp.float32)
-    temporal_grad = jnp.dot(
-        grad_base.astype(jnp.bfloat16), w_in, preferred_element_type=jnp.float32
-    ).astype(jnp.bfloat16)
-
-    depth_out = depth_out.reshape(frames * levels, SECTIONS, part).transpose(1, 0, 2)
-    temporal_grad = temporal_grad.reshape(frames, SECTIONS, -1).transpose(1, 0, 2)
-    results = jnp.concatenate(
-        [depth_out.reshape(SECTIONS, -1, HEAD), temporal_grad.reshape(SECTIONS, -1, HEAD)], axis=1
-    )
+    results = depth_part(where[3:], temporal, shares)
     results = lax.all_to_all(results, "section", split_axis=0, concat_axis=0, tiled=True)
     mine = results[SECTIONS - 1]
-    cut = frames * levels * part // HEAD
-    depth_out = mine[:cut].reshape(frames, levels, part)
-    temporal_grad = mine[cut:].reshape(frames, -1)
+    cut = frames * levels // 2
+    depth_out = jnp.concatenate([mine[:cut, :part], mine[:cut, part:]], axis=0)
+    depth_out = depth_out.reshape(frames, levels, part)
+    temporal_grad = jnp.concatenate([mine[cut : cut + frames], mine[cut + 8 : cut + 8 + frames]], axis=1)
     return (new_keys[None], new_values[None], depth_out, temporal_grad)
 
 

time: 491 us -> 481 us (0.980)
  matrix products: 29.3 us -> 0 us
  Pallas kernels: 40.5 us -> 59.8 us
  blocking collectives: 333 us -> 346 us
  waiting for transfers between devices: 20.4 us -> 12.1 us
  starting transfers between devices: 28.3 us -> 22.6 us
    dot_general x13 -> x0, matrix products: 29.3 us -> none  [the longest x5 14.8 us: contract_last(): lax.dot_general(a, b, (((1,), (1,)), ((), ())), preferred_element_type=jn...]
    pallas_call x0 -> x1, Pallas kernels: none -> 19.3 us  [depth_part(): pl.pallas_call(depth_kernel, out_shape=jax.ShapeDtypeStruct((SECTIONS, ro...]
    all_to_all x15 -> x16, blocking collectives: 182 us -> 194 us  [layer(): lax.all_to_all(jnp.broadcast_to(block[None], (CHIPS,) + block.shape), BOT...]
    all_to_all x3 -> x2, waiting for transfers between devices: 17 us -> 7.12 us  [layer(): lax.all_to_all(jnp.broadcast_to(block[None], (CHIPS,) + block.shape), BOT...]
    all_to_all x3 -> x2, starting transfers between devices: 22.2 us -> 16.6 us  [layer(): lax.all_to_all(jnp.broadcast_to(block[None], (CHIPS,) + block.shape), BOT...]
  transfers between devices with their start and end apart: 5 -> 4, of which waited for: 4 -> 3; matrix products, arithmetic and copies ran while one was open for 2% -> 2% of each run, Pallas kernels for 8% -> 8%
where the time goes in v2:
time: 481 us; the launch traced here: 479 us
  blocking collectives  346 us (72%)
  Pallas kernels  59.8 us (12%)
  starting transfers between devices  22.6 us (5%)
  local copies, waits for them, and re-layouts  17.1 us (4%)
  between operations  15.8 us (3%)
  waiting for transfers between devices  12.1 us (3%)
  other arithmetic  5.12 us (1%)
    all_to_all x16, blocking collectives, layer(): lax.all_to_all(jnp.broadcast_to(block[None], (CHIPS,) + block.shape), BOT...  194 us
    all_gather x17, blocking collectives, body(): block = lax.all_gather(block, BOTH, axis=0, axis_index_groups=pairs)[0]  79.2 us
    pallas_call x18, Pallas kernels, layer_step(): pl.pallas_call(layer_kernel, out_shape=(jax.ShapeDtypeStruct(where.shape,...  40.5 us
    all_gather x18, blocking collectives, layer(): rows = lax.all_gather(got, BOTH, axis=0, axis_index_groups=core_pairs())  40.1 us
    all_to_all x1, blocking collectives, body(): lax.all_to_all(results, 'section', split_axis=0, concat_axis=0, tiled=True)  31.2 us
    pallas_call x1, Pallas kernels, depth_part(): pl.pallas_call(depth_kernel, out_shape=jax.ShapeDtypeStruct((SECTIONS, ro...  19.3 us
    all_to_all x2, starting transfers between devices, layer(): lax.all_to_all(jnp.broadcast_to(block[None], (CHIPS,) + block.shape), BOT...  16.6 us
  transfers between devices with their start and end apart: 4, of which 3 were waited for; matrix products, arithmetic and copies ran while one was open for 2% of the time, Pallas kernels for 8%

profile of v2, /device:TPU:6, one launch (start us, length us, event | category | flops | bytes accessed | tf_op | source)
XLA Modules:
  0.0 478.6 jit_solution(1459654875572500970)
XLA Ops:
  8.7 10.0 %all-to-all-start = ((bf16[16,64,128]{2,1,0:T(8,128)(2,1)}), bf16[16,64,128]{2,1,0:T(8,128)(2,1)}, u32[]{:S(2)}, u32[]{:S(2)}) async-start(bf16[16,64,128]{2,1,0:T(8,128)(2,1)} %broadcast_in_dim.141), calls=%async_computation | async-start | bytes 524288 | tf_op jit(solution)/shard_map/all_to_all | solution.py:369
  20.2 2.2 multiply_convert_fusion.weight_ref
  25.2 2.4 all-gather
  27.6 2.2 shard_map.183
  43.9 4.4 all-gather.1
  49.1 6.6 %all-to-all-start.1 = ((bf16[16,64,128]{2,1,0:T(8,128)(2,1)}), bf16[16,64,128]{2,1,0:T(8,128)(2,1)}, u32[]{:S(2)}, u32[]{:S(2)}) async-start(bf16[16,64,128]{2,1,0:T(8,128)(2,1)} %broadcast_in_dim.144), calls=%async_computation.1 | async-start | bytes 524288 | tf_op jit(solution)/shard_map/all_to_all | solution.py:369
  55.7 6.5 %all-to-all-done.1 = bf16[16,64,128]{2,1,0:T(8,128)(2,1)} async-done(((bf16[16,64,128]{2,1,0:T(8,128)(2,1)}), bf16[16,64,128]{2,1,0:T(8,128)(2,1)}, u32[]{:S(2)}, u32[]{:S(2)}) %all-to-all-start.1) | async-done | bytes 262176 | tf_op jit(solution)/shard_map/all_to_all | solution.py:369
  62.2 2.4 all-gather.2
  64.6 2.3 shard_map.184
  68.7 12.4 %all_to_all.100 = bf16[16,64,128]{2,1,0:T(8,128)(2,1)S(1)} all-to-all(bf16[16,64,128]{2,1,0:T(8,128)(2,1)S(1)} %broadcast_in_dim.145), channel_id=1, replica_groups={{0,2,4,6,8,10,12,14,16,18,20,22,24,26,28,30},{1,3,5,7,9,11,13,15,17,19,..., dimensions={0} | all-to-all | bytes 524288 | tf_op jit(solution)/shard_map/all_to_all | solution.py:369
  81.2 2.2 all-gather.4
  83.4 2.3 shard_map.185
  85.6 5.1 %all-gather.5 = bf16[128,128]{1,0:T(8,128)(2,1)S(1)} all-gather(bf16[64,128]{1,0:T(8,128)(2,1)S(1)} %get-tuple-element.64), channel_id=7, replica_groups={{0,32},{1,33},{2,34},{3,35},{4,36},{5,37},{6,38},{7,39},{8,40},{9,41},{..., dimensions={0}, use_global_device_ids=true | all-gather | bytes 49152 | tf_op jit(solution)/shard_map/all_gather | solution.py:407
  90.7 11.9 %all_to_all.101 = bf16[16,64,128]{2,1,0:T(8,128)(2,1)S(1)} all-to-all(bf16[16,64,128]{2,1,0:T(8,128)(2,1)S(1)} %broadcast_in_dim.147), channel_id=1, replica_groups={{0,2,4,6,8,10,12,14,16,18,20,22,24,26,28,30},{1,3,5,7,9,11,13,15,17,19,..., dimensions={0} | all-to-all | bytes 524288 | tf_op jit(solution)/shard_map/all_to_all | solution.py:369
  102.7 2.4 all-gather.6
  105.0 2.3 shard_map.186
  109.2 12.3 %all_to_all.102 = bf16[16,64,128]{2,1,0:T(8,128)(2,1)S(1)} all-to-all(bf16[16,64,128]{2,1,0:T(8,128)(2,1)S(1)} %broadcast_in_dim.149), channel_id=1, replica_groups={{0,2,4,6,8,10,12,14,16,18,20,22,24,26,28,30},{1,3,5,7,9,11,13,15,17,19,..., dimensions={0} | all-to-all | bytes 524288 | tf_op jit(solution)/shard_map/all_to_all | solution.py:369
  121.4 2.4 all-gather.8
  123.8 2.2 shard_map.187
  126.1 7.2 %all-gather.9 = bf16[128,128]{1,0:T(8,128)(2,1)S(1)} all-gather(bf16[64,128]{1,0:T(8,128)(2,1)S(1)} %get-tuple-element.70), channel_id=11, replica_groups={{0,32},{1,33},{2,34},{3,35},{4,36},{5,37},{6,38},{7,39},{8,40},{9,41},{..., dimensions={0}, use_global_device_ids=true | all-gather | bytes 49152 | tf_op jit(solution)/shard_map/all_gather | solution.py:407
  133.4 11.9 %all_to_all.103 = bf16[16,64,128]{2,1,0:T(8,128)(2,1)S(1)} all-to-all(bf16[16,64,128]{2,1,0:T(8,128)(2,1)S(1)} %broadcast_in_dim.151), channel_id=1, replica_groups={{0,2,4,6,8,10,12,14,16,18,20,22,24,26,28,30},{1,3,5,7,9,11,13,15,17,19,..., dimensions={0} | all-to-all | bytes 524288 | tf_op jit(solution)/shard_map/all_to_all | solution.py:369
  145.3 2.2 all-gather.10
  147.5 2.2 shard_map.188
  151.6 12.3 %all_to_all.104 = bf16[16,64,128]{2,1,0:T(8,128)(2,1)S(1)} all-to-all(bf16[16,64,128]{2,1,0:T(8,128)(2,1)S(1)} %broadcast_in_dim.153), channel_id=1, replica_groups={{0,2,4,6,8,10,12,14,16,18,20,22,24,26,28,30},{1,3,5,7,9,11,13,15,17,19,..., dimensions={0} | all-to-all | bytes 524288 | tf_op jit(solution)/shard_map/all_to_all | solution.py:369
  163.9 2.2 all-gather.12
  166.1 2.3 shard_map.189
  168.3 8.1 %all-gather.13 = bf16[128,128]{1,0:T(8,128)(2,1)S(1)} all-gather(bf16[64,128]{1,0:T(8,128)(2,1)S(1)} %get-tuple-element.76), channel_id=15, replica_groups={{0,32},{1,33},{2,34},{3,35},{4,36},{5,37},{6,38},{7,39},{8,40},{9,41},{..., dimensions={0}, use_global_device_ids=true | all-gather | bytes 49152 | tf_op jit(solution)/shard_map/all_gather | solution.py:407
  176.4 11.9 %all_to_all.105 = bf16[16,64,128]{2,1,0:T(8,128)(2,1)S(1)} all-to-all(bf16[16,64,128]{2,1,0:T(8,128)(2,1)S(1)} %broadcast_in_dim.155), channel_id=1, replica_groups={{0,2,4,6,8,10,12,14,16,18,20,22,24,26,28,30},{1,3,5,7,9,11,13,15,17,19,..., dimensions={0} | all-to-all | bytes 524288 | tf_op jit(solution)/shard_map/all_to_all | solution.py:369
  188.4 2.2 all-gather.14
  190.5 2.2 shard_map.190
  194.7 12.3 %all_to_all.106 = bf16[16,64,128]{2,1,0:T(8,128)(2,1)S(1)} all-to-all(bf16[16,64,128]{2,1,0:T(8,128)(2,1)S(1)} %broadcast_in_dim.157), channel_id=1, replica_groups={{0,2,4,6,8,10,12,14,16,18,20,22,24,26,28,30},{1,3,5,7,9,11,13,15,17,19,..., dimensions={0} | all-to-all | bytes 524288 | tf_op jit(solution)/shard_map/all_to_all | solution.py:369
  207.0 2.2 all-gather.16
  209.1 2.3 shard_map.191
  211.4 8.2 %all-gather.17 = bf16[128,128]{1,0:T(8,128)(2,1)S(1)} all-gather(bf16[64,128]{1,0:T(8,128)(2,1)S(1)} %get-tuple-element.82), channel_id=19, replica_groups={{0,32},{1,33},{2,34},{3,35},{4,36},{5,37},{6,38},{7,39},{8,40},{9,41},{..., dimensions={0}, use_global_device_ids=true | all-gather | bytes 49152 | tf_op jit(solution)/shard_map/all_gather | solution.py:407
  219.7 11.9 %all_to_all.107 = bf16[16,64,128]{2,1,0:T(8,128)(2,1)S(1)} all-to-all(bf16[16,64,128]{2,1,0:T(8,128)(2,1)S(1)} %broadcast_in_dim.159), channel_id=1, replica_groups={{0,2,4,6,8,10,12,14,16,18,20,22,24,26,28,30},{1,3,5,7,9,11,13,15,17,19,..., dimensions={0} | all-to-all | bytes 524288 | tf_op jit(solution)/shard_map/all_to_all | solution.py:369
  231.6 2.3 all-gather.18
  233.9 2.3 shard_map.192
  238.1 12.3 %all_to_all.108 = bf16[16,64,128]{2,1,0:T(8,128)(2,1)S(1)} all-to-all(bf16[16,64,128]{2,1,0:T(8,128)(2,1)S(1)} %broadcast_in_dim.161), channel_id=1, replica_groups={{0,2,4,6,8,10,12,14,16,18,20,22,24,26,28,30},{1,3,5,7,9,11,13,15,17,19,..., dimensions={0} | all-to-all | bytes 524288 | tf_op jit(solution)/shard_map/all_to_all | solution.py:369
  250.4 2.2 all-gather.20
  252.5 2.2 shard_map.193
  254.8 7.9 %all-gather.21 = bf16[128,128]{1,0:T(8,128)(2,1)S(1)} all-gather(bf16[64,128]{1,0:T(8,128)(2,1)S(1)} %get-tuple-element.88), channel_id=23, replica_groups={{0,32},{1,33},{2,34},{3,35},{4,36},{5,37},{6,38},{7,39},{8,40},{9,41},{..., dimensions={0}, use_global_device_ids=true | all-gather | bytes 49152 | tf_op jit(solution)/shard_map/all_gather | solution.py:407
  262.7 11.9 %all_to_all.109 = bf16[16,64,128]{2,1,0:T(8,128)(2,1)S(1)} all-to-all(bf16[16,64,128]{2,1,0:T(8,128)(2,1)S(1)} %broadcast_in_dim.163), channel_id=1, replica_groups={{0,2,4,6,8,10,12,14,16,18,20,22,24,26,28,30},{1,3,5,7,9,11,13,15,17,19,..., dimensions={0} | all-to-all | bytes 524288 | tf_op jit(solution)/shard_map/all_to_all | solution.py:369
  274.7 2.2 all-gather.22
  276.8 2.3 shard_map.194
  281.0 12.3 %all_to_all.110 = bf16[16,64,128]{2,1,0:T(8,128)(2,1)S(1)} all-to-all(bf16[16,64,128]{2,1,0:T(8,128)(2,1)S(1)} %broadcast_in_dim.165), channel_id=1, replica_groups={{0,2,4,6,8,10,12,14,16,18,20,22,24,26,28,30},{1,3,5,7,9,11,13,15,17,19,..., dimensions={0} | all-to-all | bytes 524288 | tf_op jit(solution)/shard_map/all_to_all | solution.py:369
  295.4 2.2 shard_map.195
  297.7 7.9 %all-gather.25 = bf16[128,128]{1,0:T(8,128)(2,1)S(1)} all-gather(bf16[64,128]{1,0:T(8,128)(2,1)S(1)} %get-tuple-element.94), channel_id=27, replica_groups={{0,32},{1,33},{2,34},{3,35},{4,36},{5,37},{6,38},{7,39},{8,40},{9,41},{..., dimensions={0}, use_global_device_ids=true | all-gather | bytes 49152 | tf_op jit(solution)/shard_map/all_gather | solution.py:407
  305.6 11.9 %all_to_all.111 = bf16[16,64,128]{2,1,0:T(8,128)(2,1)S(1)} all-to-all(bf16[16,64,128]{2,1,0:T(8,128)(2,1)S(1)} %broadcast_in_dim.167), channel_id=1, replica_groups={{0,2,4,6,8,10,12,14,16,18,20,22,24,26,28,30},{1,3,5,7,9,11,13,15,17,19,..., dimensions={0} | all-to-all | bytes 524288 | tf_op jit(solution)/shard_map/all_to_all | solution.py:369
  319.7 2.2 shard_map.196
  323.9 12.3 %all_to_all.112 = bf16[16,64,128]{2,1,0:T(8,128)(2,1)S(1)} all-to-all(bf16[16,64,128]{2,1,0:T(8,128)(2,1)S(1)} %broadcast_in_dim.169), channel_id=1, replica_groups={{0,2,4,6,8,10,12,14,16,18,20,22,24,26,28,30},{1,3,5,7,9,11,13,15,17,19,..., dimensions={0} | all-to-all | bytes 524288 | tf_op jit(solution)/shard_map/all_to_all | solution.py:369
  338.3 2.2 shard_map.197
  340.6 7.9 %all-gather.29 = bf16[128,128]{1,0:T(8,128)(2,1)S(1)} all-gather(bf16[64,128]{1,0:T(8,128)(2,1)S(1)} %get-tuple-element.100), channel_id=31, replica_groups={{0,32},{1,33},{2,34},{3,35},{4,36},{5,37},{6,38},{7,39},{8,40},{9,41},{..., dimensions={0}, use_global_device_ids=true | all-gather | bytes 49152 | tf_op jit(solution)/shard_map/all_gather | solution.py:407
  348.5 11.9 %all_to_all.113 = bf16[16,64,128]{2,1,0:T(8,128)(2,1)S(1)} all-to-all(bf16[16,64,128]{2,1,0:T(8,128)(2,1)S(1)} %broadcast_in_dim.171), channel_id=1, replica_groups={{0,2,4,6,8,10,12,14,16,18,20,22,24,26,28,30},{1,3,5,7,9,11,13,15,17,19,..., dimensions={0} | all-to-all | bytes 524288 | tf_op jit(solution)/shard_map/all_to_all | solution.py:369
  362.6 2.2 shard_map.198
  366.8 12.3 %all_to_all.114 = bf16[16,64,128]{2,1,0:T(8,128)(2,1)S(1)} all-to-all(bf16[16,64,128]{2,1,0:T(8,128)(2,1)S(1)} %broadcast_in_dim.173), channel_id=1, replica_groups={{0,2,4,6,8,10,12,14,16,18,20,22,24,26,28,30},{1,3,5,7,9,11,13,15,17,19,..., dimensions={0} | all-to-all | bytes 524288 | tf_op jit(solution)/shard_map/all_to_all | solution.py:369
  381.2 2.2 shard_map.199
  383.5 7.9 %all-gather.33 = bf16[128,128]{1,0:T(8,128)(2,1)S(1)} all-gather(bf16[64,128]{1,0:T(8,128)(2,1)S(1)} %get-tuple-element.106), channel_id=35, replica_groups={{0,32},{1,33},{2,34},{3,35},{4,36},{5,37},{6,38},{7,39},{8,40},{9,41},{..., dimensions={0}, use_global_device_ids=true | all-gather | bytes 49152 | tf_op jit(solution)/shard_map/all_gather | solution.py:407
  391.4 11.9 %all_to_all.115 = bf16[16,64,128]{2,1,0:T(8,128)(2,1)S(1)} all-to-all(bf16[16,64,128]{2,1,0:T(8,128)(2,1)S(1)} %broadcast_in_dim.175), channel_id=1, replica_groups={{0,2,4,6,8,10,12,14,16,18,20,22,24,26,28,30},{1,3,5,7,9,11,13,15,17,19,..., dimensions={0} | all-to-all | bytes 524288 | tf_op jit(solution)/shard_map/all_to_all | solution.py:369
  403.4 2.2 all-gather.34
  405.5 2.3 shard_map.200
  408.4 5.9 %all-to-all-start.18 = ((bf16[32,4,128]{2,1,0:T(4,128)(2,1)}), bf16[32,4,128]{2,1,0:T(4,128)(2,1)S(1)}, u32[]{:S(2)}, u32[]{:S(2)}) async-start(bf16[32,4,128]{2,1,0:T(4,128)(2,1)} %bitcast.27), calls=%async_computation.18 | async-start | bytes 65536 | tf_op jit(solution)/shard_map/all_to_all | solution.py:414
  415.0 4.9 %all-to-all-done.18.temporal_ref = bf16[32,4,128]{2,1,0:T(4,128)(2,1)S(1)} async-done(((bf16[32,4,128]{2,1,0:T(4,128)(2,1)}), bf16[32,4,128]{2,1,0:T(4,128)(2,1)S(1)}, u32[]{:S(2)}, u32[]{:S(2)}) %all-to-all-start.18) | async-done | bytes 32800 | tf_op jit(solution)/shard_map/all_to_all | solution.py:414
  419.9 19.3 %shard_map.201 = bf16[16,32,128]{2,1,0:T(8,128)(2,1)S(1)} custom-call(s32[1]{0:T(128)} %slice.116.core_ref, bf16[32,4,128]{2,1,0:T(4,128)(2,1)S(1)} %all-to-all-done.18.temporal_ref, bf16[1024,8448]{1,0:T(8,128)(2,1)} %all-gather.37.cloned.1.call-done.shares_ref), custom_call_target="tpu_custom_call" | custom-call | flops 553648128 | bytes 17301504 | tf_op jit(solution)/shard_map/pallas_call | solution.py:316
  439.2 31.2 %all_to_all.116 = bf16[16,32,128]{2,1,0:T(8,128)(2,1)S(1)} all-to-all(bf16[16,32,128]{2,1,0:T(8,128)(2,1)S(1)} %shard_map.201), channel_id=1, replica_groups=mesh['section'=16,'frame'=32] {'section'}, dimensions={0} | all-to-all | bytes 262144 | tf_op jit(solution)/shard_map/all_to_all | solution.py:416
  (94 shorter events, 48.0 us)
Async XLA Ops:
  7.2 15.2 %copy-start.3 = (bf16[4,8,64]{2,1,0:T(8,128)(2,1)S(1)}, bf16[4,8,64]{2,1,0:T(8,128)(2,1)}, u32[]{:S(2)}) copy-start(bf16[4,8,64]{2,1,0:T(8,128)(2,1)} %param.31) | copy-start | bytes 12292
  7.2 20.4 %copy-start.1 = (bf16[1,256,128]{2,1,0:T(8,128)(2,1)S(1)}, bf16[1,256,128]{2,1,0:T(8,128)(2,1)}, u32[]{:S(2)}) copy-start(bf16[1,256,128]{2,1,0:T(8,128)(2,1)} %param.22) | copy-start | bytes 196612
  7.2 20.4 %copy-start = (bf16[1,256,128]{2,1,0:T(8,128)(2,1)S(1)}, bf16[1,256,128]{2,1,0:T(8,128)(2,1)}, u32[]{:S(2)}) copy-start(bf16[1,256,128]{2,1,0:T(8,128)(2,1)} %param.21) | copy-start | bytes 196612
  8.7 23.0 %copy-start.4 = (s32[4,7]{1,0:T(4,128)S(1)}, s32[4,7]{1,0:T(4,128)}, u32[]{:S(2)}) copy-start(s32[4,7]{1,0:T(4,128)} %param.29) | copy-start | bytes 340
  8.7 16.5 %all-to-all-start = ((bf16[16,64,128]{2,1,0:T(8,128)(2,1)}), bf16[16,64,128]{2,1,0:T(8,128)(2,1)}, u32[]{:S(2)}, u32[]{:S(2)}) async-start(bf16[16,64,128]{2,1,0:T(8,128)(2,1)} %broadcast_in_dim.141), calls=%async_computation | async-start | bytes 524288 | tf_op jit(solution)/shard_map/all_to_all | solution.py:369
  18.7 401.2 %all-gather.37.cloned.1.call-start = ((), (), s32[]{:S(2)}) async-start(), calls=%async_computation.20 | async-start | bytes 17842176 | tf_op jit(solution)/shard_map/all_gather | solution.py:403
  24.5 44.1 %copy-start.2 = (bf16[128,128]{1,0:T(8,128)(2,1)S(1)}, bf16[128,128]{1,0:T(8,128)(2,1)}, u32[]{:S(2)}) copy-start(bf16[128,128]{1,0:T(8,128)(2,1)} %param.16) | copy-start | bytes 98308
  49.1 13.1 %all-to-all-start.1 = ((bf16[16,64,128]{2,1,0:T(8,128)(2,1)}), bf16[16,64,128]{2,1,0:T(8,128)(2,1)}, u32[]{:S(2)}, u32[]{:S(2)}) async-start(bf16[16,64,128]{2,1,0:T(8,128)(2,1)} %broadcast_in_dim.144), calls=%async_computation.1 | async-start | bytes 524288 | tf_op jit(solution)/shard_map/all_to_all | solution.py:369
  408.4 11.5 %all-to-all-start.18 = ((bf16[32,4,128]{2,1,0:T(4,128)(2,1)}), bf16[32,4,128]{2,1,0:T(4,128)(2,1)S(1)}, u32[]{:S(2)}, u32[]{:S(2)}) async-start(bf16[32,4,128]{2,1,0:T(4,128)(2,1)} %bitcast.27), calls=%async_computation.18 | async-start | bytes 65536 | tf_op jit(solution)/shard_map/all_to_all | solution.py:414
Sparse Core Ops, SparseCore 0:
  44.0 110.5 all-gather.36

commit v3 on v2

--- a/solution.py
+++ b/solution.py
@@ -53,8 +53,9 @@
 
 
 def layer_kernel(
-    where_ref,
+    clock_ref,
     rows_ref,
+    own_ref,
     weight_ref,
     stash_k_ref,
     stash_v_ref,
@@ -63,15 +64,8 @@
     found_ref,
     send_ref,
 ):
-    tick = where_ref[0]
-    section = where_ref[1]
-    chip = where_ref[2]
-    core = where_ref[3]
-    next_ref[0] = tick + 1
-    next_ref[1] = section
-    next_ref[2] = chip
-    next_ref[3] = core
-    block = tick - section
+    block = clock_ref[0, 0]
+    next_ref[...] = clock_ref[...] + 1
     total = jnp.zeros((CH, 3 * HEAD), jnp.float32)
     squares = jnp.zeros((CH, 2 * HEAD), jnp.float32)
     per_piece = CHIPS // PIECES
@@ -109,8 +103,7 @@
     raised = jnp.exp(scores - peak)
     probs = (raised / jnp.sum(raised, axis=-1, keepdims=True)).astype(jnp.bfloat16)
     attended = jnp.dot(probs, values, preferred_element_type=jnp.float32)
-    own = rows_ref[core, chip].astype(jnp.float32)
-    x_out = (own + attended).astype(jnp.bfloat16)
+    x_out = (own_ref[...].astype(jnp.float32) + attended).astype(jnp.bfloat16)
 
     def keep(rows):
         found_ref[0, rows] = key_new
@@ -124,30 +117,32 @@
     send_ref[...] = x_out
 
 
-def layer_step(where, rows, weight, stash_k, stash_v, held):
+def layer_step(clock, rows, own, weight, stash_k, stash_v, held):
     vmem = pl.BlockSpec(memory_space=pltpu.VMEM)
-    smem = pl.BlockSpec(memory_space=pltpu.SMEM)
     return pl.pallas_call(
         layer_kernel,
         out_shape=(
-            jax.ShapeDtypeStruct(where.shape, where.dtype),
+            jax.ShapeDtypeStruct(clock.shape, clock.dtype),
             jax.ShapeDtypeStruct(held.shape, held.dtype),
-            jax.ShapeDtypeStruct((CH, HEAD), jnp.bfloat16),
+            jax.ShapeDtypeStruct(own.shape, own.dtype),
         ),
-        in_specs=[smem, vmem, vmem, vmem, vmem, vmem],
-        out_specs=(smem, vmem, vmem),
-        input_output_aliases={5: 1},
+        in_specs=[vmem] * 7,
+        out_specs=(vmem, vmem, vmem),
+        input_output_aliases={6: 1},
         compiler_params=pltpu.CompilerParams(vmem_limit_bytes=16 * 1024 * 1024),
         cost_estimate=pl.CostEstimate(
             flops=2 * CH * weight.size, bytes_accessed=2 * weight.size, transcendentals=0
         ),
-    )(where, rows, weight, stash_k, stash_v, held)
+    )(clock, rows, own, weight, stash_k, stash_v, held)
 
 
 def depth_kernel(
-    core_ref,
     temporal_ref,
-    shares_ref,
+    in_ref,
+    query_ref,
+    key_ref,
+    value_ref,
+    out_ref,
     result_ref,
     w_in,
     w_rest,
@@ -162,27 +157,16 @@
     rows = columns // LEVELS
     heads = width // DHEAD
     shift = columns // 2
-    fetch_extra = pltpu.make_async_copy(
-        shares_ref.at[:, pl.ds(pl.multiple_of(features + 4 * width + core_ref[0] * HEAD, HEAD), HEAD)],
-        extra,
-        extra_sem,
-    )
+    fetch_extra = pltpu.make_async_copy(out_ref.at[:, pl.ds(width, HEAD)], extra, extra_sem)
     fetch_extra.start()
     fetch_rest = []
-    for at in range(4):
-        span = pl.ds(features + at * width, width)
-        fetch_rest.append(
-            pltpu.make_async_copy(shares_ref.at[:, span], w_rest.at[at], rest_sem.at[at])
-        )
+    for at, ref in enumerate((query_ref, key_ref, value_ref, out_ref.at[:, pl.ds(0, width)])):
+        fetch_rest.append(pltpu.make_async_copy(ref, w_rest.at[at], rest_sem.at[at]))
     fetch_in = []
     step = width // PIECES
     for piece in range(PIECES):
         span = pl.ds(piece * step, step)
-        fetch_in.append(
-            pltpu.make_async_copy(
-                shares_ref.at[span, pl.ds(0, features)], w_in.at[span], in_sem.at[piece]
-            )
-        )
+        fetch_in.append(pltpu.make_async_copy(in_ref.at[span], w_in.at[span], in_sem.at[piece]))
     fetch_rest[3].start()
     for copy in fetch_in:
         copy.start()
@@ -308,19 +292,15 @@
                 ].astype(jnp.bfloat16)
 
 
-def depth_part(core, temporal, shares):
-    width = shares.shape[0]
-    features = 2 * CHIPS * HEAD
+def depth_part(temporal, weights):
+    width, features = weights[0].shape
     rows = temporal.shape[1] * LEVELS
     vmem = pl.BlockSpec(memory_space=pltpu.VMEM)
+    read = sum(weight.size for weight in weights)
     return pl.pallas_call(
         depth_kernel,
         out_shape=jax.ShapeDtypeStruct((SECTIONS, rows // 2 + 16, HEAD), jnp.bfloat16),
-        in_specs=[
-            pl.BlockSpec(memory_space=pltpu.SMEM),
-            vmem,
-            pl.BlockSpec(memory_space=pl.ANY),
-        ],
+        in_specs=[vmem] + [pl.BlockSpec(memory_space=pl.ANY)] * 5,
         out_specs=vmem,
         scratch_shapes=[
             pltpu.VMEM((width, features), jnp.bfloat16),
@@ -331,10 +311,8 @@
             pltpu.SemaphoreType.DMA,
         ],
         compiler_params=pltpu.CompilerParams(vmem_limit_bytes=50 * 1024 * 1024),
-        cost_estimate=pl.CostEstimate(
-            flops=64 * shares.size, bytes_accessed=2 * shares.size, transcendentals=0
-        ),
-    )(core, temporal, shares)
+        cost_estimate=pl.CostEstimate(flops=64 * read, bytes_accessed=2 * read, transcendentals=0),
+    )(temporal, *weights)
 
 
 def body(
@@ -356,16 +334,23 @@
     cotangent,
 ):
     section_id = lax.axis_index("section")
-    frame_id = lax.axis_index("frame")
     frames, levels, part = cotangent.shape
 
-    core = frame_id % 2
+    looked = jnp.take(code_table, codes, axis=0)
+    looked = jnp.pad(looked, ((0, 0), (1, 0), (0, 0))).reshape(-1, part)
+    masked = cotangent.astype(jnp.float32) * speaker_mask.astype(jnp.float32)[:, None, None]
+    masked = masked.astype(jnp.bfloat16).reshape(-1, part)
+    extra = jnp.concatenate([looked, masked], axis=0)
+    extra = jnp.pad(extra, ((0, HEAD - extra.shape[0]), (0, 0))).T
+    shares = (w_depth_in.T, w_dquery.T, w_dkey.T, w_dvalue.T, jnp.concatenate([w_dout, extra], axis=1))
+    weights = [lax.all_gather(share, "section", axis=0, tiled=True) for share in shares]
+
     gain = gains[0].astype(jnp.float32)[:, None]
     weight = jnp.concatenate([w_query[0], w_key[0], w_value[0]], axis=1)
     weight = (weight.astype(jnp.float32) * gain).astype(jnp.bfloat16)
     stash_k, stash_v = cache_keys[0], cache_values[0]
 
-    def layer(where, block, held):
+    def layer(clock, block, held):
         got = lax.all_to_all(
             jnp.broadcast_to(block[None], (CHIPS,) + block.shape),
             BOTH,
@@ -375,44 +360,22 @@
             axis_index_groups=plane_groups(),
         )
         rows = lax.all_gather(got, BOTH, axis=0, axis_index_groups=core_pairs())
-        return layer_step(where, rows, weight, stash_k, stash_v, held)
-
-    where = jnp.stack([jnp.int32(0), section_id, frame_id // 2, core]).astype(jnp.int32)
+        return layer_step(clock, rows, block, weight, stash_k, stash_v, held)
+
+    clock = jnp.zeros((8, HEAD), jnp.int32) - section_id
     held = jnp.zeros((3, 2 * CH, HEAD), jnp.bfloat16)
-    where, held, block = layer(where, inflow[:CH], held)
-    half = part // 2
-    late_core = where[3]
-    looked = jnp.take(code_table, codes + (late_core - core), axis=0)
-    looked = jnp.pad(looked, ((0, 0), (1, 0), (0, 0))).reshape(-1, part)
-    masked = cotangent.astype(jnp.float32) * speaker_mask.astype(jnp.float32)[:, None, None]
-    masked = masked.astype(jnp.bfloat16).reshape(-1, part)
-    extra = jnp.concatenate([looked, masked], axis=0)
-    extra = jnp.pad(extra, ((0, HEAD - extra.shape[0]), (0, 0))).T
-    extra = lax.all_gather(extra, BOTH, axis=1, tiled=True, axis_index_groups=core_pairs())
-    shares = jnp.concatenate(
-        [
-            lax.dynamic_slice_in_dim(share, late_core * half, half, 0)
-            for share in (w_depth_in.T, w_dquery.T, w_dkey.T, w_dvalue.T, w_dout, extra)
-        ],
-        axis=1,
-    )
-    along = [
-        [device_id(section, chip, at) for section in range(SECTIONS) for at in range(2)]
-        for chip in range(CHIPS)
-    ]
-    shares = lax.all_gather(shares, BOTH, axis=0, tiled=True, axis_index_groups=along)
-
+    clock, held, block = layer(clock, inflow[:CH], held)
     for tick in range(1, SECTIONS + 2):
         pairs = plane_pairs((tick - 1) % 2)
         block = lax.all_gather(block, BOTH, axis=0, axis_index_groups=pairs)[0]
         if tick == 2:
             block = jnp.where(section_id == 0, inflow[CH:], block)
-        where, held, block = layer(where, block, held)
+        clock, held, block = layer(clock, block, held)
     new_keys, new_values, finished = held[0], held[1], held[2]
 
     finished = finished.reshape(2 * CHIPS, frames, HEAD)
     temporal = lax.all_to_all(finished, "frame", split_axis=0, concat_axis=0, tiled=True)
-    results = depth_part(where[3:], temporal, shares)
+    results = depth_part(temporal, weights)
     results = lax.all_to_all(results, "section", split_axis=0, concat_axis=0, tiled=True)
     mine = results[SECTIONS - 1]
     cut = frames * levels // 2

time: 481 us -> 463 us (0.963)
  Pallas kernels: 59.8 us -> 37.8 us
  waiting for transfers between devices: 12.1 us -> 32.8 us
  local copies, waits for them, and re-layouts: 17.1 us -> 7.49 us
  blocking collectives: 346 us -> 338 us
    pallas_call x18, Pallas kernels: 40.5 us -> 20.7 us  [layer_step(): pl.pallas_call(layer_kernel, out_shape=(jax.ShapeDtypeStruct(clock.shape,...]
    all_gather x1 -> x5, waiting for transfers between devices: 0.01 us -> 14.8 us  [body(): lax.all_gather(share, 'section', axis=0, tiled=True)]
    all_to_all x1, blocking collectives: 31.2 us -> 24.1 us  [body(): lax.all_to_all(results, 'section', split_axis=0, concat_axis=0, tiled=True)]
    unnamed x16 -> x9, local copies, waits for them, and re-layouts: 9.55 us -> 2.83 us
  transfers between devices with their start and end apart: 4 -> 8, of which waited for: 3 -> 4; matrix products, arithmetic and copies ran while one was open for 2% -> 3% of each run, Pallas kernels for 8% -> 4%
where the time goes in v3:
time: 463 us; the launch traced here: 461 us
  blocking collectives  338 us (73%)
  Pallas kernels  37.8 us (8%)
  waiting for transfers between devices  32.8 us (7%)
  starting transfers between devices  22.2 us (5%)
  between operations  14.2 us (3%)
  other arithmetic  8.68 us (2%)
  local copies, waits for them, and re-layouts  7.49 us (2%)
    all_to_all x16, blocking collectives, layer(): lax.all_to_all(jnp.broadcast_to(block[None], (CHIPS,) + block.shape), BOT...  194 us
    all_gather x17, blocking collectives, body(): block = lax.all_gather(block, BOTH, axis=0, axis_index_groups=pairs)[0]  80.3 us
    all_gather x18, blocking collectives, layer(): rows = lax.all_gather(got, BOTH, axis=0, axis_index_groups=core_pairs())  39.5 us
    all_to_all x1, blocking collectives, body(): lax.all_to_all(results, 'section', split_axis=0, concat_axis=0, tiled=True)  24.1 us
    pallas_call x18, Pallas kernels, layer_step(): pl.pallas_call(layer_kernel, out_shape=(jax.ShapeDtypeStruct(clock.shape,...  20.7 us
    pallas_call x1, Pallas kernels, depth_part(): pl.pallas_call(depth_kernel, out_shape=jax.ShapeDtypeStruct((SECTIONS, ro...  17.1 us
    all_to_all x2, starting transfers between devices, layer(): lax.all_to_all(jnp.broadcast_to(block[None], (CHIPS,) + block.shape), BOT...  16.1 us
    all_gather x5, waiting for transfers between devices, body(): lax.all_gather(share, 'section', axis=0, tiled=True)  14.8 us
  transfers between devices with their start and end apart: 8, of which 4 were waited for; matrix products, arithmetic and copies ran while one was open for 3% of the time, Pallas kernels for 4%

profile of v3, /device:TPU:6, one launch (start us, length us, event | category | flops | bytes accessed | tf_op | source)
XLA Modules:
  0.0 461.0 jit_solution(14939912561261973276)
XLA Ops:
  14.6 1.6 pad_maximum_fusion
  18.2 9.9 %all-to-all-start = ((bf16[16,64,128]{2,1,0:T(8,128)(2,1)}), bf16[16,64,128]{2,1,0:T(8,128)(2,1)}, u32[]{:S(2)}, u32[]{:S(2)}) async-start(bf16[16,64,128]{2,1,0:T(8,128)(2,1)} %broadcast_in_dim.145), calls=%async_computation | async-start | bytes 524288 | tf_op jit(solution)/shard_map/all_to_all | solution.py:354
  28.8 2.2 multiply_convert_fusion.weight_ref
  31.1 3.5 all-to-all-done
  34.6 2.4 all-gather
  38.1 4.5 all-gather.1
  43.4 6.3 %all-to-all-start.1 = ((bf16[16,64,128]{2,1,0:T(8,128)(2,1)}), bf16[16,64,128]{2,1,0:T(8,128)(2,1)}, u32[]{:S(2)}, u32[]{:S(2)}) async-start(bf16[16,64,128]{2,1,0:T(8,128)(2,1)} %broadcast_in_dim.148), calls=%async_computation.1 | async-start | bytes 524288 | tf_op jit(solution)/shard_map/all_to_all | solution.py:354
  49.7 6.5 %all-to-all-done.1 = bf16[16,64,128]{2,1,0:T(8,128)(2,1)} async-done(((bf16[16,64,128]{2,1,0:T(8,128)(2,1)}), bf16[16,64,128]{2,1,0:T(8,128)(2,1)}, u32[]{:S(2)}, u32[]{:S(2)}) %all-to-all-start.1) | async-done | bytes 262176 | tf_op jit(solution)/shard_map/all_to_all | solution.py:354
  56.2 2.4 all-gather.2
  59.7 1.8 all-gather.3
  61.6 12.3 %all_to_all.100 = bf16[16,64,128]{2,1,0:T(8,128)(2,1)S(1)} all-to-all(bf16[16,64,128]{2,1,0:T(8,128)(2,1)S(1)} %broadcast_in_dim.149), channel_id=1, replica_groups={{0,2,4,6,8,10,12,14,16,18,20,22,24,26,28,30},{1,3,5,7,9,11,13,15,17,19,..., dimensions={0} | all-to-all | bytes 524288 | tf_op jit(solution)/shard_map/all_to_all | solution.py:354
  73.9 2.2 all-gather.4
  77.2 4.7 %all-gather.5 = bf16[128,128]{1,0:T(8,128)(2,1)S(1)} all-gather(bf16[64,128]{1,0:T(8,128)(2,1)S(1)} %get-tuple-element.63), channel_id=7, replica_groups={{0,32},{1,33},{2,34},{3,35},{4,36},{5,37},{6,38},{7,39},{8,40},{9,41},{..., dimensions={0}, use_global_device_ids=true | all-gather | bytes 49152 | tf_op jit(solution)/shard_map/all_gather | solution.py:370
  82.0 12.0 %all_to_all.101 = bf16[16,64,128]{2,1,0:T(8,128)(2,1)S(1)} all-to-all(bf16[16,64,128]{2,1,0:T(8,128)(2,1)S(1)} %broadcast_in_dim.151), channel_id=1, replica_groups={{0,2,4,6,8,10,12,14,16,18,20,22,24,26,28,30},{1,3,5,7,9,11,13,15,17,19,..., dimensions={0} | all-to-all | bytes 524288 | tf_op jit(solution)/shard_map/all_to_all | solution.py:354
  94.0 2.2 all-gather.6
  97.3 1.8 all-gather.7
  99.1 12.3 %all_to_all.102 = bf16[16,64,128]{2,1,0:T(8,128)(2,1)S(1)} all-to-all(bf16[16,64,128]{2,1,0:T(8,128)(2,1)S(1)} %broadcast_in_dim.153), channel_id=1, replica_groups={{0,2,4,6,8,10,12,14,16,18,20,22,24,26,28,30},{1,3,5,7,9,11,13,15,17,19,..., dimensions={0} | all-to-all | bytes 524288 | tf_op jit(solution)/shard_map/all_to_all | solution.py:354
  111.4 2.2 all-gather.8
  114.7 6.8 %all-gather.9 = bf16[128,128]{1,0:T(8,128)(2,1)S(1)} all-gather(bf16[64,128]{1,0:T(8,128)(2,1)S(1)} %get-tuple-element.69), channel_id=11, replica_groups={{0,32},{1,33},{2,34},{3,35},{4,36},{5,37},{6,38},{7,39},{8,40},{9,41},{..., dimensions={0}, use_global_device_ids=true | all-gather | bytes 49152 | tf_op jit(solution)/shard_map/all_gather | solution.py:370
  121.6 11.9 %all_to_all.103 = bf16[16,64,128]{2,1,0:T(8,128)(2,1)S(1)} all-to-all(bf16[16,64,128]{2,1,0:T(8,128)(2,1)S(1)} %broadcast_in_dim.155), channel_id=1, replica_groups={{0,2,4,6,8,10,12,14,16,18,20,22,24,26,28,30},{1,3,5,7,9,11,13,15,17,19,..., dimensions={0} | all-to-all | bytes 524288 | tf_op jit(solution)/shard_map/all_to_all | solution.py:354
  133.5 2.2 all-gather.10
  136.8 1.8 all-gather.11
  138.7 12.3 %all_to_all.104 = bf16[16,64,128]{2,1,0:T(8,128)(2,1)S(1)} all-to-all(bf16[16,64,128]{2,1,0:T(8,128)(2,1)S(1)} %broadcast_in_dim.157), channel_id=1, replica_groups={{0,2,4,6,8,10,12,14,16,18,20,22,24,26,28,30},{1,3,5,7,9,11,13,15,17,19,..., dimensions={0} | all-to-all | bytes 524288 | tf_op jit(solution)/shard_map/all_to_all | solution.py:354
  150.9 2.2 all-gather.12
  154.2 8.2 %all-gather.13 = bf16[128,128]{1,0:T(8,128)(2,1)S(1)} all-gather(bf16[64,128]{1,0:T(8,128)(2,1)S(1)} %get-tuple-element.75), channel_id=15, replica_groups={{0,32},{1,33},{2,34},{3,35},{4,36},{5,37},{6,38},{7,39},{8,40},{9,41},{..., dimensions={0}, use_global_device_ids=true | all-gather | bytes 49152 | tf_op jit(solution)/shard_map/all_gather | solution.py:370
  162.5 11.9 %all_to_all.105 = bf16[16,64,128]{2,1,0:T(8,128)(2,1)S(1)} all-to-all(bf16[16,64,128]{2,1,0:T(8,128)(2,1)S(1)} %broadcast_in_dim.159), channel_id=1, replica_groups={{0,2,4,6,8,10,12,14,16,18,20,22,24,26,28,30},{1,3,5,7,9,11,13,15,17,19,..., dimensions={0} | all-to-all | bytes 524288 | tf_op jit(solution)/shard_map/all_to_all | solution.py:354
  174.5 2.2 all-gather.14
  177.8 1.8 all-gather.15
  179.7 12.3 %all_to_all.106 = bf16[16,64,128]{2,1,0:T(8,128)(2,1)S(1)} all-to-all(bf16[16,64,128]{2,1,0:T(8,128)(2,1)S(1)} %broadcast_in_dim.161), channel_id=1, replica_groups={{0,2,4,6,8,10,12,14,16,18,20,22,24,26,28,30},{1,3,5,7,9,11,13,15,17,19,..., dimensions={0} | all-to-all | bytes 524288 | tf_op jit(solution)/shard_map/all_to_all | solution.py:354
  191.9 2.2 all-gather.16
  195.2 8.0 %all-gather.17 = bf16[128,128]{1,0:T(8,128)(2,1)S(1)} all-gather(bf16[64,128]{1,0:T(8,128)(2,1)S(1)} %get-tuple-element.81), channel_id=19, replica_groups={{0,32},{1,33},{2,34},{3,35},{4,36},{5,37},{6,38},{7,39},{8,40},{9,41},{..., dimensions={0}, use_global_device_ids=true | all-gather | bytes 49152 | tf_op jit(solution)/shard_map/all_gather | solution.py:370
  203.3 12.2 %all_to_all.107 = bf16[16,64,128]{2,1,0:T(8,128)(2,1)S(1)} all-to-all(bf16[16,64,128]{2,1,0:T(8,128)(2,1)S(1)} %broadcast_in_dim.163), channel_id=1, replica_groups={{0,2,4,6,8,10,12,14,16,18,20,22,24,26,28,30},{1,3,5,7,9,11,13,15,17,19,..., dimensions={0} | all-to-all | bytes 524288 | tf_op jit(solution)/shard_map/all_to_all | solution.py:354
  215.5 2.2 all-gather.18
  218.8 2.0 all-gather.19
  220.8 12.3 %all_to_all.108 = bf16[16,64,128]{2,1,0:T(8,128)(2,1)S(1)} all-to-all(bf16[16,64,128]{2,1,0:T(8,128)(2,1)S(1)} %broadcast_in_dim.165), channel_id=1, replica_groups={{0,2,4,6,8,10,12,14,16,18,20,22,24,26,28,30},{1,3,5,7,9,11,13,15,17,19,..., dimensions={0} | all-to-all | bytes 524288 | tf_op jit(solution)/shard_map/all_to_all | solution.py:354
  233.1 2.2 all-gather.20
  236.4 7.8 %all-gather.21 = bf16[128,128]{1,0:T(8,128)(2,1)S(1)} all-gather(bf16[64,128]{1,0:T(8,128)(2,1)S(1)} %get-tuple-element.87), channel_id=23, replica_groups={{0,32},{1,33},{2,34},{3,35},{4,36},{5,37},{6,38},{7,39},{8,40},{9,41},{..., dimensions={0}, use_global_device_ids=true | all-gather | bytes 49152 | tf_op jit(solution)/shard_map/all_gather | solution.py:370
  244.3 11.9 %all_to_all.109 = bf16[16,64,128]{2,1,0:T(8,128)(2,1)S(1)} all-to-all(bf16[16,64,128]{2,1,0:T(8,128)(2,1)S(1)} %broadcast_in_dim.167), channel_id=1, replica_groups={{0,2,4,6,8,10,12,14,16,18,20,22,24,26,28,30},{1,3,5,7,9,11,13,15,17,19,..., dimensions={0} | all-to-all | bytes 524288 | tf_op jit(solution)/shard_map/all_to_all | solution.py:354
  256.2 2.2 all-gather.22
  259.5 1.8 all-gather.23
  261.4 12.3 %all_to_all.110 = bf16[16,64,128]{2,1,0:T(8,128)(2,1)S(1)} all-to-all(bf16[16,64,128]{2,1,0:T(8,128)(2,1)S(1)} %broadcast_in_dim.169), channel_id=1, replica_groups={{0,2,4,6,8,10,12,14,16,18,20,22,24,26,28,30},{1,3,5,7,9,11,13,15,17,19,..., dimensions={0} | all-to-all | bytes 524288 | tf_op jit(solution)/shard_map/all_to_all | solution.py:354
  273.6 2.2 all-gather.24
  276.9 8.2 %all-gather.25 = bf16[128,128]{1,0:T(8,128)(2,1)S(1)} all-gather(bf16[64,128]{1,0:T(8,128)(2,1)S(1)} %get-tuple-element.93), channel_id=27, replica_groups={{0,32},{1,33},{2,34},{3,35},{4,36},{5,37},{6,38},{7,39},{8,40},{9,41},{..., dimensions={0}, use_global_device_ids=true | all-gather | bytes 49152 | tf_op jit(solution)/shard_map/all_gather | solution.py:370
  285.2 11.9 %all_to_all.111 = bf16[16,64,128]{2,1,0:T(8,128)(2,1)S(1)} all-to-all(bf16[16,64,128]{2,1,0:T(8,128)(2,1)S(1)} %broadcast_in_dim.171), channel_id=1, replica_groups={{0,2,4,6,8,10,12,14,16,18,20,22,24,26,28,30},{1,3,5,7,9,11,13,15,17,19,..., dimensions={0} | all-to-all | bytes 524288 | tf_op jit(solution)/shard_map/all_to_all | solution.py:354
  297.1 2.2 all-gather.26
  300.4 1.8 all-gather.27
  302.3 12.3 %all_to_all.112 = bf16[16,64,128]{2,1,0:T(8,128)(2,1)S(1)} all-to-all(bf16[16,64,128]{2,1,0:T(8,128)(2,1)S(1)} %broadcast_in_dim.173), channel_id=1, replica_groups={{0,2,4,6,8,10,12,14,16,18,20,22,24,26,28,30},{1,3,5,7,9,11,13,15,17,19,..., dimensions={0} | all-to-all | bytes 524288 | tf_op jit(solution)/shard_map/all_to_all | solution.py:354
  314.6 2.2 all-gather.28
  317.9 8.4 %all-gather.29 = bf16[128,128]{1,0:T(8,128)(2,1)S(1)} all-gather(bf16[64,128]{1,0:T(8,128)(2,1)S(1)} %get-tuple-element.99), channel_id=31, replica_groups={{0,32},{1,33},{2,34},{3,35},{4,36},{5,37},{6,38},{7,39},{8,40},{9,41},{..., dimensions={0}, use_global_device_ids=true | all-gather | bytes 49152 | tf_op jit(solution)/shard_map/all_gather | solution.py:370
  326.3 11.8 %all_to_all.113 = bf16[16,64,128]{2,1,0:T(8,128)(2,1)S(1)} all-to-all(bf16[16,64,128]{2,1,0:T(8,128)(2,1)S(1)} %broadcast_in_dim.175), channel_id=1, replica_groups={{0,2,4,6,8,10,12,14,16,18,20,22,24,26,28,30},{1,3,5,7,9,11,13,15,17,19,..., dimensions={0} | all-to-all | bytes 524288 | tf_op jit(solution)/shard_map/all_to_all | solution.py:354
  338.1 2.2 all-gather.30
  341.4 1.8 all-gather.31
  343.3 12.3 %all_to_all.114 = bf16[16,64,128]{2,1,0:T(8,128)(2,1)S(1)} all-to-all(bf16[16,64,128]{2,1,0:T(8,128)(2,1)S(1)} %broadcast_in_dim.177), channel_id=1, replica_groups={{0,2,4,6,8,10,12,14,16,18,20,22,24,26,28,30},{1,3,5,7,9,11,13,15,17,19,..., dimensions={0} | all-to-all | bytes 524288 | tf_op jit(solution)/shard_map/all_to_all | solution.py:354
  355.6 2.2 all-gather.32
  358.9 8.8 %all-gather.33 = bf16[128,128]{1,0:T(8,128)(2,1)S(1)} all-gather(bf16[64,128]{1,0:T(8,128)(2,1)S(1)} %get-tuple-element.105), channel_id=35, replica_groups={{0,32},{1,33},{2,34},{3,35},{4,36},{5,37},{6,38},{7,39},{8,40},{9,41},{..., dimensions={0}, use_global_device_ids=true | all-gather | bytes 49152 | tf_op jit(solution)/shard_map/all_gather | solution.py:370
  367.7 11.9 %all_to_all.115 = bf16[16,64,128]{2,1,0:T(8,128)(2,1)S(1)} all-to-all(bf16[16,64,128]{2,1,0:T(8,128)(2,1)S(1)} %broadcast_in_dim.179), channel_id=1, replica_groups={{0,2,4,6,8,10,12,14,16,18,20,22,24,26,28,30},{1,3,5,7,9,11,13,15,17,19,..., dimensions={0} | all-to-all | bytes 524288 | tf_op jit(solution)/shard_map/all_to_all | solution.py:354
  379.7 2.2 all-gather.34
  381.8 1.7 shard_map.200
  384.2 5.9 %all-to-all-start.18 = ((bf16[32,4,128]{2,1,0:T(4,128)(2,1)}), bf16[32,4,128]{2,1,0:T(4,128)(2,1)S(1)}, u32[]{:S(2)}, u32[]{:S(2)}) async-start(bf16[32,4,128]{2,1,0:T(4,128)(2,1)} %bitcast.24), calls=%async_computation.18 | async-start | bytes 65536 | tf_op jit(solution)/shard_map/all_to_all | solution.py:377
  390.3 5.4 %all-to-all-done.18.temporal_ref = bf16[32,4,128]{2,1,0:T(4,128)(2,1)S(1)} async-done(((bf16[32,4,128]{2,1,0:T(4,128)(2,1)}), bf16[32,4,128]{2,1,0:T(4,128)(2,1)S(1)}, u32[]{:S(2)}, u32[]{:S(2)}) %all-to-all-start.18) | async-done | bytes 32800 | tf_op jit(solution)/shard_map/all_to_all | solution.py:377
  395.7 14.7 %all-gather.41.cloned.1.call-done.in_ref = bf16[1024,4096]{1,0:T(8,128)(2,1)} async-done(((bf16[64,4096]{1,0:T(8,128)(2,1)}), bf16[1024,4096]{1,0:T(8,128)(2,1)}) %all-gather.41.cloned.1.call-update) | async-done | bytes 8388624 | tf_op jit(solution)/shard_map/all_gather | solution.py:346
  410.4 1.6 copy-done.2
  411.9 17.1 %shard_map.201 = bf16[16,32,128]{2,1,0:T(8,128)(2,1)S(1)} custom-call(bf16[32,4,128]{2,1,0:T(4,128)(2,1)S(1)} %all-to-all-done.18.temporal_ref, bf16[1024,4096]{1,0:T(8,128)(2,1)} %all-gather.41.cloned.1.call-done.in_ref, bf16[1024,1024]{1,0:T(8,128)(2,1)S(1)} %copy-done.2, bf16[1024,1024]{1,0:T(8,128)(2,1)} %all-gather.45.cloned.1.call-done.key_ref, ...), custom_call_target="tpu_custom_call" | custom-call | flops 545259520 | bytes 17039360 | tf_op jit(solution)/shard_map/pallas_call | solution.py:300
  429.1 24.1 %all_to_all.116 = bf16[16,32,128]{2,1,0:T(8,128)(2,1)S(1)} all-to-all(bf16[16,32,128]{2,1,0:T(8,128)(2,1)S(1)} %shard_map.201), channel_id=1, replica_groups=mesh['section'=16,'frame'=32] {'section'}, dimensions={0} | all-to-all | bytes 262144 | tf_op jit(solution)/shard_map/all_to_all | solution.py:379
  (97 shorter events, 32.6 us)
Async XLA Ops:
  7.2 29.8 %copy-start = (bf16[1,256,128]{2,1,0:T(8,128)(2,1)S(1)}, bf16[1,256,128]{2,1,0:T(8,128)(2,1)}, u32[]{:S(2)}) copy-start(bf16[1,256,128]{2,1,0:T(8,128)(2,1)} %param.21) | copy-start | bytes 196612
  7.2 29.8 %copy-start.1 = (bf16[1,256,128]{2,1,0:T(8,128)(2,1)S(1)}, bf16[1,256,128]{2,1,0:T(8,128)(2,1)}, u32[]{:S(2)}) copy-start(bf16[1,256,128]{2,1,0:T(8,128)(2,1)} %param.22) | copy-start | bytes 196612
  7.2 383.0 %all-gather.43.cloned.1.call-start = ((), (), s32[]{:S(2)}) async-start(), calls=%async_computation.21 | async-start | bytes 2228224 | tf_op jit(solution)/shard_map/all_gather | solution.py:346
  7.9 382.3 %all-gather.45.cloned.1.call-start = ((), (), s32[]{:S(2)}) async-start(), calls=%async_computation.22 | async-start | bytes 2228224 | tf_op jit(solution)/shard_map/all_gather | solution.py:346
  8.7 381.5 %all-gather.47.cloned.1.call-start = ((), (), s32[]{:S(2)}) async-start(), calls=%async_computation.23 | async-start | bytes 2228224 | tf_op jit(solution)/shard_map/all_gather | solution.py:346
  9.4 380.8 %all-gather.49.cloned.1.call-start = ((), (), s32[]{:S(2)}) async-start(), calls=%async_computation.24 | async-start | bytes 2506752 | tf_op jit(solution)/shard_map/all_gather | solution.py:346
  16.2 394.2 %all-gather.41.cloned.1.call-start = ((), (), s32[]{:S(2)}) async-start(), calls=%async_computation.20 | async-start | bytes 8912896 | tf_op jit(solution)/shard_map/all_gather | solution.py:346
  18.2 16.4 %all-to-all-start = ((bf16[16,64,128]{2,1,0:T(8,128)(2,1)}), bf16[16,64,128]{2,1,0:T(8,128)(2,1)}, u32[]{:S(2)}, u32[]{:S(2)}) async-start(bf16[16,64,128]{2,1,0:T(8,128)(2,1)} %broadcast_in_dim.145), calls=%async_computation | async-start | bytes 524288 | tf_op jit(solution)/shard_map/all_to_all | solution.py:354
  31.0 30.5 %copy-start.3 = (bf16[128,128]{1,0:T(8,128)(2,1)S(1)}, bf16[128,128]{1,0:T(8,128)(2,1)}, u32[]{:S(2)}) copy-start(bf16[128,128]{1,0:T(8,128)(2,1)} %param.16) | copy-start | bytes 98308
  43.4 12.7 %all-to-all-start.1 = ((bf16[16,64,128]{2,1,0:T(8,128)(2,1)}), bf16[16,64,128]{2,1,0:T(8,128)(2,1)}, u32[]{:S(2)}, u32[]{:S(2)}) async-start(bf16[16,64,128]{2,1,0:T(8,128)(2,1)} %broadcast_in_dim.148), calls=%async_computation.1 | async-start | bytes 524288 | tf_op jit(solution)/shard_map/all_to_all | solution.py:354
  384.2 11.5 %all-to-all-start.18 = ((bf16[32,4,128]{2,1,0:T(4,128)(2,1)}), bf16[32,4,128]{2,1,0:T(4,128)(2,1)S(1)}, u32[]{:S(2)}, u32[]{:S(2)}) async-start(bf16[32,4,128]{2,1,0:T(4,128)(2,1)} %bitcast.24), calls=%async_computation.18 | async-start | bytes 65536 | tf_op jit(solution)/shard_map/all_to_all | solution.py:377
  410.3 1.6 copy-start.2
Sparse Core Ops, SparseCore 0:
  10.1 77.9 all-gather.42
  90.1 70.0 all-gather.44
  162.3 69.9 all-gather.46
  234.3 71.1 all-gather.48
  307.4 102.9 all-gather.40

commit v4 on v3

--- a/solution.py
+++ b/solution.py
@@ -136,13 +136,65 @@
     )(clock, rows, own, weight, stash_k, stash_v, held)
 
 
-def depth_kernel(
-    temporal_ref,
-    in_ref,
+def pack_kernel(
+    codes_ref,
+    table_ref,
+    cotangent_ref,
     query_ref,
     key_ref,
     value_ref,
     out_ref,
+    packed_ref,
+    small,
+    sems,
+):
+    part = out_ref.shape[0]
+    copies = [
+        pltpu.make_async_copy(ref, packed_ref.at[pl.ds(at * part, part)], sems.at[at])
+        for at, ref in enumerate((query_ref, key_ref, value_ref, out_ref))
+    ]
+    for copy in copies:
+        copy.start()
+    rows = cotangent_ref.shape[0]
+    entries = table_ref.shape[1]
+    picked = lax.broadcasted_iota(jnp.int32, (entries, HEAD), 0) == codes_ref[...]
+    looked = jnp.dot(
+        table_ref[...], picked.astype(jnp.bfloat16), preferred_element_type=jnp.float32
+    )
+    wide = cotangent_ref[...].astype(jnp.float32)
+    wide = jnp.concatenate([wide, jnp.zeros((rows, HEAD - part), jnp.float32)], axis=1)
+    wide = jnp.concatenate([wide, jnp.zeros((HEAD - rows, HEAD), jnp.float32)], axis=0)
+    lane = lax.broadcasted_iota(jnp.int32, (part, HEAD), 1)
+    extra = jnp.where(lane < rows, looked, pltpu.roll(wide.T[:part], rows, 1)).astype(jnp.bfloat16)
+    strips = [extra[at : at + 16] for at in range(0, part, 16)]
+    strips.append(jnp.zeros((16, small.shape[1] - part // 16 * HEAD), jnp.bfloat16))
+    small[...] = jnp.concatenate(strips, axis=1)
+    last = pltpu.make_async_copy(small, packed_ref.at[pl.ds(4 * part, 16)], sems.at[4])
+    last.start()
+    for copy in copies:
+        copy.wait()
+    last.wait()
+
+
+def pack(codes, table, cotangent, weights):
+    part, width = weights[0].shape
+    vmem = pl.BlockSpec(memory_space=pltpu.VMEM)
+    anywhere = pl.BlockSpec(memory_space=pl.ANY)
+    return pl.pallas_call(
+        pack_kernel,
+        out_shape=jax.ShapeDtypeStruct((4 * part + 16, width), jnp.bfloat16),
+        in_specs=[vmem] * 3 + [anywhere] * 4,
+        out_specs=anywhere,
+        scratch_shapes=[pltpu.VMEM((16, width), jnp.bfloat16), pltpu.SemaphoreType.DMA((5,))],
+        compiler_params=pltpu.CompilerParams(vmem_limit_bytes=16 * 1024 * 1024),
+    )(codes, table, cotangent, *weights)
+
+
+def depth_kernel(
+    temporal_ref,
+    mask_ref,
+    in_ref,
+    packed_ref,
     result_ref,
     w_in,
     w_rest,
@@ -157,22 +209,39 @@
     rows = columns // LEVELS
     heads = width // DHEAD
     shift = columns // 2
-    fetch_extra = pltpu.make_async_copy(out_ref.at[:, pl.ds(width, HEAD)], extra, extra_sem)
-    fetch_extra.start()
+    part = width // SECTIONS
+    fetch_extra = []
+    for at in range(part // 16):
+        fetch_extra.append(
+            pltpu.make_async_copy(
+                packed_ref.at[:, pl.ds(4 * part, 16), pl.ds(at * HEAD, HEAD)],
+                extra.at[:, pl.ds(at * 16, 16), :],
+                extra_sem.at[at],
+            )
+        )
     fetch_rest = []
-    for at, ref in enumerate((query_ref, key_ref, value_ref, out_ref.at[:, pl.ds(0, width)])):
-        fetch_rest.append(pltpu.make_async_copy(ref, w_rest.at[at], rest_sem.at[at]))
+    for at in range(4):
+        fetch_rest.append(
+            pltpu.make_async_copy(
+                packed_ref.at[:, pl.ds(at * part, part), :], w_rest.at[at], rest_sem.at[at]
+            )
+        )
     fetch_in = []
     step = width // PIECES
     for piece in range(PIECES):
         span = pl.ds(piece * step, step)
         fetch_in.append(pltpu.make_async_copy(in_ref.at[span], w_in.at[span], in_sem.at[piece]))
+    for copy in fetch_extra:
+        copy.start()
     fetch_rest[3].start()
     for copy in fetch_in:
         copy.start()
     for copy in fetch_rest[:3]:
         copy.start()
 
+    def rest(at):
+        return w_rest[at].reshape(width, width)
+
     def iota(shape, axis):
         return lax.broadcasted_iota(jnp.int32, shape, axis)
 
@@ -184,14 +253,15 @@
     same = (source == target % rows).astype(jnp.bfloat16)
     behind = ((source == target % rows - distance) & (level >= distance)).astype(jnp.bfloat16)
 
-    fetch_extra.wait()
-    known = extra[...]
+    for copy in fetch_extra:
+        copy.wait()
+    known = extra[...].reshape(width, HEAD)
     own = (iota((HEAD, HEAD), 0) == iota((HEAD, HEAD), 1) + rows).astype(jnp.bfloat16)
     own = jnp.where(iota((HEAD, HEAD), 1) < rows, own, jnp.zeros_like(own))
-    masked = product(known, own).astype(jnp.bfloat16)
+    masked = (product(known, own) * mask_ref[...]).astype(jnp.bfloat16)
     masked_all = product(masked, same).astype(jnp.bfloat16)
     fetch_rest[3].wait()
-    w_out = w_rest[3]
+    w_out = rest(3)
     grad_mixed = product(w_out, masked_all)
 
     parts = []
@@ -221,9 +291,9 @@
     z_behind = product(z_low, behind).astype(jnp.bfloat16)
     for copy in fetch_rest[:3]:
         copy.wait()
-    query = product(w_rest[0], z_same)
-    key = product(w_rest[1], z_behind)
-    value = product(w_rest[2], z_behind)
+    query = product(rest(0), z_same)
+    key = product(rest(1), z_behind)
+    value = product(rest(2), z_behind)
 
     def per_head(terms):
         return jnp.sum(terms.reshape(heads, DHEAD, columns), axis=1)
@@ -269,7 +339,7 @@
     grad_base = summed[24:32]
     for slot in range(3):
         grad_base = grad_base + product(
-            summed[8 * slot : 8 * slot + 8].astype(jnp.bfloat16), w_rest[slot]
+            summed[8 * slot : 8 * slot + 8].astype(jnp.bfloat16), rest(slot)
         )
     grad = product(grad_base.astype(jnp.bfloat16), w_in[...])
 
@@ -292,27 +362,29 @@
                 ].astype(jnp.bfloat16)
 
 
-def depth_part(temporal, weights):
-    width, features = weights[0].shape
+def depth_part(temporal, mask, w_in, packed):
+    width, features = w_in.shape
+    part = width // SECTIONS
     rows = temporal.shape[1] * LEVELS
     vmem = pl.BlockSpec(memory_space=pltpu.VMEM)
-    read = sum(weight.size for weight in weights)
+    anywhere = pl.BlockSpec(memory_space=pl.ANY)
+    read = w_in.size + packed.size
     return pl.pallas_call(
         depth_kernel,
         out_shape=jax.ShapeDtypeStruct((SECTIONS, rows // 2 + 16, HEAD), jnp.bfloat16),
-        in_specs=[vmem] + [pl.BlockSpec(memory_space=pl.ANY)] * 5,
+        in_specs=[vmem, vmem, anywhere, anywhere],
         out_specs=vmem,
         scratch_shapes=[
             pltpu.VMEM((width, features), jnp.bfloat16),
-            pltpu.VMEM((4, width, width), jnp.bfloat16),
-            pltpu.VMEM((width, HEAD), jnp.bfloat16),
+            pltpu.VMEM((4, SECTIONS, part, width), jnp.bfloat16),
+            pltpu.VMEM((SECTIONS, part, HEAD), jnp.bfloat16),
             pltpu.SemaphoreType.DMA((PIECES,)),
             pltpu.SemaphoreType.DMA((4,)),
-            pltpu.SemaphoreType.DMA,
+            pltpu.SemaphoreType.DMA((part // 16,)),
         ],
         compiler_params=pltpu.CompilerParams(vmem_limit_bytes=50 * 1024 * 1024),
         cost_estimate=pl.CostEstimate(flops=64 * read, bytes_accessed=2 * read, transcendentals=0),
-    )(temporal, *weights)
+    )(temporal, mask, w_in, packed)
 
 
 def body(
@@ -336,14 +408,18 @@
     section_id = lax.axis_index("section")
     frames, levels, part = cotangent.shape
 
-    looked = jnp.take(code_table, codes, axis=0)
-    looked = jnp.pad(looked, ((0, 0), (1, 0), (0, 0))).reshape(-1, part)
-    masked = cotangent.astype(jnp.float32) * speaker_mask.astype(jnp.float32)[:, None, None]
-    masked = masked.astype(jnp.bfloat16).reshape(-1, part)
-    extra = jnp.concatenate([looked, masked], axis=0)
-    extra = jnp.pad(extra, ((0, HEAD - extra.shape[0]), (0, 0))).T
-    shares = (w_depth_in.T, w_dquery.T, w_dkey.T, w_dvalue.T, jnp.concatenate([w_dout, extra], axis=1))
-    weights = [lax.all_gather(share, "section", axis=0, tiled=True) for share in shares]
+    rows = frames * levels
+    codes = jnp.pad(codes, ((0, 0), (1, 0)), constant_values=-1).reshape(1, rows)
+    codes = jnp.pad(codes, ((0, 0), (0, HEAD - rows)), constant_values=-1)
+    packed = pack(
+        codes,
+        code_table.T,
+        cotangent.reshape(rows, part),
+        (w_dquery.T, w_dkey.T, w_dvalue.T, w_dout),
+    )
+    packed = lax.all_gather(packed, "section", axis=0)
+    w_in = lax.all_gather(w_depth_in.T, "section", axis=0, tiled=True)
+    mask = jnp.pad(jnp.repeat(speaker_mask.astype(jnp.float32), levels), (0, HEAD - rows))[None]
 
     gain = gains[0].astype(jnp.float32)[:, None]
     weight = jnp.concatenate([w_query[0], w_key[0], w_value[0]], axis=1)
@@ -375,7 +451,7 @@
 
     finished = finished.reshape(2 * CHIPS, frames, HEAD)
     temporal = lax.all_to_all(finished, "frame", split_axis=0, concat_axis=0, tiled=True)
-    results = depth_part(temporal, weights)
+    results = depth_part(temporal, mask, w_in, packed)
     results = lax.all_to_all(results, "section", split_axis=0, concat_axis=0, tiled=True)
     mine = results[SECTIONS - 1]
     cut = frames * levels // 2

time: 463 us -> 454 us (0.981)
  waiting for transfers between devices: 32.8 us -> 22.6 us
  starting transfers between devices: 22.2 us -> 28.3 us
    all_gather x5 -> x2, waiting for transfers between devices: 14.8 us -> 0.01 us  [the longest x1 0.01 us: body(): w_in = lax.all_gather(w_depth_in.T, 'section', axis=0, tiled=True)]
    all_to_all x16 -> x15, blocking collectives: 194 us -> 182 us  [layer(): lax.all_to_all(jnp.broadcast_to(block[None], (CHIPS,) + block.shape), BOT...]
    all_to_all x1, blocking collectives: 24.1 us -> 31.3 us  [body(): lax.all_to_all(results, 'section', split_axis=0, concat_axis=0, tiled=True)]
    all_to_all x2 -> x3, waiting for transfers between devices: 10 us -> 16.4 us  [layer(): lax.all_to_all(jnp.broadcast_to(block[None], (CHIPS,) + block.shape), BOT...]
    all_to_all x2 -> x3, starting transfers between devices: 16.1 us -> 22.2 us  [layer(): lax.all_to_all(jnp.broadcast_to(block[None], (CHIPS,) + block.shape), BOT...]
  transfers between devices with their start and end apart: 8 -> 6, of which waited for: 4 -> 4; matrix products, arithmetic and copies ran while one was open for 3% -> 2% of each run, Pallas kernels for 4% -> 5%
where the time goes in v4:
time: 454 us; the launch traced here: 452 us
  blocking collectives  334 us (74%)
  Pallas kernels  37.9 us (8%)
  starting transfers between devices  28.3 us (6%)
  waiting for transfers between devices  22.6 us (5%)
  between operations  14.4 us (3%)
  local copies, waits for them, and re-layouts  10.8 us (2%)
    all_to_all x15, blocking collectives, layer(): lax.all_to_all(jnp.broadcast_to(block[None], (CHIPS,) + block.shape), BOT...  182 us
    all_gather x17, blocking collectives, body(): block = lax.all_gather(block, BOTH, axis=0, axis_index_groups=pairs)[0]  81 us
    all_gather x18, blocking collectives, layer(): rows = lax.all_gather(got, BOTH, axis=0, axis_index_groups=core_pairs())  39.7 us
    all_to_all x1, blocking collectives, body(): lax.all_to_all(results, 'section', split_axis=0, concat_axis=0, tiled=True)  31.3 us
    all_to_all x3, starting transfers between devices, layer(): lax.all_to_all(jnp.broadcast_to(block[None], (CHIPS,) + block.shape), BOT...  22.2 us
    pallas_call x18, Pallas kernels, layer_step(): pl.pallas_call(layer_kernel, out_shape=(jax.ShapeDtypeStruct(clock.shape,...  20.7 us
    all_to_all x3, waiting for transfers between devices, layer(): lax.all_to_all(jnp.broadcast_to(block[None], (CHIPS,) + block.shape), BOT...  16.4 us
    pallas_call x1, Pallas kernels, depth_part(): pl.pallas_call(depth_kernel, out_shape=jax.ShapeDtypeStruct((SECTIONS, ro...  16.3 us
  transfers between devices with their start and end apart: 6, of which 4 were waited for; matrix products, arithmetic and copies ran while one was open for 2% of the time, Pallas kernels for 5%

profile of v4, /device:TPU:6, one launch (start us, length us, event | category | flops | bytes accessed | tf_op | source)
XLA Modules:
  0.0 451.8 jit_solution(9296030209161535798)
XLA Ops:
  16.5 9.8 %all-to-all-start = ((bf16[16,64,128]{2,1,0:T(8,128)(2,1)}), bf16[16,64,128]{2,1,0:T(8,128)(2,1)}, u32[]{:S(2)}, u32[]{:S(2)}) async-start(bf16[16,64,128]{2,1,0:T(8,128)(2,1)} %broadcast_in_dim.138), calls=%async_computation | async-start | bytes 524288 | tf_op jit(solution)/shard_map/all_to_all | solution.py:430
  27.1 2.2 multiply_convert_fusion.weight_ref
  29.3 3.5 all-to-all-done
  32.8 2.4 all-gather
  36.4 4.7 %all-gather.1 = bf16[128,128]{1,0:T(8,128)(2,1)S(1)} all-gather(bf16[64,128]{1,0:T(8,128)(2,1)S(1)} %get-tuple-element.57), channel_id=3, replica_groups={{0,32},{1,33},{2,34},{3,35},{4,36},{5,37},{6,38},{7,39},{8,40},{9,41},{..., dimensions={0}, use_global_device_ids=true | all-gather | bytes 49152 | tf_op jit(solution)/shard_map/all_gather | solution.py:446
  41.9 6.2 %all-to-all-start.1 = ((bf16[16,64,128]{2,1,0:T(8,128)(2,1)}), bf16[16,64,128]{2,1,0:T(8,128)(2,1)}, u32[]{:S(2)}, u32[]{:S(2)}) async-start(bf16[16,64,128]{2,1,0:T(8,128)(2,1)} %broadcast_in_dim.141), calls=%async_computation.1 | async-start | bytes 524288 | tf_op jit(solution)/shard_map/all_to_all | solution.py:430
  48.1 6.5 %all-to-all-done.1 = bf16[16,64,128]{2,1,0:T(8,128)(2,1)} async-done(((bf16[16,64,128]{2,1,0:T(8,128)(2,1)}), bf16[16,64,128]{2,1,0:T(8,128)(2,1)}, u32[]{:S(2)}, u32[]{:S(2)}) %all-to-all-start.1) | async-done | bytes 262176 | tf_op jit(solution)/shard_map/all_to_all | solution.py:430
  54.6 2.4 all-gather.2
  56.9 1.1 shard_map.184
  58.1 1.8 all-gather.3
  60.0 12.3 %all_to_all.100 = bf16[16,64,128]{2,1,0:T(8,128)(2,1)S(1)} all-to-all(bf16[16,64,128]{2,1,0:T(8,128)(2,1)S(1)} %broadcast_in_dim.142), channel_id=1, replica_groups={{0,2,4,6,8,10,12,14,16,18,20,22,24,26,28,30},{1,3,5,7,9,11,13,15,17,19,..., dimensions={0} | all-to-all | bytes 524288 | tf_op jit(solution)/shard_map/all_to_all | solution.py:430
  72.3 2.2 all-gather.4
  75.6 5.1 %all-gather.5 = bf16[128,128]{1,0:T(8,128)(2,1)S(1)} all-gather(bf16[64,128]{1,0:T(8,128)(2,1)S(1)} %get-tuple-element.63), channel_id=7, replica_groups={{0,32},{1,33},{2,34},{3,35},{4,36},{5,37},{6,38},{7,39},{8,40},{9,41},{..., dimensions={0}, use_global_device_ids=true | all-gather | bytes 49152 | tf_op jit(solution)/shard_map/all_gather | solution.py:446
  80.7 11.9 %all_to_all.101 = bf16[16,64,128]{2,1,0:T(8,128)(2,1)S(1)} all-to-all(bf16[16,64,128]{2,1,0:T(8,128)(2,1)S(1)} %broadcast_in_dim.144), channel_id=1, replica_groups={{0,2,4,6,8,10,12,14,16,18,20,22,24,26,28,30},{1,3,5,7,9,11,13,15,17,19,..., dimensions={0} | all-to-all | bytes 524288 | tf_op jit(solution)/shard_map/all_to_all | solution.py:430
  92.7 2.2 all-gather.6
  96.0 1.8 all-gather.7
  97.9 12.3 %all_to_all.102 = bf16[16,64,128]{2,1,0:T(8,128)(2,1)S(1)} all-to-all(bf16[16,64,128]{2,1,0:T(8,128)(2,1)S(1)} %broadcast_in_dim.146), channel_id=1, replica_groups={{0,2,4,6,8,10,12,14,16,18,20,22,24,26,28,30},{1,3,5,7,9,11,13,15,17,19,..., dimensions={0} | all-to-all | bytes 524288 | tf_op jit(solution)/shard_map/all_to_all | solution.py:430
  110.1 2.2 all-gather.8
  113.4 7.4 %all-gather.9 = bf16[128,128]{1,0:T(8,128)(2,1)S(1)} all-gather(bf16[64,128]{1,0:T(8,128)(2,1)S(1)} %get-tuple-element.69), channel_id=11, replica_groups={{0,32},{1,33},{2,34},{3,35},{4,36},{5,37},{6,38},{7,39},{8,40},{9,41},{..., dimensions={0}, use_global_device_ids=true | all-gather | bytes 49152 | tf_op jit(solution)/shard_map/all_gather | solution.py:446
  120.9 11.9 %all_to_all.103 = bf16[16,64,128]{2,1,0:T(8,128)(2,1)S(1)} all-to-all(bf16[16,64,128]{2,1,0:T(8,128)(2,1)S(1)} %broadcast_in_dim.148), channel_id=1, replica_groups={{0,2,4,6,8,10,12,14,16,18,20,22,24,26,28,30},{1,3,5,7,9,11,13,15,17,19,..., dimensions={0} | all-to-all | bytes 524288 | tf_op jit(solution)/shard_map/all_to_all | solution.py:430
  132.8 2.2 all-gather.10
  136.1 1.8 all-gather.11
  138.0 12.3 %all_to_all.104 = bf16[16,64,128]{2,1,0:T(8,128)(2,1)S(1)} all-to-all(bf16[16,64,128]{2,1,0:T(8,128)(2,1)S(1)} %broadcast_in_dim.150), channel_id=1, replica_groups={{0,2,4,6,8,10,12,14,16,18,20,22,24,26,28,30},{1,3,5,7,9,11,13,15,17,19,..., dimensions={0} | all-to-all | bytes 524288 | tf_op jit(solution)/shard_map/all_to_all | solution.py:430
  150.2 2.2 all-gather.12
  153.5 8.5 %all-gather.13 = bf16[128,128]{1,0:T(8,128)(2,1)S(1)} all-gather(bf16[64,128]{1,0:T(8,128)(2,1)S(1)} %get-tuple-element.75), channel_id=15, replica_groups={{0,32},{1,33},{2,34},{3,35},{4,36},{5,37},{6,38},{7,39},{8,40},{9,41},{..., dimensions={0}, use_global_device_ids=true | all-gather | bytes 49152 | tf_op jit(solution)/shard_map/all_gather | solution.py:446
  162.1 11.9 %all_to_all.105 = bf16[16,64,128]{2,1,0:T(8,128)(2,1)S(1)} all-to-all(bf16[16,64,128]{2,1,0:T(8,128)(2,1)S(1)} %broadcast_in_dim.152), channel_id=1, replica_groups={{0,2,4,6,8,10,12,14,16,18,20,22,24,26,28,30},{1,3,5,7,9,11,13,15,17,19,..., dimensions={0} | all-to-all | bytes 524288 | tf_op jit(solution)/shard_map/all_to_all | solution.py:430
  174.1 2.2 all-gather.14
  177.3 1.8 all-gather.15
  179.2 12.3 %all_to_all.106 = bf16[16,64,128]{2,1,0:T(8,128)(2,1)S(1)} all-to-all(bf16[16,64,128]{2,1,0:T(8,128)(2,1)S(1)} %broadcast_in_dim.154), channel_id=1, replica_groups={{0,2,4,6,8,10,12,14,16,18,20,22,24,26,28,30},{1,3,5,7,9,11,13,15,17,19,..., dimensions={0} | all-to-all | bytes 524288 | tf_op jit(solution)/shard_map/all_to_all | solution.py:430
  191.5 2.2 all-gather.16
  194.8 8.7 %all-gather.17 = bf16[128,128]{1,0:T(8,128)(2,1)S(1)} all-gather(bf16[64,128]{1,0:T(8,128)(2,1)S(1)} %get-tuple-element.81), channel_id=19, replica_groups={{0,32},{1,33},{2,34},{3,35},{4,36},{5,37},{6,38},{7,39},{8,40},{9,41},{..., dimensions={0}, use_global_device_ids=true | all-gather | bytes 49152 | tf_op jit(solution)/shard_map/all_gather | solution.py:446
  203.5 11.9 %all_to_all.107 = bf16[16,64,128]{2,1,0:T(8,128)(2,1)S(1)} all-to-all(bf16[16,64,128]{2,1,0:T(8,128)(2,1)S(1)} %broadcast_in_dim.156), channel_id=1, replica_groups={{0,2,4,6,8,10,12,14,16,18,20,22,24,26,28,30},{1,3,5,7,9,11,13,15,17,19,..., dimensions={0} | all-to-all | bytes 524288 | tf_op jit(solution)/shard_map/all_to_all | solution.py:430
  215.5 2.2 all-gather.18
  218.7 1.8 all-gather.19
  220.6 12.3 %all_to_all.108 = bf16[16,64,128]{2,1,0:T(8,128)(2,1)S(1)} all-to-all(bf16[16,64,128]{2,1,0:T(8,128)(2,1)S(1)} %broadcast_in_dim.158), channel_id=1, replica_groups={{0,2,4,6,8,10,12,14,16,18,20,22,24,26,28,30},{1,3,5,7,9,11,13,15,17,19,..., dimensions={0} | all-to-all | bytes 524288 | tf_op jit(solution)/shard_map/all_to_all | solution.py:430
  232.9 2.2 all-gather.20
  236.2 8.1 %all-gather.21 = bf16[128,128]{1,0:T(8,128)(2,1)S(1)} all-gather(bf16[64,128]{1,0:T(8,128)(2,1)S(1)} %get-tuple-element.87), channel_id=23, replica_groups={{0,32},{1,33},{2,34},{3,35},{4,36},{5,37},{6,38},{7,39},{8,40},{9,41},{..., dimensions={0}, use_global_device_ids=true | all-gather | bytes 49152 | tf_op jit(solution)/shard_map/all_gather | solution.py:446
  244.4 11.9 %all_to_all.109 = bf16[16,64,128]{2,1,0:T(8,128)(2,1)S(1)} all-to-all(bf16[16,64,128]{2,1,0:T(8,128)(2,1)S(1)} %broadcast_in_dim.160), channel_id=1, replica_groups={{0,2,4,6,8,10,12,14,16,18,20,22,24,26,28,30},{1,3,5,7,9,11,13,15,17,19,..., dimensions={0} | all-to-all | bytes 524288 | tf_op jit(solution)/shard_map/all_to_all | solution.py:430
  256.3 2.2 all-gather.22
  259.6 1.8 all-gather.23
  261.5 12.3 %all_to_all.110 = bf16[16,64,128]{2,1,0:T(8,128)(2,1)S(1)} all-to-all(bf16[16,64,128]{2,1,0:T(8,128)(2,1)S(1)} %broadcast_in_dim.162), channel_id=1, replica_groups={{0,2,4,6,8,10,12,14,16,18,20,22,24,26,28,30},{1,3,5,7,9,11,13,15,17,19,..., dimensions={0} | all-to-all | bytes 524288 | tf_op jit(solution)/shard_map/all_to_all | solution.py:430
  273.8 2.2 all-gather.24
  277.1 8.0 %all-gather.25 = bf16[128,128]{1,0:T(8,128)(2,1)S(1)} all-gather(bf16[64,128]{1,0:T(8,128)(2,1)S(1)} %get-tuple-element.93), channel_id=27, replica_groups={{0,32},{1,33},{2,34},{3,35},{4,36},{5,37},{6,38},{7,39},{8,40},{9,41},{..., dimensions={0}, use_global_device_ids=true | all-gather | bytes 49152 | tf_op jit(solution)/shard_map/all_gather | solution.py:446
  285.2 11.9 %all_to_all.111 = bf16[16,64,128]{2,1,0:T(8,128)(2,1)S(1)} all-to-all(bf16[16,64,128]{2,1,0:T(8,128)(2,1)S(1)} %broadcast_in_dim.164), channel_id=1, replica_groups={{0,2,4,6,8,10,12,14,16,18,20,22,24,26,28,30},{1,3,5,7,9,11,13,15,17,19,..., dimensions={0} | all-to-all | bytes 524288 | tf_op jit(solution)/shard_map/all_to_all | solution.py:430
  297.1 2.2 all-gather.26
  300.4 1.8 all-gather.27
  302.3 12.3 %all_to_all.112 = bf16[16,64,128]{2,1,0:T(8,128)(2,1)S(1)} all-to-all(bf16[16,64,128]{2,1,0:T(8,128)(2,1)S(1)} %broadcast_in_dim.166), channel_id=1, replica_groups={{0,2,4,6,8,10,12,14,16,18,20,22,24,26,28,30},{1,3,5,7,9,11,13,15,17,19,..., dimensions={0} | all-to-all | bytes 524288 | tf_op jit(solution)/shard_map/all_to_all | solution.py:430
  314.6 2.2 all-gather.28
  317.9 7.9 %all-gather.29 = bf16[128,128]{1,0:T(8,128)(2,1)S(1)} all-gather(bf16[64,128]{1,0:T(8,128)(2,1)S(1)} %get-tuple-element.99), channel_id=31, replica_groups={{0,32},{1,33},{2,34},{3,35},{4,36},{5,37},{6,38},{7,39},{8,40},{9,41},{..., dimensions={0}, use_global_device_ids=true | all-gather | bytes 49152 | tf_op jit(solution)/shard_map/all_gather | solution.py:446
  325.8 11.9 %all_to_all.113 = bf16[16,64,128]{2,1,0:T(8,128)(2,1)S(1)} all-to-all(bf16[16,64,128]{2,1,0:T(8,128)(2,1)S(1)} %broadcast_in_dim.168), channel_id=1, replica_groups={{0,2,4,6,8,10,12,14,16,18,20,22,24,26,28,30},{1,3,5,7,9,11,13,15,17,19,..., dimensions={0} | all-to-all | bytes 524288 | tf_op jit(solution)/shard_map/all_to_all | solution.py:430
  337.8 2.2 all-gather.30
  341.1 1.8 all-gather.31
  342.9 12.3 %all_to_all.114 = bf16[16,64,128]{2,1,0:T(8,128)(2,1)S(1)} all-to-all(bf16[16,64,128]{2,1,0:T(8,128)(2,1)S(1)} %broadcast_in_dim.170), channel_id=1, replica_groups={{0,2,4,6,8,10,12,14,16,18,20,22,24,26,28,30},{1,3,5,7,9,11,13,15,17,19,..., dimensions={0} | all-to-all | bytes 524288 | tf_op jit(solution)/shard_map/all_to_all | solution.py:430
  355.2 2.2 all-gather.32
  357.4 1.1 shard_map.199
  358.5 7.9 %all-gather.33 = bf16[128,128]{1,0:T(8,128)(2,1)S(1)} all-gather(bf16[64,128]{1,0:T(8,128)(2,1)S(1)} %get-tuple-element.105), channel_id=35, replica_groups={{0,32},{1,33},{2,34},{3,35},{4,36},{5,37},{6,38},{7,39},{8,40},{9,41},{..., dimensions={0}, use_global_device_ids=true | all-gather | bytes 49152 | tf_op jit(solution)/shard_map/all_gather | solution.py:446
  367.2 6.2 %all-to-all-start.17 = ((bf16[16,64,128]{2,1,0:T(8,128)(2,1)}), bf16[16,64,128]{2,1,0:T(8,128)(2,1)}, u32[]{:S(2)}, u32[]{:S(2)}) async-start(bf16[16,64,128]{2,1,0:T(8,128)(2,1)} %broadcast_in_dim.172), calls=%async_computation.17 | async-start | bytes 524288 | tf_op jit(solution)/shard_map/all_to_all | solution.py:430
  373.5 6.3 %all-to-all-done.17 = bf16[16,64,128]{2,1,0:T(8,128)(2,1)} async-done(((bf16[16,64,128]{2,1,0:T(8,128)(2,1)}), bf16[16,64,128]{2,1,0:T(8,128)(2,1)}, u32[]{:S(2)}, u32[]{:S(2)}) %all-to-all-start.17) | async-done | bytes 262176 | tf_op jit(solution)/shard_map/all_to_all | solution.py:430
  379.9 2.4 all-gather.34
  382.2 1.7 shard_map.200
  384.6 6.0 %all-to-all-start.18 = ((bf16[32,4,128]{2,1,0:T(4,128)(2,1)}), bf16[32,4,128]{2,1,0:T(4,128)(2,1)S(1)}, u32[]{:S(2)}, u32[]{:S(2)}) async-start(bf16[32,4,128]{2,1,0:T(4,128)(2,1)} %bitcast.24), calls=%async_computation.18 | async-start | bytes 65536 | tf_op jit(solution)/shard_map/all_to_all | solution.py:453
  390.6 5.5 %all-to-all-done.18.temporal_ref = bf16[32,4,128]{2,1,0:T(4,128)(2,1)S(1)} async-done(((bf16[32,4,128]{2,1,0:T(4,128)(2,1)}), bf16[32,4,128]{2,1,0:T(4,128)(2,1)S(1)}, u32[]{:S(2)}, u32[]{:S(2)}) %all-to-all-start.18) | async-done | bytes 32800 | tf_op jit(solution)/shard_map/all_to_all | solution.py:453
  396.1 16.3 %shard_map.202 = bf16[16,32,128]{2,1,0:T(8,128)(2,1)S(1)} custom-call(bf16[32,4,128]{2,1,0:T(4,128)(2,1)S(1)} %all-to-all-done.18.temporal_ref, f32[1,128]{1,0:T(1,128)S(1)} %pad_bitcast_fusion.mask_ref, bf16[1024,4096]{1,0:T(8,128)(2,1)} %all-gather.39.cloned.1.call-done.in_ref, bf16[16,272,1024]{2,1,0:T(8,128)(2,1)} %bitcast.101), custom_call_target="tpu_custom_call" | custom-call | flops 553648128 | bytes 17301504 | tf_op jit(solution)/shard_map/pallas_call | solution.py:372
  412.4 31.3 %all_to_all.115 = bf16[16,32,128]{2,1,0:T(8,128)(2,1)S(1)} all-to-all(bf16[16,32,128]{2,1,0:T(8,128)(2,1)S(1)} %shard_map.202), channel_id=1, replica_groups=mesh['section'=16,'frame'=32] {'section'}, dimensions={0} | all-to-all | bytes 262144 | tf_op jit(solution)/shard_map/all_to_all | solution.py:455
  (94 shorter events, 31.1 us)
Async XLA Ops:
  7.2 28.1 %copy-start = (bf16[1,256,128]{2,1,0:T(8,128)(2,1)S(1)}, bf16[1,256,128]{2,1,0:T(8,128)(2,1)}, u32[]{:S(2)}) copy-start(bf16[1,256,128]{2,1,0:T(8,128)(2,1)} %param.21) | copy-start | bytes 196612
  7.2 28.1 %copy-start.1 = (bf16[1,256,128]{2,1,0:T(8,128)(2,1)S(1)}, bf16[1,256,128]{2,1,0:T(8,128)(2,1)}, u32[]{:S(2)}) copy-start(bf16[1,256,128]{2,1,0:T(8,128)(2,1)} %param.22) | copy-start | bytes 196612
  7.2 388.9 %all-gather.39.cloned.1.call-start = ((), (), s32[]{:S(2)}) async-start(), calls=%async_computation.20 | async-start | bytes 8912896 | tf_op jit(solution)/shard_map/all_gather | solution.py:421
  7.9 388.2 %all-gather.41.cloned.1.call-start = ((), (), s32[]{:S(2)}) async-start(), calls=%async_computation.21 | async-start | bytes 9469952 | tf_op jit(solution)/shard_map/all_gather | solution.py:420
  8.8 1.0 copy-start.2
  9.8 0.9 copy-start.3
  10.7 0.9 copy-start.4
  11.6 0.9 copy-start.5
  12.5 0.9 copy-start.6
  13.4 0.7 copy-start.7
  16.5 16.3 %all-to-all-start = ((bf16[16,64,128]{2,1,0:T(8,128)(2,1)}), bf16[16,64,128]{2,1,0:T(8,128)(2,1)}, u32[]{:S(2)}, u32[]{:S(2)}) async-start(bf16[16,64,128]{2,1,0:T(8,128)(2,1)} %broadcast_in_dim.138), calls=%async_computation | async-start | bytes 524288 | tf_op jit(solution)/shard_map/all_to_all | solution.py:430
  29.3 30.6 %copy-start.8 = (bf16[128,128]{1,0:T(8,128)(2,1)S(1)}, bf16[128,128]{1,0:T(8,128)(2,1)}, u32[]{:S(2)}) copy-start(bf16[128,128]{1,0:T(8,128)(2,1)} %param.16) | copy-start | bytes 98308
  41.9 12.7 %all-to-all-start.1 = ((bf16[16,64,128]{2,1,0:T(8,128)(2,1)}), bf16[16,64,128]{2,1,0:T(8,128)(2,1)}, u32[]{:S(2)}, u32[]{:S(2)}) async-start(bf16[16,64,128]{2,1,0:T(8,128)(2,1)} %broadcast_in_dim.141), calls=%async_computation.1 | async-start | bytes 524288 | tf_op jit(solution)/shard_map/all_to_all | solution.py:430
  317.9 55.5 %copy-start.9 = (s32[4]{0:T(128)S(1)}, s32[4]{0:T(128)}, u32[]{:S(2)}) copy-start(s32[4]{0:T(128)} %param.30) | copy-start | bytes 52
  367.2 12.7 %all-to-all-start.17 = ((bf16[16,64,128]{2,1,0:T(8,128)(2,1)}), bf16[16,64,128]{2,1,0:T(8,128)(2,1)}, u32[]{:S(2)}, u32[]{:S(2)}) async-start(bf16[16,64,128]{2,1,0:T(8,128)(2,1)} %broadcast_in_dim.172), calls=%async_computation.17 | async-start | bytes 524288 | tf_op jit(solution)/shard_map/all_to_all | solution.py:430
  384.6 11.5 %all-to-all-start.18 = ((bf16[32,4,128]{2,1,0:T(4,128)(2,1)}), bf16[32,4,128]{2,1,0:T(4,128)(2,1)S(1)}, u32[]{:S(2)}, u32[]{:S(2)}) async-start(bf16[32,4,128]{2,1,0:T(4,128)(2,1)} %bitcast.24), calls=%async_computation.18 | async-start | bytes 65536 | tf_op jit(solution)/shard_map/all_to_all | solution.py:453
Sparse Core Ops, SparseCore 0:
  10.1 110.3 all-gather.38
  122.6 109.8 all-gather.40

commit v5 on v4

--- a/solution.py
+++ b/solution.py
@@ -157,7 +157,7 @@
         copy.start()
     rows = cotangent_ref.shape[0]
     entries = table_ref.shape[1]
-    picked = lax.broadcasted_iota(jnp.int32, (entries, HEAD), 0) == codes_ref[...]
+    picked = lax.broadcasted_iota(jnp.int32, (entries, HEAD), 0) == codes_ref[:1]
     looked = jnp.dot(
         table_ref[...], picked.astype(jnp.bfloat16), preferred_element_type=jnp.float32
     )
@@ -165,7 +165,8 @@
     wide = jnp.concatenate([wide, jnp.zeros((rows, HEAD - part), jnp.float32)], axis=1)
     wide = jnp.concatenate([wide, jnp.zeros((HEAD - rows, HEAD), jnp.float32)], axis=0)
     lane = lax.broadcasted_iota(jnp.int32, (part, HEAD), 1)
-    extra = jnp.where(lane < rows, looked, pltpu.roll(wide.T[:part], rows, 1)).astype(jnp.bfloat16)
+    masked = wide.T[:part] * codes_ref[1:].astype(jnp.float32)
+    extra = jnp.where(lane < rows, looked, pltpu.roll(masked, rows, 1)).astype(jnp.bfloat16)
     strips = [extra[at : at + 16] for at in range(0, part, 16)]
     strips.append(jnp.zeros((16, small.shape[1] - part // 16 * HEAD), jnp.bfloat16))
     small[...] = jnp.concatenate(strips, axis=1)
@@ -186,13 +187,12 @@
         in_specs=[vmem] * 3 + [anywhere] * 4,
         out_specs=anywhere,
         scratch_shapes=[pltpu.VMEM((16, width), jnp.bfloat16), pltpu.SemaphoreType.DMA((5,))],
-        compiler_params=pltpu.CompilerParams(vmem_limit_bytes=16 * 1024 * 1024),
+        compiler_params=pltpu.CompilerParams(vmem_limit_bytes=56 * 1024 * 1024),
     )(codes, table, cotangent, *weights)
 
 
 def depth_kernel(
     temporal_ref,
-    mask_ref,
     in_ref,
     packed_ref,
     result_ref,
@@ -258,7 +258,7 @@
     known = extra[...].reshape(width, HEAD)
     own = (iota((HEAD, HEAD), 0) == iota((HEAD, HEAD), 1) + rows).astype(jnp.bfloat16)
     own = jnp.where(iota((HEAD, HEAD), 1) < rows, own, jnp.zeros_like(own))
-    masked = (product(known, own) * mask_ref[...]).astype(jnp.bfloat16)
+    masked = product(known, own).astype(jnp.bfloat16)
     masked_all = product(masked, same).astype(jnp.bfloat16)
     fetch_rest[3].wait()
     w_out = rest(3)
@@ -355,14 +355,12 @@
         for up in range(2):
             section = 2 * pair + up
             result_ref[section, : rows // 2] = outs[up].astype(jnp.bfloat16)
-            for half in range(2):
-                first = section * share + half * HEAD
-                result_ref[section, rows // 2 + 8 * half : rows // 2 + 8 * half + 8] = grad[
-                    :, first : first + HEAD
-                ].astype(jnp.bfloat16)
-
-
-def depth_part(temporal, mask, w_in, packed):
+            first = section * share
+            halves = [grad[:frames, first + at : first + at + HEAD] for at in (0, HEAD)]
+            result_ref[section, rows // 2 :] = jnp.concatenate(halves, axis=0).astype(jnp.bfloat16)
+
+
+def depth_part(temporal, w_in, packed):
     width, features = w_in.shape
     part = width // SECTIONS
     rows = temporal.shape[1] * LEVELS
@@ -371,8 +369,8 @@
     read = w_in.size + packed.size
     return pl.pallas_call(
         depth_kernel,
-        out_shape=jax.ShapeDtypeStruct((SECTIONS, rows // 2 + 16, HEAD), jnp.bfloat16),
-        in_specs=[vmem, vmem, anywhere, anywhere],
+        out_shape=jax.ShapeDtypeStruct((SECTIONS, rows // 2 + 8, HEAD), jnp.bfloat16),
+        in_specs=[vmem, anywhere, anywhere],
         out_specs=vmem,
         scratch_shapes=[
             pltpu.VMEM((width, features), jnp.bfloat16),
@@ -384,7 +382,32 @@
         ],
         compiler_params=pltpu.CompilerParams(vmem_limit_bytes=50 * 1024 * 1024),
         cost_estimate=pl.CostEstimate(flops=64 * read, bytes_accessed=2 * read, transcendentals=0),
-    )(temporal, mask, w_in, packed)
+    )(temporal, w_in, packed)
+
+
+def unpack_kernel(result_ref, depth_ref, grad_ref):
+    mine = result_ref[SECTIONS - 1].astype(jnp.float32)
+    rows, part = depth_ref.shape
+    frames = grad_ref.shape[0]
+    cut = rows // 2
+    depth = jnp.concatenate([mine[:cut, :part], mine[:cut, part:]], axis=0)
+    depth_ref[...] = depth.astype(jnp.bfloat16)
+    grad = jnp.concatenate([mine[cut : cut + frames], mine[cut + frames :]], axis=1)
+    grad_ref[...] = grad.astype(jnp.bfloat16)
+
+
+def unpack(results, frames, part):
+    vmem = pl.BlockSpec(memory_space=pltpu.VMEM)
+    depth, grad = pl.pallas_call(
+        unpack_kernel,
+        out_shape=(
+            jax.ShapeDtypeStruct((frames * LEVELS, part), jnp.bfloat16),
+            jax.ShapeDtypeStruct((frames, 2 * HEAD), jnp.bfloat16),
+        ),
+        in_specs=[vmem],
+        out_specs=(vmem, vmem),
+    )(results)
+    return depth.reshape(frames, LEVELS, part), grad
 
 
 def body(
@@ -410,7 +433,10 @@
 
     rows = frames * levels
     codes = jnp.pad(codes, ((0, 0), (1, 0)), constant_values=-1).reshape(1, rows)
-    codes = jnp.pad(codes, ((0, 0), (0, HEAD - rows)), constant_values=-1)
+    mask = jnp.broadcast_to(speaker_mask[:, None], (frames, levels)).reshape(1, rows)
+    codes = jnp.pad(
+        jnp.concatenate([codes, mask], axis=0), ((0, 0), (0, HEAD - rows)), constant_values=-1
+    )
     packed = pack(
         codes,
         code_table.T,
@@ -419,7 +445,6 @@
     )
     packed = lax.all_gather(packed, "section", axis=0)
     w_in = lax.all_gather(w_depth_in.T, "section", axis=0, tiled=True)
-    mask = jnp.pad(jnp.repeat(speaker_mask.astype(jnp.float32), levels), (0, HEAD - rows))[None]
 
     gain = gains[0].astype(jnp.float32)[:, None]
     weight = jnp.concatenate([w_query[0], w_key[0], w_value[0]], axis=1)
@@ -445,19 +470,15 @@
         pairs = plane_pairs((tick - 1) % 2)
         block = lax.all_gather(block, BOTH, axis=0, axis_index_groups=pairs)[0]
         if tick == 2:
-            block = jnp.where(section_id == 0, inflow[CH:], block)
+            block = jnp.where(clock[:1] == tick, inflow[CH:], block)
         clock, held, block = layer(clock, block, held)
     new_keys, new_values, finished = held[0], held[1], held[2]
 
     finished = finished.reshape(2 * CHIPS, frames, HEAD)
     temporal = lax.all_to_all(finished, "frame", split_axis=0, concat_axis=0, tiled=True)
-    results = depth_part(temporal, mask, w_in, packed)
+    results = depth_part(temporal, w_in, packed)
     results = lax.all_to_all(results, "section", split_axis=0, concat_axis=0, tiled=True)
-    mine = results[SECTIONS - 1]
-    cut = frames * levels // 2
-    depth_out = jnp.concatenate([mine[:cut, :part], mine[:cut, part:]], axis=0)
-    depth_out = depth_out.reshape(frames, levels, part)
-    temporal_grad = jnp.concatenate([mine[cut : cut + frames], mine[cut + 8 : cut + 8 + frames]], axis=1)
+    depth_out, temporal_grad = unpack(results, frames, part)
     return (new_keys[None], new_values[None], depth_out, temporal_grad)
 
 

time: 454 us -> 463 us (1.020)
  blocking collectives: 334 us -> 368 us
  starting transfers between devices: 28.3 us -> 9.32 us
  Pallas kernels: 37.9 us -> 56.7 us
  waiting for transfers between devices: 22.6 us -> 4.1 us
  local copies, waits for them, and re-layouts: 10.8 us -> 5.18 us
    all_to_all x15 -> x17, blocking collectives: 182 us -> 206 us  [layer(): lax.all_to_all(jnp.broadcast_to(block[None], (CHIPS,) + block.shape), BOT...]
    pallas_call x1, Pallas kernels: 0.89 us -> 18 us  [pack(): pl.pallas_call(pack_kernel, out_shape=jax.ShapeDtypeStruct((4 * part + 16...]
    all_to_all x3 -> x1, starting transfers between devices: 22.2 us -> 9.25 us  [layer(): lax.all_to_all(jnp.broadcast_to(block[None], (CHIPS,) + block.shape), BOT...]
    all_to_all x3 -> x1, waiting for transfers between devices: 16.4 us -> 3.4 us  [layer(): lax.all_to_all(jnp.broadcast_to(block[None], (CHIPS,) + block.shape), BOT...]
    all_to_all x0 -> x1, blocking collectives: none -> 11.2 us  [body(): lax.all_to_all(finished, 'frame', split_axis=0, concat_axis=0, tiled=True)]
    all_to_all x1 -> x0, starting transfers between devices: 5.96 us -> none  [body(): lax.all_to_all(finished, 'frame', split_axis=0, concat_axis=0, tiled=True)]
    all_to_all x1 -> x0, waiting for transfers between devices: 5.51 us -> none  [body(): lax.all_to_all(finished, 'frame', split_axis=0, concat_axis=0, tiled=True)]
    unnamed x20 -> x6, local copies, waits for them, and re-layouts: 5.28 us -> 0.01 us
  transfers between devices with their start and end apart: 6 -> 3, of which waited for: 4 -> 1; matrix products, arithmetic and copies ran while one was open for 2% -> 2% of each run, Pallas kernels for 5% -> 8%
where the time goes in v5:
time: 463 us; the launch traced here: 461 us
  blocking collectives  368 us (79%)
  Pallas kernels  56.7 us (12%)
  between operations  14.4 us (3%)
  starting transfers between devices  9.32 us (2%)
  local copies, waits for them, and re-layouts  5.18 us (1%)
    all_to_all x17, blocking collectives, layer(): lax.all_to_all(jnp.broadcast_to(block[None], (CHIPS,) + block.shape), BOT...  206 us
    all_gather x17, blocking collectives, body(): block = lax.all_gather(block, BOTH, axis=0, axis_index_groups=pairs)[0]  81.3 us
    all_gather x18, blocking collectives, layer(): rows = lax.all_gather(got, BOTH, axis=0, axis_index_groups=core_pairs())  39.2 us
    all_to_all x1, blocking collectives, body(): lax.all_to_all(results, 'section', split_axis=0, concat_axis=0, tiled=True)  30.7 us
    pallas_call x18, Pallas kernels, layer_step(): pl.pallas_call(layer_kernel, out_shape=(jax.ShapeDtypeStruct(clock.shape,...  20.8 us
    pallas_call x1, Pallas kernels, pack(): pl.pallas_call(pack_kernel, out_shape=jax.ShapeDtypeStruct((4 * part + 16...  18 us
    pallas_call x1, Pallas kernels, depth_part(): pl.pallas_call(depth_kernel, out_shape=jax.ShapeDtypeStruct((SECTIONS, ro...  16.3 us
    all_to_all x1, blocking collectives, body(): lax.all_to_all(finished, 'frame', split_axis=0, concat_axis=0, tiled=True)  11.2 us
  transfers between devices with their start and end apart: 3, of which 1 were waited for; matrix products, arithmetic and copies ran while one was open for 2% of the time, Pallas kernels for 8%

profile of v5, /device:TPU:6, one launch (start us, length us, event | category | flops | bytes accessed | tf_op | source)
XLA Modules:
  0.0 460.7 jit_solution(1680879748659971464)
XLA Ops:
  10.2 18.0 %shard_map.201 = bf16[272,1024]{1,0:T(8,128)(2,1)} custom-call(s32[2,128]{1,0:T(2,128)} %pad.9.codes_ref, bf16[64,2048]{1,0:T(8,128)(2,1)} %bitcast.94, bf16[32,64]{1,0:T(8,128)(2,1)} %bitcast.100, bf16[64,1024]{1,0:T(8,128)(2,1)} %bitcast.95, bf16[64,1024]{1,0:T(8,128)(2,1)} %bitcast.96, bf16[64,1024]{1,0:T(8,128)(2,1)} %bitcast.97, bf16[64,1024]{1,0:T(8,128)(2,1)} %out_ref.1), custom_call_target="tpu_custom_call" | custom-call | tf_op jit(solution)/shard_map/pallas_call | solution.py:184
  29.7 9.2 %all-to-all-start = ((bf16[16,64,128]{2,1,0:T(8,128)(2,1)}), bf16[16,64,128]{2,1,0:T(8,128)(2,1)S(1)}, u32[]{:S(2)}, u32[]{:S(2)}) async-start(bf16[16,64,128]{2,1,0:T(8,128)(2,1)} %broadcast_in_dim.148), calls=%async_computation | async-start | bytes 524288 | tf_op jit(solution)/shard_map/all_to_all | solution.py:455
  39.7 2.2 multiply_convert_fusion.weight_ref
  41.9 3.4 all-to-all-done
  45.3 2.3 all-gather
  47.7 1.1 shard_map.183
  48.8 4.7 %all-gather.1 = bf16[128,128]{1,0:T(8,128)(2,1)S(1)} all-gather(bf16[64,128]{1,0:T(8,128)(2,1)S(1)} %get-tuple-element.59), channel_id=3, replica_groups={{0,32},{1,33},{2,34},{3,35},{4,36},{5,37},{6,38},{7,39},{8,40},{9,41},{..., dimensions={0}, use_global_device_ids=true | all-gather | bytes 49152 | tf_op jit(solution)/shard_map/all_gather | solution.py:471
  53.6 12.0 %all_to_all.100 = bf16[16,64,128]{2,1,0:T(8,128)(2,1)S(1)} all-to-all(bf16[16,64,128]{2,1,0:T(8,128)(2,1)S(1)} %broadcast_in_dim.151), channel_id=1, replica_groups={{0,2,4,6,8,10,12,14,16,18,20,22,24,26,28,30},{1,3,5,7,9,11,13,15,17,19,..., dimensions={0} | all-to-all | bytes 524288 | tf_op jit(solution)/shard_map/all_to_all | solution.py:455
  65.6 2.2 all-gather.2
  68.9 1.8 all-gather.3
  70.8 12.3 %all_to_all.101 = bf16[16,64,128]{2,1,0:T(8,128)(2,1)S(1)} all-to-all(bf16[16,64,128]{2,1,0:T(8,128)(2,1)S(1)} %broadcast_in_dim.154), channel_id=1, replica_groups={{0,2,4,6,8,10,12,14,16,18,20,22,24,26,28,30},{1,3,5,7,9,11,13,15,17,19,..., dimensions={0} | all-to-all | bytes 524288 | tf_op jit(solution)/shard_map/all_to_all | solution.py:455
  83.1 2.2 all-gather.4
  85.2 1.1 shard_map.185
  86.4 5.1 %all-gather.5 = bf16[128,128]{1,0:T(8,128)(2,1)S(1)} all-gather(bf16[64,128]{1,0:T(8,128)(2,1)S(1)} %get-tuple-element.65), channel_id=7, replica_groups={{0,32},{1,33},{2,34},{3,35},{4,36},{5,37},{6,38},{7,39},{8,40},{9,41},{..., dimensions={0}, use_global_device_ids=true | all-gather | bytes 49152 | tf_op jit(solution)/shard_map/all_gather | solution.py:471
  91.5 11.9 %all_to_all.102 = bf16[16,64,128]{2,1,0:T(8,128)(2,1)S(1)} all-to-all(bf16[16,64,128]{2,1,0:T(8,128)(2,1)S(1)} %broadcast_in_dim.156), channel_id=1, replica_groups={{0,2,4,6,8,10,12,14,16,18,20,22,24,26,28,30},{1,3,5,7,9,11,13,15,17,19,..., dimensions={0} | all-to-all | bytes 524288 | tf_op jit(solution)/shard_map/all_to_all | solution.py:455
  103.4 2.2 all-gather.6
  106.7 1.8 all-gather.7
  108.6 12.3 %all_to_all.103 = bf16[16,64,128]{2,1,0:T(8,128)(2,1)S(1)} all-to-all(bf16[16,64,128]{2,1,0:T(8,128)(2,1)S(1)} %broadcast_in_dim.158), channel_id=1, replica_groups={{0,2,4,6,8,10,12,14,16,18,20,22,24,26,28,30},{1,3,5,7,9,11,13,15,17,19,..., dimensions={0} | all-to-all | bytes 524288 | tf_op jit(solution)/shard_map/all_to_all | solution.py:455
  120.9 2.2 all-gather.8
  124.2 8.1 %all-gather.9 = bf16[128,128]{1,0:T(8,128)(2,1)S(1)} all-gather(bf16[64,128]{1,0:T(8,128)(2,1)S(1)} %get-tuple-element.71), channel_id=11, replica_groups={{0,32},{1,33},{2,34},{3,35},{4,36},{5,37},{6,38},{7,39},{8,40},{9,41},{..., dimensions={0}, use_global_device_ids=true | all-gather | bytes 49152 | tf_op jit(solution)/shard_map/all_gather | solution.py:471
  132.4 11.9 %all_to_all.104 = bf16[16,64,128]{2,1,0:T(8,128)(2,1)S(1)} all-to-all(bf16[16,64,128]{2,1,0:T(8,128)(2,1)S(1)} %broadcast_in_dim.160), channel_id=1, replica_groups={{0,2,4,6,8,10,12,14,16,18,20,22,24,26,28,30},{1,3,5,7,9,11,13,15,17,19,..., dimensions={0} | all-to-all | bytes 524288 | tf_op jit(solution)/shard_map/all_to_all | solution.py:455
  144.3 2.2 all-gather.10
  147.6 1.8 all-gather.11
  149.5 12.3 %all_to_all.105 = bf16[16,64,128]{2,1,0:T(8,128)(2,1)S(1)} all-to-all(bf16[16,64,128]{2,1,0:T(8,128)(2,1)S(1)} %broadcast_in_dim.162), channel_id=1, replica_groups={{0,2,4,6,8,10,12,14,16,18,20,22,24,26,28,30},{1,3,5,7,9,11,13,15,17,19,..., dimensions={0} | all-to-all | bytes 524288 | tf_op jit(solution)/shard_map/all_to_all | solution.py:455
  161.8 2.2 all-gather.12
  165.1 8.6 %all-gather.13 = bf16[128,128]{1,0:T(8,128)(2,1)S(1)} all-gather(bf16[64,128]{1,0:T(8,128)(2,1)S(1)} %get-tuple-element.77), channel_id=15, replica_groups={{0,32},{1,33},{2,34},{3,35},{4,36},{5,37},{6,38},{7,39},{8,40},{9,41},{..., dimensions={0}, use_global_device_ids=true | all-gather | bytes 49152 | tf_op jit(solution)/shard_map/all_gather | solution.py:471
  173.7 11.9 %all_to_all.106 = bf16[16,64,128]{2,1,0:T(8,128)(2,1)S(1)} all-to-all(bf16[16,64,128]{2,1,0:T(8,128)(2,1)S(1)} %broadcast_in_dim.164), channel_id=1, replica_groups={{0,2,4,6,8,10,12,14,16,18,20,22,24,26,28,30},{1,3,5,7,9,11,13,15,17,19,..., dimensions={0} | all-to-all | bytes 524288 | tf_op jit(solution)/shard_map/all_to_all | solution.py:455
  185.7 2.2 all-gather.14
  189.0 1.8 all-gather.15
  190.9 12.3 %all_to_all.107 = bf16[16,64,128]{2,1,0:T(8,128)(2,1)S(1)} all-to-all(bf16[16,64,128]{2,1,0:T(8,128)(2,1)S(1)} %broadcast_in_dim.166), channel_id=1, replica_groups={{0,2,4,6,8,10,12,14,16,18,20,22,24,26,28,30},{1,3,5,7,9,11,13,15,17,19,..., dimensions={0} | all-to-all | bytes 524288 | tf_op jit(solution)/shard_map/all_to_all | solution.py:455
  203.2 2.2 all-gather.16
  206.4 8.2 %all-gather.17 = bf16[128,128]{1,0:T(8,128)(2,1)S(1)} all-gather(bf16[64,128]{1,0:T(8,128)(2,1)S(1)} %get-tuple-element.83), channel_id=19, replica_groups={{0,32},{1,33},{2,34},{3,35},{4,36},{5,37},{6,38},{7,39},{8,40},{9,41},{..., dimensions={0}, use_global_device_ids=true | all-gather | bytes 49152 | tf_op jit(solution)/shard_map/all_gather | solution.py:471
  214.7 11.9 %all_to_all.108 = bf16[16,64,128]{2,1,0:T(8,128)(2,1)S(1)} all-to-all(bf16[16,64,128]{2,1,0:T(8,128)(2,1)S(1)} %broadcast_in_dim.168), channel_id=1, replica_groups={{0,2,4,6,8,10,12,14,16,18,20,22,24,26,28,30},{1,3,5,7,9,11,13,15,17,19,..., dimensions={0} | all-to-all | bytes 524288 | tf_op jit(solution)/shard_map/all_to_all | solution.py:455
  226.7 2.2 all-gather.18
  230.0 1.8 all-gather.19
  231.9 12.3 %all_to_all.109 = bf16[16,64,128]{2,1,0:T(8,128)(2,1)S(1)} all-to-all(bf16[16,64,128]{2,1,0:T(8,128)(2,1)S(1)} %broadcast_in_dim.170), channel_id=1, replica_groups={{0,2,4,6,8,10,12,14,16,18,20,22,24,26,28,30},{1,3,5,7,9,11,13,15,17,19,..., dimensions={0} | all-to-all | bytes 524288 | tf_op jit(solution)/shard_map/all_to_all | solution.py:455
  244.1 2.2 all-gather.20
  247.4 8.1 %all-gather.21 = bf16[128,128]{1,0:T(8,128)(2,1)S(1)} all-gather(bf16[64,128]{1,0:T(8,128)(2,1)S(1)} %get-tuple-element.89), channel_id=23, replica_groups={{0,32},{1,33},{2,34},{3,35},{4,36},{5,37},{6,38},{7,39},{8,40},{9,41},{..., dimensions={0}, use_global_device_ids=true | all-gather | bytes 49152 | tf_op jit(solution)/shard_map/all_gather | solution.py:471
  255.6 11.9 %all_to_all.110 = bf16[16,64,128]{2,1,0:T(8,128)(2,1)S(1)} all-to-all(bf16[16,64,128]{2,1,0:T(8,128)(2,1)S(1)} %broadcast_in_dim.172), channel_id=1, replica_groups={{0,2,4,6,8,10,12,14,16,18,20,22,24,26,28,30},{1,3,5,7,9,11,13,15,17,19,..., dimensions={0} | all-to-all | bytes 524288 | tf_op jit(solution)/shard_map/all_to_all | solution.py:455
  267.5 2.2 all-gather.22
  269.7 1.1 shard_map.194
  270.8 1.8 all-gather.23
  272.7 12.3 %all_to_all.111 = bf16[16,64,128]{2,1,0:T(8,128)(2,1)S(1)} all-to-all(bf16[16,64,128]{2,1,0:T(8,128)(2,1)S(1)} %broadcast_in_dim.174), channel_id=1, replica_groups={{0,2,4,6,8,10,12,14,16,18,20,22,24,26,28,30},{1,3,5,7,9,11,13,15,17,19,..., dimensions={0} | all-to-all | bytes 524288 | tf_op jit(solution)/shard_map/all_to_all | solution.py:455
  285.0 2.2 all-gather.24
  288.3 8.0 %all-gather.25 = bf16[128,128]{1,0:T(8,128)(2,1)S(1)} all-gather(bf16[64,128]{1,0:T(8,128)(2,1)S(1)} %get-tuple-element.95), channel_id=27, replica_groups={{0,32},{1,33},{2,34},{3,35},{4,36},{5,37},{6,38},{7,39},{8,40},{9,41},{..., dimensions={0}, use_global_device_ids=true | all-gather | bytes 49152 | tf_op jit(solution)/shard_map/all_gather | solution.py:471
  296.3 11.9 %all_to_all.112 = bf16[16,64,128]{2,1,0:T(8,128)(2,1)S(1)} all-to-all(bf16[16,64,128]{2,1,0:T(8,128)(2,1)S(1)} %broadcast_in_dim.176), channel_id=1, replica_groups={{0,2,4,6,8,10,12,14,16,18,20,22,24,26,28,30},{1,3,5,7,9,11,13,15,17,19,..., dimensions={0} | all-to-all | bytes 524288 | tf_op jit(solution)/shard_map/all_to_all | solution.py:455
  308.3 2.2 all-gather.26
  311.6 1.8 all-gather.27
  313.5 12.3 %all_to_all.113 = bf16[16,64,128]{2,1,0:T(8,128)(2,1)S(1)} all-to-all(bf16[16,64,128]{2,1,0:T(8,128)(2,1)S(1)} %broadcast_in_dim.178), channel_id=1, replica_groups={{0,2,4,6,8,10,12,14,16,18,20,22,24,26,28,30},{1,3,5,7,9,11,13,15,17,19,..., dimensions={0} | all-to-all | bytes 524288 | tf_op jit(solution)/shard_map/all_to_all | solution.py:455
  325.7 2.2 all-gather.28
  329.0 7.9 %all-gather.29 = bf16[128,128]{1,0:T(8,128)(2,1)S(1)} all-gather(bf16[64,128]{1,0:T(8,128)(2,1)S(1)} %get-tuple-element.101), channel_id=31, replica_groups={{0,32},{1,33},{2,34},{3,35},{4,36},{5,37},{6,38},{7,39},{8,40},{9,41},{..., dimensions={0}, use_global_device_ids=true | all-gather | bytes 49152 | tf_op jit(solution)/shard_map/all_gather | solution.py:471
  337.0 11.9 %all_to_all.114 = bf16[16,64,128]{2,1,0:T(8,128)(2,1)S(1)} all-to-all(bf16[16,64,128]{2,1,0:T(8,128)(2,1)S(1)} %broadcast_in_dim.180), channel_id=1, replica_groups={{0,2,4,6,8,10,12,14,16,18,20,22,24,26,28,30},{1,3,5,7,9,11,13,15,17,19,..., dimensions={0} | all-to-all | bytes 524288 | tf_op jit(solution)/shard_map/all_to_all | solution.py:455
  348.9 2.2 all-gather.30
  352.2 1.8 all-gather.31
  354.1 12.3 %all_to_all.115 = bf16[16,64,128]{2,1,0:T(8,128)(2,1)S(1)} all-to-all(bf16[16,64,128]{2,1,0:T(8,128)(2,1)S(1)} %broadcast_in_dim.182), channel_id=1, replica_groups={{0,2,4,6,8,10,12,14,16,18,20,22,24,26,28,30},{1,3,5,7,9,11,13,15,17,19,..., dimensions={0} | all-to-all | bytes 524288 | tf_op jit(solution)/shard_map/all_to_all | solution.py:455
  366.4 2.2 all-gather.32
  369.7 7.9 %all-gather.33 = bf16[128,128]{1,0:T(8,128)(2,1)S(1)} all-gather(bf16[64,128]{1,0:T(8,128)(2,1)S(1)} %get-tuple-element.107), channel_id=35, replica_groups={{0,32},{1,33},{2,34},{3,35},{4,36},{5,37},{6,38},{7,39},{8,40},{9,41},{..., dimensions={0}, use_global_device_ids=true | all-gather | bytes 49152 | tf_op jit(solution)/shard_map/all_gather | solution.py:471
  377.6 11.9 %all_to_all.116 = bf16[16,64,128]{2,1,0:T(8,128)(2,1)S(1)} all-to-all(bf16[16,64,128]{2,1,0:T(8,128)(2,1)S(1)} %broadcast_in_dim.184), channel_id=1, replica_groups={{0,2,4,6,8,10,12,14,16,18,20,22,24,26,28,30},{1,3,5,7,9,11,13,15,17,19,..., dimensions={0} | all-to-all | bytes 524288 | tf_op jit(solution)/shard_map/all_to_all | solution.py:455
  389.5 2.2 all-gather.34
  391.7 1.7 shard_map.200
  394.1 11.2 %all_to_all.117.temporal_ref = bf16[32,4,128]{2,1,0:T(4,128)(2,1)S(1)} all-to-all(bf16[32,4,128]{2,1,0:T(4,128)(2,1)S(1)} %bitcast.98), channel_id=1, replica_groups=mesh['section'=16,'frame'=32] {'frame'}, dimensions={0} | all-to-all | bytes 65536 | tf_op jit(solution)/shard_map/all_to_all | solution.py:478
  405.3 16.3 %shard_map.202 = bf16[16,24,128]{2,1,0:T(8,128)(2,1)S(1)} custom-call(bf16[32,4,128]{2,1,0:T(4,128)(2,1)S(1)} %all_to_all.117.temporal_ref, bf16[1024,4096]{1,0:T(8,128)(2,1)} %all-gather.39.cloned.1.call-done.in_ref, bf16[16,272,1024]{2,1,0:T(8,128)(2,1)} %bitcast.89), custom_call_target="tpu_custom_call" | custom-call | flops 553648128 | bytes 17301504 | tf_op jit(solution)/shard_map/pallas_call | solution.py:370
  421.6 30.7 %all_to_all.118.result_ref = bf16[16,24,128]{2,1,0:T(8,128)(2,1)} all-to-all(bf16[16,24,128]{2,1,0:T(8,128)(2,1)S(1)} %shard_map.202), channel_id=1, replica_groups=mesh['section'=16,'frame'=32] {'section'}, dimensions={0} | all-to-all | bytes 196608 | tf_op jit(solution)/shard_map/all_to_all | solution.py:480
  452.3 1.6 shard_map.203
  (73 shorter events, 22.4 us)
Async XLA Ops:
  7.2 40.5 %copy-start = (bf16[1,256,128]{2,1,0:T(8,128)(2,1)S(1)}, bf16[1,256,128]{2,1,0:T(8,128)(2,1)}, u32[]{:S(2)}) copy-start(bf16[1,256,128]{2,1,0:T(8,128)(2,1)} %param.21) | copy-start | bytes 196612
  7.2 40.5 %copy-start.1 = (bf16[1,256,128]{2,1,0:T(8,128)(2,1)S(1)}, bf16[1,256,128]{2,1,0:T(8,128)(2,1)}, u32[]{:S(2)}) copy-start(bf16[1,256,128]{2,1,0:T(8,128)(2,1)} %param.22) | copy-start | bytes 196612
  7.2 398.1 %all-gather.39.cloned.1.call-start = ((), (), s32[]{:S(2)}) async-start(), calls=%async_computation.20 | async-start | bytes 8912896 | tf_op jit(solution)/shard_map/all_gather | solution.py:447
  7.9 397.4 %all-gather.41.cloned.1.call-start = ((), (), s32[]{:S(2)}) async-start(), calls=%async_computation.21 | async-start | bytes 9469952 | tf_op jit(solution)/shard_map/all_gather | solution.py:446
  29.7 15.6 %all-to-all-start = ((bf16[16,64,128]{2,1,0:T(8,128)(2,1)}), bf16[16,64,128]{2,1,0:T(8,128)(2,1)S(1)}, u32[]{:S(2)}, u32[]{:S(2)}) async-start(bf16[16,64,128]{2,1,0:T(8,128)(2,1)} %broadcast_in_dim.148), calls=%async_computation | async-start | bytes 524288 | tf_op jit(solution)/shard_map/all_to_all | solution.py:455
  45.3 25.4 %copy-start.2 = (bf16[128,128]{1,0:T(8,128)(2,1)S(1)}, bf16[128,128]{1,0:T(8,128)(2,1)}, u32[]{:S(2)}) copy-start(bf16[128,128]{1,0:T(8,128)(2,1)} %param.16) | copy-start | bytes 98308
Sparse Core Ops, SparseCore 0:
  10.1 110.3 all-gather.38
  122.6 109.8 all-gather.40

commit v6 on v5

--- a/solution.py
+++ b/solution.py
@@ -138,6 +138,7 @@
 
 def pack_kernel(
     codes_ref,
+    mask_ref,
     table_ref,
     cotangent_ref,
     query_ref,
@@ -145,7 +146,6 @@
     value_ref,
     out_ref,
     packed_ref,
-    small,
     sems,
 ):
     part = out_ref.shape[0]
@@ -157,7 +157,15 @@
         copy.start()
     rows = cotangent_ref.shape[0]
     entries = table_ref.shape[1]
-    picked = lax.broadcasted_iota(jnp.int32, (entries, HEAD), 0) == codes_ref[:1]
+    frames, coded = codes_ref.shape
+    column = lax.broadcasted_iota(jnp.int32, (1, HEAD), 1)
+    codes = jnp.full((1, HEAD), -1, jnp.int32)
+    mask = jnp.zeros((1, HEAD), jnp.float32)
+    for frame in range(frames):
+        mask = jnp.where(column // LEVELS == frame, mask_ref[frame].astype(jnp.float32), mask)
+        for at in range(coded):
+            codes = jnp.where(column == frame * LEVELS + at + 1, codes_ref[frame, at], codes)
+    picked = lax.broadcasted_iota(jnp.int32, (entries, HEAD), 0) == codes
     looked = jnp.dot(
         table_ref[...], picked.astype(jnp.bfloat16), preferred_element_type=jnp.float32
     )
@@ -165,30 +173,28 @@
     wide = jnp.concatenate([wide, jnp.zeros((rows, HEAD - part), jnp.float32)], axis=1)
     wide = jnp.concatenate([wide, jnp.zeros((HEAD - rows, HEAD), jnp.float32)], axis=0)
     lane = lax.broadcasted_iota(jnp.int32, (part, HEAD), 1)
-    masked = wide.T[:part] * codes_ref[1:].astype(jnp.float32)
+    masked = wide.T[:part] * mask
     extra = jnp.where(lane < rows, looked, pltpu.roll(masked, rows, 1)).astype(jnp.bfloat16)
     strips = [extra[at : at + 16] for at in range(0, part, 16)]
-    strips.append(jnp.zeros((16, small.shape[1] - part // 16 * HEAD), jnp.bfloat16))
-    small[...] = jnp.concatenate(strips, axis=1)
-    last = pltpu.make_async_copy(small, packed_ref.at[pl.ds(4 * part, 16)], sems.at[4])
-    last.start()
+    strips.append(jnp.zeros((16, packed_ref.shape[1] - part // 16 * HEAD), jnp.bfloat16))
+    packed_ref[pl.ds(4 * part, 16)] = jnp.concatenate(strips, axis=1)
     for copy in copies:
         copy.wait()
-    last.wait()
-
-
-def pack(codes, table, cotangent, weights):
+
+
+def pack(codes, mask, table, cotangent, weights):
     part, width = weights[0].shape
     vmem = pl.BlockSpec(memory_space=pltpu.VMEM)
+    smem = pl.BlockSpec(memory_space=pltpu.SMEM)
     anywhere = pl.BlockSpec(memory_space=pl.ANY)
     return pl.pallas_call(
         pack_kernel,
         out_shape=jax.ShapeDtypeStruct((4 * part + 16, width), jnp.bfloat16),
-        in_specs=[vmem] * 3 + [anywhere] * 4,
-        out_specs=anywhere,
-        scratch_shapes=[pltpu.VMEM((16, width), jnp.bfloat16), pltpu.SemaphoreType.DMA((5,))],
+        in_specs=[smem, smem, vmem, vmem] + [anywhere] * 4,
+        out_specs=vmem,
+        scratch_shapes=[pltpu.SemaphoreType.DMA((4,))],
         compiler_params=pltpu.CompilerParams(vmem_limit_bytes=56 * 1024 * 1024),
-    )(codes, table, cotangent, *weights)
+    )(codes, mask, table, cotangent, *weights)
 
 
 def depth_kernel(
@@ -431,16 +437,11 @@
     section_id = lax.axis_index("section")
     frames, levels, part = cotangent.shape
 
-    rows = frames * levels
-    codes = jnp.pad(codes, ((0, 0), (1, 0)), constant_values=-1).reshape(1, rows)
-    mask = jnp.broadcast_to(speaker_mask[:, None], (frames, levels)).reshape(1, rows)
-    codes = jnp.pad(
-        jnp.concatenate([codes, mask], axis=0), ((0, 0), (0, HEAD - rows)), constant_values=-1
-    )
     packed = pack(
         codes,
+        speaker_mask,
         code_table.T,
-        cotangent.reshape(rows, part),
+        cotangent.reshape(frames * levels, part),
         (w_dquery.T, w_dkey.T, w_dvalue.T, w_dout),
     )
     packed = lax.all_gather(packed, "section", axis=0)

time: 463 us -> 446 us (0.963)
  Pallas kernels: 56.7 us -> 41.5 us
    pallas_call x1, Pallas kernels: 18 us -> 2.92 us  [pack(): pl.pallas_call(pack_kernel, out_shape=jax.ShapeDtypeStruct((4 * part + 16...]
  transfers between devices with their start and end apart: 3 -> 3, of which waited for: 1 -> 1; matrix products, arithmetic and copies ran while one was open for 2% -> 1% of each run, Pallas kernels for 8% -> 5%
where the time goes in v6:
time: 446 us; the launch traced here: 443 us
  blocking collectives  368 us (83%)
  Pallas kernels  41.5 us (9%)
  between operations  14.4 us (3%)
  starting transfers between devices  9.32 us (2%)
    all_to_all x17, blocking collectives, layer(): lax.all_to_all(jnp.broadcast_to(block[None], (CHIPS,) + block.shape), BOT...  205 us
    all_gather x17, blocking collectives, body(): block = lax.all_gather(block, BOTH, axis=0, axis_index_groups=pairs)[0]  81.7 us
    all_gather x18, blocking collectives, layer(): rows = lax.all_gather(got, BOTH, axis=0, axis_index_groups=core_pairs())  39.4 us
    all_to_all x1, blocking collectives, body(): lax.all_to_all(results, 'section', split_axis=0, concat_axis=0, tiled=True)  30.4 us
    pallas_call x18, Pallas kernels, layer_step(): pl.pallas_call(layer_kernel, out_shape=(jax.ShapeDtypeStruct(clock.shape,...  20.7 us
    pallas_call x1, Pallas kernels, depth_part(): pl.pallas_call(depth_kernel, out_shape=jax.ShapeDtypeStruct((SECTIONS, ro...  16.3 us
    all_to_all x1, blocking collectives, body(): lax.all_to_all(finished, 'frame', split_axis=0, concat_axis=0, tiled=True)  11.2 us
    all_to_all x1, starting transfers between devices, layer(): lax.all_to_all(jnp.broadcast_to(block[None], (CHIPS,) + block.shape), BOT...  9.25 us
  transfers between devices with their start and end apart: 3, of which 1 were waited for; matrix products, arithmetic and copies ran while one was open for 1% of the time, Pallas kernels for 5%

profile of v6, /device:TPU:6, one launch (start us, length us, event | category | flops | bytes accessed | tf_op | source)
XLA Modules:
  0.0 443.5 jit_solution(10796190388197418439)
XLA Ops:
  8.0 2.9 shard_map.201
  12.4 9.2 %all-to-all-start = ((bf16[16,64,128]{2,1,0:T(8,128)(2,1)}), bf16[16,64,128]{2,1,0:T(8,128)(2,1)S(1)}, u32[]{:S(2)}, u32[]{:S(2)}) async-start(bf16[16,64,128]{2,1,0:T(8,128)(2,1)} %broadcast_in_dim.142), calls=%async_computation | async-start | bytes 524288 | tf_op jit(solution)/shard_map/all_to_all | solution.py:456
  22.4 2.2 multiply_convert_fusion.weight_ref
  24.6 3.4 all-to-all-done
  28.1 2.3 all-gather
  30.4 1.1 shard_map.183
  31.5 4.7 %all-gather.1 = bf16[128,128]{1,0:T(8,128)(2,1)S(1)} all-gather(bf16[64,128]{1,0:T(8,128)(2,1)S(1)} %get-tuple-element.59), channel_id=3, replica_groups={{0,32},{1,33},{2,34},{3,35},{4,36},{5,37},{6,38},{7,39},{8,40},{9,41},{..., dimensions={0}, use_global_device_ids=true | all-gather | bytes 49152 | tf_op jit(solution)/shard_map/all_gather | solution.py:472
  36.3 11.8 %all_to_all.100 = bf16[16,64,128]{2,1,0:T(8,128)(2,1)S(1)} all-to-all(bf16[16,64,128]{2,1,0:T(8,128)(2,1)S(1)} %broadcast_in_dim.145), channel_id=1, replica_groups={{0,2,4,6,8,10,12,14,16,18,20,22,24,26,28,30},{1,3,5,7,9,11,13,15,17,19,..., dimensions={0} | all-to-all | bytes 524288 | tf_op jit(solution)/shard_map/all_to_all | solution.py:456
  48.1 2.2 all-gather.2
  51.4 1.8 all-gather.3
  53.3 12.3 %all_to_all.101 = bf16[16,64,128]{2,1,0:T(8,128)(2,1)S(1)} all-to-all(bf16[16,64,128]{2,1,0:T(8,128)(2,1)S(1)} %broadcast_in_dim.148), channel_id=1, replica_groups={{0,2,4,6,8,10,12,14,16,18,20,22,24,26,28,30},{1,3,5,7,9,11,13,15,17,19,..., dimensions={0} | all-to-all | bytes 524288 | tf_op jit(solution)/shard_map/all_to_all | solution.py:456
  65.6 2.2 all-gather.4
  67.8 1.1 shard_map.185
  68.9 5.2 %all-gather.5 = bf16[128,128]{1,0:T(8,128)(2,1)S(1)} all-gather(bf16[64,128]{1,0:T(8,128)(2,1)S(1)} %get-tuple-element.65), channel_id=7, replica_groups={{0,32},{1,33},{2,34},{3,35},{4,36},{5,37},{6,38},{7,39},{8,40},{9,41},{..., dimensions={0}, use_global_device_ids=true | all-gather | bytes 49152 | tf_op jit(solution)/shard_map/all_gather | solution.py:472
  74.2 11.9 %all_to_all.102 = bf16[16,64,128]{2,1,0:T(8,128)(2,1)S(1)} all-to-all(bf16[16,64,128]{2,1,0:T(8,128)(2,1)S(1)} %broadcast_in_dim.150), channel_id=1, replica_groups={{0,2,4,6,8,10,12,14,16,18,20,22,24,26,28,30},{1,3,5,7,9,11,13,15,17,19,..., dimensions={0} | all-to-all | bytes 524288 | tf_op jit(solution)/shard_map/all_to_all | solution.py:456
  86.1 2.2 all-gather.6
  89.4 1.8 all-gather.7
  91.3 12.3 %all_to_all.103 = bf16[16,64,128]{2,1,0:T(8,128)(2,1)S(1)} all-to-all(bf16[16,64,128]{2,1,0:T(8,128)(2,1)S(1)} %broadcast_in_dim.152), channel_id=1, replica_groups={{0,2,4,6,8,10,12,14,16,18,20,22,24,26,28,30},{1,3,5,7,9,11,13,15,17,19,..., dimensions={0} | all-to-all | bytes 524288 | tf_op jit(solution)/shard_map/all_to_all | solution.py:456
  103.6 2.2 all-gather.8
  106.9 8.2 %all-gather.9 = bf16[128,128]{1,0:T(8,128)(2,1)S(1)} all-gather(bf16[64,128]{1,0:T(8,128)(2,1)S(1)} %get-tuple-element.71), channel_id=11, replica_groups={{0,32},{1,33},{2,34},{3,35},{4,36},{5,37},{6,38},{7,39},{8,40},{9,41},{..., dimensions={0}, use_global_device_ids=true | all-gather | bytes 49152 | tf_op jit(solution)/shard_map/all_gather | solution.py:472
  115.1 11.9 %all_to_all.104 = bf16[16,64,128]{2,1,0:T(8,128)(2,1)S(1)} all-to-all(bf16[16,64,128]{2,1,0:T(8,128)(2,1)S(1)} %broadcast_in_dim.154), channel_id=1, replica_groups={{0,2,4,6,8,10,12,14,16,18,20,22,24,26,28,30},{1,3,5,7,9,11,13,15,17,19,..., dimensions={0} | all-to-all | bytes 524288 | tf_op jit(solution)/shard_map/all_to_all | solution.py:456
  127.1 2.2 all-gather.10
  130.4 1.8 all-gather.11
  132.2 12.3 %all_to_all.105 = bf16[16,64,128]{2,1,0:T(8,128)(2,1)S(1)} all-to-all(bf16[16,64,128]{2,1,0:T(8,128)(2,1)S(1)} %broadcast_in_dim.156), channel_id=1, replica_groups={{0,2,4,6,8,10,12,14,16,18,20,22,24,26,28,30},{1,3,5,7,9,11,13,15,17,19,..., dimensions={0} | all-to-all | bytes 524288 | tf_op jit(solution)/shard_map/all_to_all | solution.py:456
  144.5 2.2 all-gather.12
  147.8 8.3 %all-gather.13 = bf16[128,128]{1,0:T(8,128)(2,1)S(1)} all-gather(bf16[64,128]{1,0:T(8,128)(2,1)S(1)} %get-tuple-element.77), channel_id=15, replica_groups={{0,32},{1,33},{2,34},{3,35},{4,36},{5,37},{6,38},{7,39},{8,40},{9,41},{..., dimensions={0}, use_global_device_ids=true | all-gather | bytes 49152 | tf_op jit(solution)/shard_map/all_gather | solution.py:472
  156.1 11.9 %all_to_all.106 = bf16[16,64,128]{2,1,0:T(8,128)(2,1)S(1)} all-to-all(bf16[16,64,128]{2,1,0:T(8,128)(2,1)S(1)} %broadcast_in_dim.158), channel_id=1, replica_groups={{0,2,4,6,8,10,12,14,16,18,20,22,24,26,28,30},{1,3,5,7,9,11,13,15,17,19,..., dimensions={0} | all-to-all | bytes 524288 | tf_op jit(solution)/shard_map/all_to_all | solution.py:456
  168.1 2.2 all-gather.14
  171.4 1.8 all-gather.15
  173.3 12.3 %all_to_all.107 = bf16[16,64,128]{2,1,0:T(8,128)(2,1)S(1)} all-to-all(bf16[16,64,128]{2,1,0:T(8,128)(2,1)S(1)} %broadcast_in_dim.160), channel_id=1, replica_groups={{0,2,4,6,8,10,12,14,16,18,20,22,24,26,28,30},{1,3,5,7,9,11,13,15,17,19,..., dimensions={0} | all-to-all | bytes 524288 | tf_op jit(solution)/shard_map/all_to_all | solution.py:456
  185.5 2.2 all-gather.16
  188.8 8.7 %all-gather.17 = bf16[128,128]{1,0:T(8,128)(2,1)S(1)} all-gather(bf16[64,128]{1,0:T(8,128)(2,1)S(1)} %get-tuple-element.83), channel_id=19, replica_groups={{0,32},{1,33},{2,34},{3,35},{4,36},{5,37},{6,38},{7,39},{8,40},{9,41},{..., dimensions={0}, use_global_device_ids=true | all-gather | bytes 49152 | tf_op jit(solution)/shard_map/all_gather | solution.py:472
  197.5 11.9 %all_to_all.108 = bf16[16,64,128]{2,1,0:T(8,128)(2,1)S(1)} all-to-all(bf16[16,64,128]{2,1,0:T(8,128)(2,1)S(1)} %broadcast_in_dim.162), channel_id=1, replica_groups={{0,2,4,6,8,10,12,14,16,18,20,22,24,26,28,30},{1,3,5,7,9,11,13,15,17,19,..., dimensions={0} | all-to-all | bytes 524288 | tf_op jit(solution)/shard_map/all_to_all | solution.py:456
  209.5 2.2 all-gather.18
  212.8 1.8 all-gather.19
  214.7 12.3 %all_to_all.109 = bf16[16,64,128]{2,1,0:T(8,128)(2,1)S(1)} all-to-all(bf16[16,64,128]{2,1,0:T(8,128)(2,1)S(1)} %broadcast_in_dim.164), channel_id=1, replica_groups={{0,2,4,6,8,10,12,14,16,18,20,22,24,26,28,30},{1,3,5,7,9,11,13,15,17,19,..., dimensions={0} | all-to-all | bytes 524288 | tf_op jit(solution)/shard_map/all_to_all | solution.py:456
  226.9 2.3 all-gather.20
  230.4 8.1 %all-gather.21 = bf16[128,128]{1,0:T(8,128)(2,1)S(1)} all-gather(bf16[64,128]{1,0:T(8,128)(2,1)S(1)} %get-tuple-element.89), channel_id=23, replica_groups={{0,32},{1,33},{2,34},{3,35},{4,36},{5,37},{6,38},{7,39},{8,40},{9,41},{..., dimensions={0}, use_global_device_ids=true | all-gather | bytes 49152 | tf_op jit(solution)/shard_map/all_gather | solution.py:472
  238.5 11.9 %all_to_all.110 = bf16[16,64,128]{2,1,0:T(8,128)(2,1)S(1)} all-to-all(bf16[16,64,128]{2,1,0:T(8,128)(2,1)S(1)} %broadcast_in_dim.166), channel_id=1, replica_groups={{0,2,4,6,8,10,12,14,16,18,20,22,24,26,28,30},{1,3,5,7,9,11,13,15,17,19,..., dimensions={0} | all-to-all | bytes 524288 | tf_op jit(solution)/shard_map/all_to_all | solution.py:456
  250.5 2.2 all-gather.22
  253.8 1.8 all-gather.23
  255.7 12.3 %all_to_all.111 = bf16[16,64,128]{2,1,0:T(8,128)(2,1)S(1)} all-to-all(bf16[16,64,128]{2,1,0:T(8,128)(2,1)S(1)} %broadcast_in_dim.168), channel_id=1, replica_groups={{0,2,4,6,8,10,12,14,16,18,20,22,24,26,28,30},{1,3,5,7,9,11,13,15,17,19,..., dimensions={0} | all-to-all | bytes 524288 | tf_op jit(solution)/shard_map/all_to_all | solution.py:456
  267.9 2.2 all-gather.24
  270.1 1.1 shard_map.195
  271.2 8.1 %all-gather.25 = bf16[128,128]{1,0:T(8,128)(2,1)S(1)} all-gather(bf16[64,128]{1,0:T(8,128)(2,1)S(1)} %get-tuple-element.95), channel_id=27, replica_groups={{0,32},{1,33},{2,34},{3,35},{4,36},{5,37},{6,38},{7,39},{8,40},{9,41},{..., dimensions={0}, use_global_device_ids=true | all-gather | bytes 49152 | tf_op jit(solution)/shard_map/all_gather | solution.py:472
  279.4 11.9 %all_to_all.112 = bf16[16,64,128]{2,1,0:T(8,128)(2,1)S(1)} all-to-all(bf16[16,64,128]{2,1,0:T(8,128)(2,1)S(1)} %broadcast_in_dim.170), channel_id=1, replica_groups={{0,2,4,6,8,10,12,14,16,18,20,22,24,26,28,30},{1,3,5,7,9,11,13,15,17,19,..., dimensions={0} | all-to-all | bytes 524288 | tf_op jit(solution)/shard_map/all_to_all | solution.py:456
  291.3 2.2 all-gather.26
  294.6 1.8 all-gather.27
  296.5 12.3 %all_to_all.113 = bf16[16,64,128]{2,1,0:T(8,128)(2,1)S(1)} all-to-all(bf16[16,64,128]{2,1,0:T(8,128)(2,1)S(1)} %broadcast_in_dim.172), channel_id=1, replica_groups={{0,2,4,6,8,10,12,14,16,18,20,22,24,26,28,30},{1,3,5,7,9,11,13,15,17,19,..., dimensions={0} | all-to-all | bytes 524288 | tf_op jit(solution)/shard_map/all_to_all | solution.py:456
  308.7 2.2 all-gather.28
  312.0 7.9 %all-gather.29 = bf16[128,128]{1,0:T(8,128)(2,1)S(1)} all-gather(bf16[64,128]{1,0:T(8,128)(2,1)S(1)} %get-tuple-element.101), channel_id=31, replica_groups={{0,32},{1,33},{2,34},{3,35},{4,36},{5,37},{6,38},{7,39},{8,40},{9,41},{..., dimensions={0}, use_global_device_ids=true | all-gather | bytes 49152 | tf_op jit(solution)/shard_map/all_gather | solution.py:472
  320.0 11.9 %all_to_all.114 = bf16[16,64,128]{2,1,0:T(8,128)(2,1)S(1)} all-to-all(bf16[16,64,128]{2,1,0:T(8,128)(2,1)S(1)} %broadcast_in_dim.174), channel_id=1, replica_groups={{0,2,4,6,8,10,12,14,16,18,20,22,24,26,28,30},{1,3,5,7,9,11,13,15,17,19,..., dimensions={0} | all-to-all | bytes 524288 | tf_op jit(solution)/shard_map/all_to_all | solution.py:456
  331.9 2.2 all-gather.30
  335.2 1.8 all-gather.31
  337.1 12.3 %all_to_all.115 = bf16[16,64,128]{2,1,0:T(8,128)(2,1)S(1)} all-to-all(bf16[16,64,128]{2,1,0:T(8,128)(2,1)S(1)} %broadcast_in_dim.176), channel_id=1, replica_groups={{0,2,4,6,8,10,12,14,16,18,20,22,24,26,28,30},{1,3,5,7,9,11,13,15,17,19,..., dimensions={0} | all-to-all | bytes 524288 | tf_op jit(solution)/shard_map/all_to_all | solution.py:456
  349.4 2.2 all-gather.32
  352.7 7.9 %all-gather.33 = bf16[128,128]{1,0:T(8,128)(2,1)S(1)} all-gather(bf16[64,128]{1,0:T(8,128)(2,1)S(1)} %get-tuple-element.107), channel_id=35, replica_groups={{0,32},{1,33},{2,34},{3,35},{4,36},{5,37},{6,38},{7,39},{8,40},{9,41},{..., dimensions={0}, use_global_device_ids=true | all-gather | bytes 49152 | tf_op jit(solution)/shard_map/all_gather | solution.py:472
  360.6 11.9 %all_to_all.116 = bf16[16,64,128]{2,1,0:T(8,128)(2,1)S(1)} all-to-all(bf16[16,64,128]{2,1,0:T(8,128)(2,1)S(1)} %broadcast_in_dim.178), channel_id=1, replica_groups={{0,2,4,6,8,10,12,14,16,18,20,22,24,26,28,30},{1,3,5,7,9,11,13,15,17,19,..., dimensions={0} | all-to-all | bytes 524288 | tf_op jit(solution)/shard_map/all_to_all | solution.py:456
  372.5 2.2 all-gather.34
  374.7 1.7 shard_map.200
  377.1 11.2 %all_to_all.117.temporal_ref = bf16[32,4,128]{2,1,0:T(4,128)(2,1)S(1)} all-to-all(bf16[32,4,128]{2,1,0:T(4,128)(2,1)S(1)} %bitcast.98), channel_id=1, replica_groups=mesh['section'=16,'frame'=32] {'frame'}, dimensions={0} | all-to-all | bytes 65536 | tf_op jit(solution)/shard_map/all_to_all | solution.py:479
  388.3 16.3 %shard_map.202 = bf16[16,24,128]{2,1,0:T(8,128)(2,1)S(1)} custom-call(bf16[32,4,128]{2,1,0:T(4,128)(2,1)S(1)} %all_to_all.117.temporal_ref, bf16[1024,4096]{1,0:T(8,128)(2,1)} %all-gather.39.cloned.1.call-done.in_ref, bf16[16,272,1024]{2,1,0:T(8,128)(2,1)} %bitcast.89), custom_call_target="tpu_custom_call" | custom-call | flops 553648128 | bytes 17301504 | tf_op jit(solution)/shard_map/pallas_call | solution.py:376
  404.6 30.4 %all_to_all.118.result_ref = bf16[16,24,128]{2,1,0:T(8,128)(2,1)} all-to-all(bf16[16,24,128]{2,1,0:T(8,128)(2,1)S(1)} %shard_map.202), channel_id=1, replica_groups=mesh['section'=16,'frame'=32] {'section'}, dimensions={0} | all-to-all | bytes 196608 | tf_op jit(solution)/shard_map/all_to_all | solution.py:481
  435.1 1.6 shard_map.203
  (67 shorter events, 20.1 us)
Async XLA Ops:
  7.2 23.2 %copy-start = (bf16[1,256,128]{2,1,0:T(8,128)(2,1)S(1)}, bf16[1,256,128]{2,1,0:T(8,128)(2,1)}, u32[]{:S(2)}) copy-start(bf16[1,256,128]{2,1,0:T(8,128)(2,1)} %param.21) | copy-start | bytes 196612
  7.2 23.2 %copy-start.1 = (bf16[1,256,128]{2,1,0:T(8,128)(2,1)S(1)}, bf16[1,256,128]{2,1,0:T(8,128)(2,1)}, u32[]{:S(2)}) copy-start(bf16[1,256,128]{2,1,0:T(8,128)(2,1)} %param.22) | copy-start | bytes 196612
  7.2 381.1 %all-gather.39.cloned.1.call-start = ((), (), s32[]{:S(2)}) async-start(), calls=%async_computation.20 | async-start | bytes 8912896 | tf_op jit(solution)/shard_map/all_gather | solution.py:448
  7.9 380.4 %all-gather.41.cloned.1.call-start = ((), (), s32[]{:S(2)}) async-start(), calls=%async_computation.21 | async-start | bytes 9469952 | tf_op jit(solution)/shard_map/all_gather | solution.py:447
  12.4 15.6 %all-to-all-start = ((bf16[16,64,128]{2,1,0:T(8,128)(2,1)}), bf16[16,64,128]{2,1,0:T(8,128)(2,1)S(1)}, u32[]{:S(2)}, u32[]{:S(2)}) async-start(bf16[16,64,128]{2,1,0:T(8,128)(2,1)} %broadcast_in_dim.142), calls=%async_computation | async-start | bytes 524288 | tf_op jit(solution)/shard_map/all_to_all | solution.py:456
  28.1 25.2 %copy-start.2 = (bf16[128,128]{1,0:T(8,128)(2,1)S(1)}, bf16[128,128]{1,0:T(8,128)(2,1)}, u32[]{:S(2)}) copy-start(bf16[128,128]{1,0:T(8,128)(2,1)} %param.16) | copy-start | bytes 98308
Sparse Core Ops, SparseCore 0:
  10.1 110.3 all-gather.38
  122.6 110.1 all-gather.40

commit v7 on v6

--- a/solution.py
+++ b/solution.py
@@ -13,6 +13,7 @@
 SECTIONS = 16
 CHIPS = 16
 PIECES = 8
+JOINT_AFTER = 10
 
 EPSILON = 1e-05
 MASKED = -1e30
@@ -36,6 +37,14 @@
     return pairs
 
 
+def joint_groups():
+    return [
+        [device_id(low + up, chip, core) for up in range(2) for chip in range(CHIPS)]
+        for low in range(0, SECTIONS, 2)
+        for core in range(2)
+    ]
+
+
 def plane_groups():
     return [
         [device_id(section, chip, core) for chip in range(CHIPS)]
@@ -55,7 +64,6 @@
 def layer_kernel(
     clock_ref,
     rows_ref,
-    own_ref,
     weight_ref,
     stash_k_ref,
     stash_v_ref,
@@ -65,7 +73,8 @@
     send_ref,
 ):
     block = clock_ref[0, 0]
-    next_ref[...] = clock_ref[...] + 1
+    first_row = lax.broadcasted_iota(jnp.int32, clock_ref.shape, 0) == 0
+    next_ref[...] = clock_ref[...] + first_row.astype(jnp.int32)
     total = jnp.zeros((CH, 3 * HEAD), jnp.float32)
     squares = jnp.zeros((CH, 2 * HEAD), jnp.float32)
     per_piece = CHIPS // PIECES
@@ -103,7 +112,8 @@
     raised = jnp.exp(scores - peak)
     probs = (raised / jnp.sum(raised, axis=-1, keepdims=True)).astype(jnp.bfloat16)
     attended = jnp.dot(probs, values, preferred_element_type=jnp.float32)
-    x_out = (own_ref[...].astype(jnp.float32) + attended).astype(jnp.bfloat16)
+    own = rows_ref[clock_ref[2, 0], clock_ref[1, 0]]
+    x_out = (own.astype(jnp.float32) + attended).astype(jnp.bfloat16)
 
     def keep(rows):
         found_ref[0, rows] = key_new
@@ -117,23 +127,23 @@
     send_ref[...] = x_out
 
 
-def layer_step(clock, rows, own, weight, stash_k, stash_v, held):
+def layer_step(clock, rows, weight, stash_k, stash_v, held):
     vmem = pl.BlockSpec(memory_space=pltpu.VMEM)
     return pl.pallas_call(
         layer_kernel,
         out_shape=(
             jax.ShapeDtypeStruct(clock.shape, clock.dtype),
             jax.ShapeDtypeStruct(held.shape, held.dtype),
-            jax.ShapeDtypeStruct(own.shape, own.dtype),
+            jax.ShapeDtypeStruct((CH, HEAD), held.dtype),
         ),
-        in_specs=[vmem] * 7,
+        in_specs=[vmem] * 6,
         out_specs=(vmem, vmem, vmem),
-        input_output_aliases={6: 1},
+        input_output_aliases={5: 1},
         compiler_params=pltpu.CompilerParams(vmem_limit_bytes=16 * 1024 * 1024),
         cost_estimate=pl.CostEstimate(
             flops=2 * CH * weight.size, bytes_accessed=2 * weight.size, transcendentals=0
         ),
-    )(clock, rows, own, weight, stash_k, stash_v, held)
+    )(clock, rows, weight, stash_k, stash_v, held)
 
 
 def pack_kernel(
@@ -435,6 +445,7 @@
     cotangent,
 ):
     section_id = lax.axis_index("section")
+    frame_id = lax.axis_index("frame")
     frames, levels, part = cotangent.shape
 
     packed = pack(
@@ -452,27 +463,30 @@
     weight = (weight.astype(jnp.float32) * gain).astype(jnp.bfloat16)
     stash_k, stash_v = cache_keys[0], cache_values[0]
 
-    def layer(clock, block, held):
-        got = lax.all_to_all(
-            jnp.broadcast_to(block[None], (CHIPS,) + block.shape),
-            BOTH,
-            split_axis=0,
-            concat_axis=0,
-            tiled=True,
-            axis_index_groups=plane_groups(),
-        )
+    def spread(block, groups):
+        copies = jnp.broadcast_to(block[None], (len(groups[0]),) + block.shape)
+        return lax.all_to_all(
+            copies, BOTH, split_axis=0, concat_axis=0, tiled=True, axis_index_groups=groups
+        )[:CHIPS]
+
+    def layer(clock, got, held):
         rows = lax.all_gather(got, BOTH, axis=0, axis_index_groups=core_pairs())
-        return layer_step(clock, rows, block, weight, stash_k, stash_v, held)
-
-    clock = jnp.zeros((8, HEAD), jnp.int32) - section_id
+        return layer_step(clock, rows, weight, stash_k, stash_v, held)
+
+    row = lax.broadcasted_iota(jnp.int32, (8, HEAD), 0)
+    clock = jnp.where(row == 0, -section_id, jnp.where(row == 1, frame_id // 2, frame_id % 2))
     held = jnp.zeros((3, 2 * CH, HEAD), jnp.bfloat16)
-    clock, held, block = layer(clock, inflow[:CH], held)
+    clock, held, block = layer(clock, spread(inflow[:CH], plane_groups()), held)
     for tick in range(1, SECTIONS + 2):
-        pairs = plane_pairs((tick - 1) % 2)
-        block = lax.all_gather(block, BOTH, axis=0, axis_index_groups=pairs)[0]
-        if tick == 2:
-            block = jnp.where(clock[:1] == tick, inflow[CH:], block)
-        clock, held, block = layer(clock, block, held)
+        if tick > JOINT_AFTER and tick % 2 == 1:
+            got = spread(block, joint_groups())
+        else:
+            pairs = plane_pairs((tick - 1) % 2)
+            block = lax.all_gather(block, BOTH, axis=0, axis_index_groups=pairs)[0]
+            if tick == 2:
+                block = jnp.where(clock[:1] == tick, inflow[CH:], block)
+            got = spread(block, plane_groups())
+        clock, held, block = layer(clock, got, held)
     new_keys, new_values, finished = held[0], held[1], held[2]
 
     finished = finished.reshape(2 * CHIPS, frames, HEAD)

time: 446 us -> 443 us (level)
    all_to_all x17, blocking collectives: 205 us -> 239 us  [spread(): lax.all_to_all(copies, BOTH, split_axis=0, concat_axis=0, tiled=True, axi...]
    all_gather x17 -> x13, blocking collectives: 81.7 us -> 49.8 us  [body(): block = lax.all_gather(block, BOTH, axis=0, axis_index_groups=pairs)[0]]
  transfers between devices with their start and end apart: 3 -> 3, of which waited for: 1 -> 1; matrix products, arithmetic and copies ran while one was open for 1% -> 2% of each run, Pallas kernels for 5% -> 5%
where the time goes in v7:
time: 443 us; the launch traced here: 441 us
  blocking collectives  365 us (82%)
  Pallas kernels  41.6 us (9%)
  between operations  14.4 us (3%)
  starting transfers between devices  9.32 us (2%)
    all_to_all x17, blocking collectives, spread(): lax.all_to_all(copies, BOTH, split_axis=0, concat_axis=0, tiled=True, axi...  239 us
    all_gather x13, blocking collectives, body(): block = lax.all_gather(block, BOTH, axis=0, axis_index_groups=pairs)[0]  49.8 us
    all_gather x18, blocking collectives, layer(): rows = lax.all_gather(got, BOTH, axis=0, axis_index_groups=core_pairs())  39.2 us
    all_to_all x1, blocking collectives, body(): lax.all_to_all(results, 'section', split_axis=0, concat_axis=0, tiled=True)  26.5 us
    pallas_call x18, Pallas kernels, layer_step(): pl.pallas_call(layer_kernel, out_shape=(jax.ShapeDtypeStruct(clock.shape,...  20.8 us
    pallas_call x1, Pallas kernels, depth_part(): pl.pallas_call(depth_kernel, out_shape=jax.ShapeDtypeStruct((SECTIONS, ro...  16.3 us
    all_to_all x1, blocking collectives, body(): lax.all_to_all(finished, 'frame', split_axis=0, concat_axis=0, tiled=True)  10.7 us
    all_to_all x1, starting transfers between devices, spread(): lax.all_to_all(copies, BOTH, split_axis=0, concat_axis=0, tiled=True, axi...  9.25 us
  transfers between devices with their start and end apart: 3, of which 1 were waited for; matrix products, arithmetic and copies ran while one was open for 2% of the time, Pallas kernels for 5%

profile of v7, /device:TPU:6, one launch (start us, length us, event | category | flops | bytes accessed | tf_op | source)
XLA Modules:
  0.0 440.9 jit_solution(14414902878672064)
XLA Ops:
  8.0 2.9 shard_map.201
  12.4 9.2 %all-to-all-start = ((bf16[16,64,128]{2,1,0:T(8,128)(2,1)}), bf16[16,64,128]{2,1,0:T(8,128)(2,1)S(1)}, u32[]{:S(2)}, u32[]{:S(2)}) async-start(bf16[16,64,128]{2,1,0:T(8,128)(2,1)} %broadcast_in_dim.149), calls=%async_computation | async-start | bytes 524288 | tf_op jit(solution)/shard_map/all_to_all | solution.py:468
  21.7 1.3 convert_element_type.20
  23.0 2.2 multiply_convert_fusion.weight_ref
  25.3 2.7 all-to-all-done
  28.1 2.3 all-gather
  30.4 1.1 shard_map.183
  31.5 4.7 %all-gather.1 = bf16[128,128]{1,0:T(8,128)(2,1)S(1)} all-gather(bf16[64,128]{1,0:T(8,128)(2,1)S(1)} %get-tuple-element.59), channel_id=3, replica_groups={{0,32},{1,33},{2,34},{3,35},{4,36},{5,37},{6,38},{7,39},{8,40},{9,41},{..., dimensions={0}, use_global_device_ids=true | all-gather | bytes 49152 | tf_op jit(solution)/shard_map/all_gather | solution.py:485
  36.3 11.8 %all_to_all.100 = bf16[16,64,128]{2,1,0:T(8,128)(2,1)S(1)} all-to-all(bf16[16,64,128]{2,1,0:T(8,128)(2,1)S(1)} %broadcast_in_dim.152), channel_id=1, replica_groups={{0,2,4,6,8,10,12,14,16,18,20,22,24,26,28,30},{1,3,5,7,9,11,13,15,17,19,..., dimensions={0} | all-to-all | bytes 524288 | tf_op jit(solution)/shard_map/all_to_all | solution.py:468
  48.2 2.2 all-gather.2
  50.3 1.1 shard_map.184
  51.5 1.8 all-gather.3
  53.4 12.3 %all_to_all.101 = bf16[16,64,128]{2,1,0:T(8,128)(2,1)S(1)} all-to-all(bf16[16,64,128]{2,1,0:T(8,128)(2,1)S(1)} %broadcast_in_dim.155), channel_id=1, replica_groups={{0,2,4,6,8,10,12,14,16,18,20,22,24,26,28,30},{1,3,5,7,9,11,13,15,17,19,..., dimensions={0} | all-to-all | bytes 524288 | tf_op jit(solution)/shard_map/all_to_all | solution.py:468
  65.6 2.2 all-gather.4
  67.8 1.1 shard_map.185
  68.9 5.2 %all-gather.5 = bf16[128,128]{1,0:T(8,128)(2,1)S(1)} all-gather(bf16[64,128]{1,0:T(8,128)(2,1)S(1)} %get-tuple-element.65), channel_id=7, replica_groups={{0,32},{1,33},{2,34},{3,35},{4,36},{5,37},{6,38},{7,39},{8,40},{9,41},{..., dimensions={0}, use_global_device_ids=true | all-gather | bytes 49152 | tf_op jit(solution)/shard_map/all_gather | solution.py:485
  74.2 11.9 %all_to_all.102 = bf16[16,64,128]{2,1,0:T(8,128)(2,1)S(1)} all-to-all(bf16[16,64,128]{2,1,0:T(8,128)(2,1)S(1)} %broadcast_in_dim.157), channel_id=1, replica_groups={{0,2,4,6,8,10,12,14,16,18,20,22,24,26,28,30},{1,3,5,7,9,11,13,15,17,19,..., dimensions={0} | all-to-all | bytes 524288 | tf_op jit(solution)/shard_map/all_to_all | solution.py:468
  86.1 2.2 all-gather.6
  88.3 1.1 shard_map.186
  89.4 1.8 all-gather.7
  91.3 12.3 %all_to_all.103 = bf16[16,64,128]{2,1,0:T(8,128)(2,1)S(1)} all-to-all(bf16[16,64,128]{2,1,0:T(8,128)(2,1)S(1)} %broadcast_in_dim.159), channel_id=1, replica_groups={{0,2,4,6,8,10,12,14,16,18,20,22,24,26,28,30},{1,3,5,7,9,11,13,15,17,19,..., dimensions={0} | all-to-all | bytes 524288 | tf_op jit(solution)/shard_map/all_to_all | solution.py:468
  103.6 2.2 all-gather.8
  106.9 8.2 %all-gather.9 = bf16[128,128]{1,0:T(8,128)(2,1)S(1)} all-gather(bf16[64,128]{1,0:T(8,128)(2,1)S(1)} %get-tuple-element.71), channel_id=11, replica_groups={{0,32},{1,33},{2,34},{3,35},{4,36},{5,37},{6,38},{7,39},{8,40},{9,41},{..., dimensions={0}, use_global_device_ids=true | all-gather | bytes 49152 | tf_op jit(solution)/shard_map/all_gather | solution.py:485
  115.2 11.9 %all_to_all.104 = bf16[16,64,128]{2,1,0:T(8,128)(2,1)S(1)} all-to-all(bf16[16,64,128]{2,1,0:T(8,128)(2,1)S(1)} %broadcast_in_dim.161), channel_id=1, replica_groups={{0,2,4,6,8,10,12,14,16,18,20,22,24,26,28,30},{1,3,5,7,9,11,13,15,17,19,..., dimensions={0} | all-to-all | bytes 524288 | tf_op jit(solution)/shard_map/all_to_all | solution.py:468
  127.1 2.2 all-gather.10
  130.4 1.8 all-gather.11
  132.3 12.3 %all_to_all.105 = bf16[16,64,128]{2,1,0:T(8,128)(2,1)S(1)} all-to-all(bf16[16,64,128]{2,1,0:T(8,128)(2,1)S(1)} %broadcast_in_dim.163), channel_id=1, replica_groups={{0,2,4,6,8,10,12,14,16,18,20,22,24,26,28,30},{1,3,5,7,9,11,13,15,17,19,..., dimensions={0} | all-to-all | bytes 524288 | tf_op jit(solution)/shard_map/all_to_all | solution.py:468
  144.6 2.2 all-gather.12
  147.9 8.3 %all-gather.13 = bf16[128,128]{1,0:T(8,128)(2,1)S(1)} all-gather(bf16[64,128]{1,0:T(8,128)(2,1)S(1)} %get-tuple-element.77), channel_id=15, replica_groups={{0,32},{1,33},{2,34},{3,35},{4,36},{5,37},{6,38},{7,39},{8,40},{9,41},{..., dimensions={0}, use_global_device_ids=true | all-gather | bytes 49152 | tf_op jit(solution)/shard_map/all_gather | solution.py:485
  156.2 11.9 %all_to_all.106 = bf16[16,64,128]{2,1,0:T(8,128)(2,1)S(1)} all-to-all(bf16[16,64,128]{2,1,0:T(8,128)(2,1)S(1)} %broadcast_in_dim.165), channel_id=1, replica_groups={{0,2,4,6,8,10,12,14,16,18,20,22,24,26,28,30},{1,3,5,7,9,11,13,15,17,19,..., dimensions={0} | all-to-all | bytes 524288 | tf_op jit(solution)/shard_map/all_to_all | solution.py:468
  168.1 2.2 all-gather.14
  171.4 1.8 all-gather.15
  173.3 12.3 %all_to_all.107 = bf16[16,64,128]{2,1,0:T(8,128)(2,1)S(1)} all-to-all(bf16[16,64,128]{2,1,0:T(8,128)(2,1)S(1)} %broadcast_in_dim.167), channel_id=1, replica_groups={{0,2,4,6,8,10,12,14,16,18,20,22,24,26,28,30},{1,3,5,7,9,11,13,15,17,19,..., dimensions={0} | all-to-all | bytes 524288 | tf_op jit(solution)/shard_map/all_to_all | solution.py:468
  185.6 2.2 all-gather.16
  187.7 1.1 shard_map.191
  188.9 8.7 %all-gather.17 = bf16[128,128]{1,0:T(8,128)(2,1)S(1)} all-gather(bf16[64,128]{1,0:T(8,128)(2,1)S(1)} %get-tuple-element.83), channel_id=19, replica_groups={{0,32},{1,33},{2,34},{3,35},{4,36},{5,37},{6,38},{7,39},{8,40},{9,41},{..., dimensions={0}, use_global_device_ids=true | all-gather | bytes 49152 | tf_op jit(solution)/shard_map/all_gather | solution.py:485
  197.6 11.9 %all_to_all.108 = bf16[16,64,128]{2,1,0:T(8,128)(2,1)S(1)} all-to-all(bf16[16,64,128]{2,1,0:T(8,128)(2,1)S(1)} %broadcast_in_dim.169), channel_id=1, replica_groups={{0,2,4,6,8,10,12,14,16,18,20,22,24,26,28,30},{1,3,5,7,9,11,13,15,17,19,..., dimensions={0} | all-to-all | bytes 524288 | tf_op jit(solution)/shard_map/all_to_all | solution.py:468
  209.6 2.2 all-gather.18
  211.7 1.1 shard_map.192
  212.9 1.8 all-gather.19
  214.7 12.3 %all_to_all.109 = bf16[16,64,128]{2,1,0:T(8,128)(2,1)S(1)} all-to-all(bf16[16,64,128]{2,1,0:T(8,128)(2,1)S(1)} %broadcast_in_dim.171), channel_id=1, replica_groups={{0,2,4,6,8,10,12,14,16,18,20,22,24,26,28,30},{1,3,5,7,9,11,13,15,17,19,..., dimensions={0} | all-to-all | bytes 524288 | tf_op jit(solution)/shard_map/all_to_all | solution.py:468
  227.0 2.2 all-gather.20
  230.4 21.3 %all_to_all.110 = bf16[32,64,128]{2,1,0:T(8,128)(2,1)S(1)} all-to-all(bf16[32,64,128]{2,1,0:T(8,128)(2,1)S(1)} %broadcast_in_dim.172), channel_id=1, replica_groups={{0,2,4,6,8,10,12,14,16,18,20,22,24,26,28,30,32,34,36,38,40,42,44,46,48,..., dimensions={0} | all-to-all | bytes 1048576 | tf_op jit(solution)/shard_map/all_to_all | solution.py:468
  251.7 2.2 all-gather.21
  255.0 1.8 all-gather.22
  256.9 11.8 %all_to_all.111 = bf16[16,64,128]{2,1,0:T(8,128)(2,1)S(1)} all-to-all(bf16[16,64,128]{2,1,0:T(8,128)(2,1)S(1)} %broadcast_in_dim.174), channel_id=1, replica_groups={{0,2,4,6,8,10,12,14,16,18,20,22,24,26,28,30},{1,3,5,7,9,11,13,15,17,19,..., dimensions={0} | all-to-all | bytes 524288 | tf_op jit(solution)/shard_map/all_to_all | solution.py:468
  268.7 2.2 all-gather.23
  272.1 21.3 %all_to_all.112 = bf16[32,64,128]{2,1,0:T(8,128)(2,1)S(1)} all-to-all(bf16[32,64,128]{2,1,0:T(8,128)(2,1)S(1)} %broadcast_in_dim.175), channel_id=1, replica_groups={{0,2,4,6,8,10,12,14,16,18,20,22,24,26,28,30,32,34,36,38,40,42,44,46,48,..., dimensions={0} | all-to-all | bytes 1048576 | tf_op jit(solution)/shard_map/all_to_all | solution.py:468
  293.4 2.2 all-gather.24
  296.7 1.8 all-gather.25
  298.6 11.8 %all_to_all.113 = bf16[16,64,128]{2,1,0:T(8,128)(2,1)S(1)} all-to-all(bf16[16,64,128]{2,1,0:T(8,128)(2,1)S(1)} %broadcast_in_dim.177), channel_id=1, replica_groups={{0,2,4,6,8,10,12,14,16,18,20,22,24,26,28,30},{1,3,5,7,9,11,13,15,17,19,..., dimensions={0} | all-to-all | bytes 524288 | tf_op jit(solution)/shard_map/all_to_all | solution.py:468
  310.4 2.2 all-gather.26
  313.8 19.8 %all_to_all.114 = bf16[32,64,128]{2,1,0:T(8,128)(2,1)S(1)} all-to-all(bf16[32,64,128]{2,1,0:T(8,128)(2,1)S(1)} %broadcast_in_dim.178), channel_id=1, replica_groups={{0,2,4,6,8,10,12,14,16,18,20,22,24,26,28,30,32,34,36,38,40,42,44,46,48,..., dimensions={0} | all-to-all | bytes 1048576 | tf_op jit(solution)/shard_map/all_to_all | solution.py:468
  333.6 2.2 all-gather.27
  336.9 1.8 all-gather.28
  338.8 11.8 %all_to_all.115 = bf16[16,64,128]{2,1,0:T(8,128)(2,1)S(1)} all-to-all(bf16[16,64,128]{2,1,0:T(8,128)(2,1)S(1)} %broadcast_in_dim.180), channel_id=1, replica_groups={{0,2,4,6,8,10,12,14,16,18,20,22,24,26,28,30},{1,3,5,7,9,11,13,15,17,19,..., dimensions={0} | all-to-all | bytes 524288 | tf_op jit(solution)/shard_map/all_to_all | solution.py:468
  350.6 2.2 all-gather.29
  354.0 20.4 %all_to_all.116 = bf16[32,64,128]{2,1,0:T(8,128)(2,1)S(1)} all-to-all(bf16[32,64,128]{2,1,0:T(8,128)(2,1)S(1)} %broadcast_in_dim.181), channel_id=1, replica_groups={{0,2,4,6,8,10,12,14,16,18,20,22,24,26,28,30,32,34,36,38,40,42,44,46,48,..., dimensions={0} | all-to-all | bytes 1048576 | tf_op jit(solution)/shard_map/all_to_all | solution.py:468
  374.4 2.2 all-gather.30
  376.6 1.7 shard_map.200
  379.0 10.7 %all_to_all.117.temporal_ref = bf16[32,4,128]{2,1,0:T(4,128)(2,1)S(1)} all-to-all(bf16[32,4,128]{2,1,0:T(4,128)(2,1)S(1)} %bitcast.98), channel_id=1, replica_groups=mesh['section'=16,'frame'=32] {'frame'}, dimensions={0} | all-to-all | bytes 65536 | tf_op jit(solution)/shard_map/all_to_all | solution.py:493
  389.7 16.3 %shard_map.202 = bf16[16,24,128]{2,1,0:T(8,128)(2,1)S(1)} custom-call(bf16[32,4,128]{2,1,0:T(4,128)(2,1)S(1)} %all_to_all.117.temporal_ref, bf16[1024,4096]{1,0:T(8,128)(2,1)} %all-gather.35.cloned.1.call-done.in_ref, bf16[16,272,1024]{2,1,0:T(8,128)(2,1)} %bitcast.89), custom_call_target="tpu_custom_call" | custom-call | flops 553648128 | bytes 17301504 | tf_op jit(solution)/shard_map/pallas_call | solution.py:386
  406.1 26.5 %all_to_all.118.result_ref = bf16[16,24,128]{2,1,0:T(8,128)(2,1)} all-to-all(bf16[16,24,128]{2,1,0:T(8,128)(2,1)S(1)} %shard_map.202), channel_id=1, replica_groups=mesh['section'=16,'frame'=32] {'section'}, dimensions={0} | all-to-all | bytes 196608 | tf_op jit(solution)/shard_map/all_to_all | solution.py:495
  432.5 1.6 shard_map.203
  (65 shorter events, 16.5 us)
Async XLA Ops:
  7.2 23.2 %copy-start = (bf16[1,256,128]{2,1,0:T(8,128)(2,1)S(1)}, bf16[1,256,128]{2,1,0:T(8,128)(2,1)}, u32[]{:S(2)}) copy-start(bf16[1,256,128]{2,1,0:T(8,128)(2,1)} %param.21) | copy-start | bytes 196612
  7.2 23.2 %copy-start.1 = (bf16[1,256,128]{2,1,0:T(8,128)(2,1)S(1)}, bf16[1,256,128]{2,1,0:T(8,128)(2,1)}, u32[]{:S(2)}) copy-start(bf16[1,256,128]{2,1,0:T(8,128)(2,1)} %param.22) | copy-start | bytes 196612
  7.2 382.5 %all-gather.35.cloned.1.call-start = ((), (), s32[]{:S(2)}) async-start(), calls=%async_computation.20 | async-start | bytes 8912896 | tf_op jit(solution)/shard_map/all_gather | solution.py:459
  7.9 381.8 %all-gather.37.cloned.1.call-start = ((), (), s32[]{:S(2)}) async-start(), calls=%async_computation.21 | async-start | bytes 9469952 | tf_op jit(solution)/shard_map/all_gather | solution.py:458
  12.4 15.6 %all-to-all-start = ((bf16[16,64,128]{2,1,0:T(8,128)(2,1)}), bf16[16,64,128]{2,1,0:T(8,128)(2,1)S(1)}, u32[]{:S(2)}, u32[]{:S(2)}) async-start(bf16[16,64,128]{2,1,0:T(8,128)(2,1)} %broadcast_in_dim.149), calls=%async_computation | async-start | bytes 524288 | tf_op jit(solution)/shard_map/all_to_all | solution.py:468
  28.1 25.2 %copy-start.2 = (bf16[128,128]{1,0:T(8,128)(2,1)S(1)}, bf16[128,128]{1,0:T(8,128)(2,1)}, u32[]{:S(2)}) copy-start(bf16[128,128]{1,0:T(8,128)(2,1)} %param.16) | copy-start | bytes 98308
Sparse Core Ops, SparseCore 0:
  10.1 110.3 all-gather.34
  122.6 110.1 all-gather.36
